TPU v7x, 32 devices: a whole 2x2x4 slice. The times are simulated.
32 devices in a mesh: seq: 2 (over x), fsdp: 16 (over z, y, core).
Axes of the slice: x: 2, y: 2, z: 4, core: 2. Of those that a mesh axis runs over, the one named last changes fastest.
Arguments:
- tokens: bfloat16 [16, 1024, 1536], P('fsdp', 'seq'), may hold values from -6 to 6
- cotangent: bfloat16 [16, 1024, 1536], P('fsdp', 'seq'), may hold values from -6 to 6
- segment_ids: int32 [16, 1024], P('fsdp', 'seq'), may hold values from 0 to 8, as said below
- route_ids: int32 [16, 1024, 4], P('fsdp', 'seq'), may hold values from 0 to 7, all different within a row; in each aligned block of 512 rows (0 to 511, 512 to 1023, ..., all dimensions but the last counted through in order) at most 320 rows name the same one
- query_key_value_weight: float32 [1536, 2048], P(('seq', 'fsdp')), may hold values from -0.15625 to 0.15625
- out_weight: float32 [1536, 1536], P(('seq', 'fsdp')), may hold values from -1.25 to 1.25
- router_weight: float32 [1536, 8], P(('seq', 'fsdp')), may hold values from -0.078125 to 0.078125
- expert_in: float32 [8, 1536, 1536], P(None, ('seq', 'fsdp')), may hold values from -0.15625 to 0.15625
- expert_down: float32 [8, 768, 1536], P(None, ('seq', 'fsdp')), may hold values from -1.75 to 1.75
- norm_gains: float32 [1536, 2], P(('seq', 'fsdp')), may hold values from 0.3 to 2.5, as said below
- query_key_value_moment: float32 [1536, 2048], P(('seq', 'fsdp')), may hold values from -0.00024414062 to 0.00024414062
- out_moment: float32 [1536, 1536], P(('seq', 'fsdp')), may hold values from -6.1035156e-05 to 6.1035156e-05
- router_moment: float32 [1536, 8], P(('seq', 'fsdp')), may hold values from -0.00024414062 to 0.00024414062
- in_moment: float32 [8, 1536, 1536], P(None, ('seq', 'fsdp')), may hold values from -0.00024414062 to 0.00024414062
- down_moment: float32 [8, 768, 1536], P(None, ('seq', 'fsdp')), may hold values from -9.536743e-06 to 9.536743e-06
- gains_moment: float32 [1536, 2], P(('seq', 'fsdp')), may hold values from -0.0008544922 to 0.0008544922
- query_key_value_second: float32 [1536, 2048], P(('seq', 'fsdp')), may hold values from 1.5665672e-09 to 6.207153e-09
- out_second: float32 [1536, 1536], P(('seq', 'fsdp')), may hold values from 7.0938894e-11 to 2.8079977e-10
- router_second: float32 [1536, 8], P(('seq', 'fsdp')), may hold values from 1.5665672e-09 to 6.207153e-09
- in_second: float32 [8, 1536, 1536], P(None, ('seq', 'fsdp')), may hold values from 1.5665672e-09 to 6.207153e-09
- down_second: float32 [8, 768, 1536], P(None, ('seq', 'fsdp')), may hold values from 1.8917038e-12 to 7.3894675e-12
- gains_second: float32 [1536, 2], P(('seq', 'fsdp')), may hold values from 1.3892199e-08 to 5.6159955e-08
Outputs:
- output: bfloat16 [16, 1024, 1536], P('fsdp', 'seq')
- input_grad: bfloat16 [16, 1024, 1536], P('fsdp', 'seq')
- grad_norm: float32 [], replicated
- qkv_new: float32 [1536, 2048], P(('seq', 'fsdp'))
- out_new: float32 [1536, 1536], P(('seq', 'fsdp'))
- router_new: float32 [1536, 8], P(('seq', 'fsdp'))
- in_new: float32 [8, 1536, 1536], P(None, ('seq', 'fsdp'))
- down_new: float32 [8, 768, 1536], P(None, ('seq', 'fsdp'))
- gains_new: float32 [1536, 2], P(('seq', 'fsdp'))
- qkv_moment_new: float32 [1536, 2048], P(('seq', 'fsdp'))
- out_moment_new: float32 [1536, 1536], P(('seq', 'fsdp'))
- router_moment_new: float32 [1536, 8], P(('seq', 'fsdp'))
- in_moment_new: float32 [8, 1536, 1536], P(None, ('seq', 'fsdp'))
- down_moment_new: float32 [8, 768, 1536], P(None, ('seq', 'fsdp'))
- gains_moment_new: float32 [1536, 2], P(('seq', 'fsdp'))
- qkv_second_new: float32 [1536, 2048], P(('seq', 'fsdp'))
- out_second_new: float32 [1536, 1536], P(('seq', 'fsdp'))
- router_second_new: float32 [1536, 8], P(('seq', 'fsdp'))
- in_second_new: float32 [8, 1536, 1536], P(None, ('seq', 'fsdp'))
- down_second_new: float32 [8, 768, 1536], P(None, ('seq', 'fsdp'))
- gains_second_new: float32 [1536, 2], P(('seq', 'fsdp'))
Inputs may be any that keep to these rules, and one draw needn't show every extreme that they name: `segment_ids`: segment numbers start at 0 in every pack and never fall along it. `route_ids`: each row names 4 different experts. The rows of one device (aligned blocks of 512 rows in pack order) name no expert more than 320 times, a bound that some block reaches. `norm_gains`: positive gains.
All inputs are finite; a program needn't handle non-finite values.
Results may differ from a plain program's by a relative error of at most 0.019.
The roundings to bfloat16 on the way count: a program that leaves them out, or rounds other values in their place, can miss the bound.
Values may be sent and summed in bfloat16 or wider, within the bound.
No kernel may reach another device: no remote copies, remote signals or barrier semaphores. Data moves between devices by JAX's collectives and lax.ppermute only.
A program may use at most 448 MiB of HBM per device.

v0:
```python
import jax
import jax.numpy as jnp
from jax import lax
from jax.sharding import PartitionSpec as P

MODEL_DIMENSION = 1536
QUERY_HEADS = 12
KEY_VALUE_HEADS = 2
HEAD_DIMENSION = 128
F = 768
EXPERTS = 8
TOPK = 4
STEP = 10
CAP = 320


PRECISE = lax.Precision.HIGHEST
NORM_EPS = 1e-06
CLIP_NORM = 1.0
BETA_ONE = 0.9
BETA_TWO = 0.95
ADAM_EPS = 1e-08
DECAY_RATE = 0.1
ROPE_BASE = 10000.0
MASKED_SCORE = -1e30


def rms_scale(values):
    return lax.rsqrt(jnp.mean(values * values, axis=-1, keepdims=True) + NORM_EPS)


def rotation_embedding(values, token_positions):
    half_size = values.shape[-1] // 2
    frequency = ROPE_BASE ** (-2.0 * jnp.arange(half_size, dtype=jnp.float32) / values.shape[-1])
    angles = token_positions[:, None] * frequency[None, :]
    cosine = jnp.cos(angles)[:, None, :]
    sine_part = jnp.sin(angles)[:, None, :]
    former = values[..., :half_size]
    latter = values[..., half_size:]
    return jnp.concatenate(
        [former * cosine - latter * sine_part, latter * cosine + former * sine_part], axis=-1
    )


def slot_tables(route_rows):
    flat_routes = route_rows.reshape(-1)
    assigned = flat_routes.shape[0]
    chosen = (flat_routes[:, None] == jnp.arange(EXPERTS, dtype=jnp.int32)[None, :]).astype(
        jnp.int32
    )
    running = jnp.cumsum(chosen, axis=0)
    slot_index = jnp.sum(running * chosen, axis=1) - 1
    targets = flat_routes * CAP + slot_index
    slot_owner = (
        jnp.full((EXPERTS * CAP,), assigned, jnp.int32)
        .at[targets]
        .set(jnp.arange(assigned, dtype=jnp.int32))
    )
    return (targets, slot_owner)


def step_sizes():
    return (
        MODEL_DIMENSION ** (-0.5),
        (QUERY_HEADS * HEAD_DIMENSION // 64) ** (-0.5),
        (4 * MODEL_DIMENSION) ** (-0.5),
        MODEL_DIMENSION ** (-0.5),
        (F // 64) ** (-0.5),
        0.3,
    )


def adam_step(weight, gradient, moment, second, step_size, decay_value):
    moment_new = BETA_ONE * moment + (1.0 - BETA_ONE) * gradient
    second_new = BETA_TWO * second + (1.0 - BETA_TWO) * gradient * gradient
    corrected = (
        moment_new
        / (1.0 - BETA_ONE**STEP)
        / (jnp.sqrt(second_new / (1.0 - BETA_TWO**STEP)) + ADAM_EPS)
    )
    return (weight - step_size * (corrected + decay_value * weight), moment_new, second_new)


def update_all(weights, gradients, moments, seconds, factor):
    sizes_list = step_sizes()
    decays = (DECAY_RATE, DECAY_RATE, DECAY_RATE, DECAY_RATE, DECAY_RATE, 0.0)
    new_weights = []
    new_moments = []
    new_seconds = []
    for position in range(6):
        weight_new, moment_new, second_new = adam_step(
            weights[position],
            gradients[position] * factor,
            moments[position],
            seconds[position],
            sizes_list[position],
            decays[position],
        )
        new_weights.append(weight_new)
        new_moments.append(moment_new)
        new_seconds.append(second_new)
    return (new_weights, new_moments, new_seconds)


def norm_backward(values, norm_scale, gain_row, upstream):
    scaled = gain_row * upstream
    gain_grad = jnp.sum(values * norm_scale * upstream, axis=0)
    value_grad = norm_scale * scaled - values * norm_scale**3 * jnp.mean(
        values * scaled, axis=-1, keepdims=True
    )
    return (value_grad, gain_grad)


def masked_scores(
    query_part, key_block_rows, position_part, segment_part, key_positions, key_segments
):
    scores = jnp.einsum(
        "bhgd,khd->hgbk", query_part, key_block_rows, preferred_element_type=jnp.float32
    ) * query_part.shape[-1] ** (-0.5)
    allowed = (segment_part[:, None] == key_segments[None, :]) & (
        key_positions[None, :] <= position_part[:, None]
    )
    return jnp.where(allowed, scores, MASKED_SCORE)


def split_blocks(queries, query_positions, query_segments, kv_heads):
    row_count, head_count, head_size = queries.shape
    block_rows = min(512, row_count)
    block_count = row_count // block_rows
    grouped = queries.reshape(block_count, block_rows, kv_heads, head_count // kv_heads, head_size)
    return (
        grouped,
        query_positions.reshape(block_count, block_rows),
        query_segments.reshape(block_count, block_rows),
    )


def attend_forward(
    queries,
    key_block_rows,
    value_block_rows,
    query_positions,
    query_segments,
    key_positions,
    key_segments,
):
    grouped, position_blocks, segment_blocks = split_blocks(
        queries, query_positions, query_segments, key_block_rows.shape[1]
    )

    def one_block(packed):
        query_part, position_part, segment_part = packed
        scores = masked_scores(
            query_part, key_block_rows, position_part, segment_part, key_positions, key_segments
        )
        highest = jnp.max(scores, axis=-1, keepdims=True)
        exponent = jnp.exp(scores - highest)
        totals = jnp.sum(exponent, axis=-1, keepdims=True)
        weights = (exponent / totals).astype(jnp.bfloat16)
        mixed_rows = jnp.einsum(
            "hgbk,khd->bhgd", weights, value_block_rows, preferred_element_type=jnp.float32
        )
        return (mixed_rows, highest[..., 0] + jnp.log(totals[..., 0]))

    mixed_rows, log_sums = lax.map(one_block, (grouped, position_blocks, segment_blocks))
    return (mixed_rows.reshape(queries.shape), log_sums)


def attend_backward(
    queries,
    key_block_rows,
    value_block_rows,
    query_positions,
    query_segments,
    key_positions,
    key_segments,
    log_sums,
    out_grad,
):
    grouped, position_blocks, segment_blocks = split_blocks(
        queries, query_positions, query_segments, key_block_rows.shape[1]
    )
    grad_blocks = out_grad.reshape(grouped.shape)
    scale_value = queries.shape[-1] ** (-0.5)

    def one_block(state_pair, packed):
        key_grad, value_grad = state_pair
        query_part, position_part, segment_part, log_part, grad_part = packed
        scores = masked_scores(
            query_part, key_block_rows, position_part, segment_part, key_positions, key_segments
        )
        weights = jnp.exp(scores - log_part[..., None])
        weight_grad = jnp.einsum(
            "bhgd,khd->hgbk", grad_part, value_block_rows, preferred_element_type=jnp.float32
        )
        score_grad = (
            weights * (weight_grad - jnp.sum(weights * weight_grad, axis=-1, keepdims=True))
        ).astype(jnp.bfloat16)
        query_grad = (
            jnp.einsum(
                "hgbk,khd->bhgd", score_grad, key_block_rows, preferred_element_type=jnp.float32
            )
            * scale_value
        )
        key_grad = (
            key_grad
            + jnp.einsum(
                "hgbk,bhgd->khd", score_grad, query_part, preferred_element_type=jnp.float32
            )
            * scale_value
        )
        value_grad = value_grad + jnp.einsum(
            "hgbk,bhgd->khd",
            weights.astype(jnp.bfloat16),
            grad_part,
            preferred_element_type=jnp.float32,
        )
        return ((key_grad, value_grad), query_grad)

    zero_rows = jnp.zeros(key_block_rows.shape, jnp.float32)
    (key_grad, value_grad), query_grad = lax.scan(
        one_block,
        (zero_rows, zero_rows),
        (grouped, position_blocks, segment_blocks, log_sums, grad_blocks),
    )
    return (query_grad.reshape(queries.shape), key_grad, value_grad)


def shards(
    tokens,
    cotangent,
    segment_ids,
    route_ids,
    query_key_value_weight,
    out_weight,
    router_weight,
    expert_in,
    expert_down,
    norm_gains,
    query_key_value_moment,
    out_moment,
    router_moment,
    in_moment,
    down_moment,
    gains_moment,
    query_key_value_second,
    out_second,
    router_second,
    in_second,
    down_second,
    gains_second,
):
    qkv_low, out_low, router_low, gains_low = (
        lax.all_gather(
            query_key_value_weight.astype(jnp.bfloat16), ("seq", "fsdp"), axis=0, tiled=True
        ),
        lax.all_gather(out_weight.astype(jnp.bfloat16), ("seq", "fsdp"), axis=0, tiled=True),
        lax.all_gather(router_weight.astype(jnp.bfloat16), ("seq", "fsdp"), axis=0, tiled=True),
        lax.all_gather(norm_gains.astype(jnp.bfloat16), ("seq", "fsdp"), axis=0, tiled=True),
    )
    in_low, down_low = (
        lax.all_gather(expert_in.astype(jnp.bfloat16), ("seq", "fsdp"), axis=1, tiled=True),
        lax.all_gather(expert_down.astype(jnp.bfloat16), ("seq", "fsdp"), axis=1, tiled=True),
    )
    pack_segments = lax.all_gather(segment_ids[0], "seq", axis=0, tiled=True)
    local_rows = tokens.shape[1]
    sequence_length = local_rows * lax.axis_size("seq")
    seq_index = lax.axis_index("seq")
    own_positions = seq_index * local_rows + jnp.arange(local_rows, dtype=jnp.int32)
    pack_positions = jnp.arange(sequence_length, dtype=jnp.int32)
    rotation_positions = own_positions.astype(jnp.float32)
    query_width_total = QUERY_HEADS * HEAD_DIMENSION
    key_width_total = KEY_VALUE_HEADS * HEAD_DIMENSION
    inputs = tokens[0].astype(jnp.float32)
    attn_gain = gains_low[:, 0].astype(jnp.float32)
    ffn_gain = gains_low[:, 1].astype(jnp.float32)
    first_scale = rms_scale(inputs)
    normed = (inputs * first_scale * attn_gain).astype(jnp.bfloat16)
    mixed_query_key_value = jnp.dot(normed, qkv_low, preferred_element_type=jnp.float32)
    queries = rotation_embedding(
        mixed_query_key_value[:, :query_width_total].reshape(
            local_rows, QUERY_HEADS, HEAD_DIMENSION
        ),
        rotation_positions,
    ).astype(jnp.bfloat16)
    key_block_rows = rotation_embedding(
        mixed_query_key_value[:, query_width_total : query_width_total + key_width_total].reshape(
            local_rows, KEY_VALUE_HEADS, HEAD_DIMENSION
        ),
        rotation_positions,
    ).astype(jnp.bfloat16)
    value_block_rows = (
        mixed_query_key_value[:, query_width_total + key_width_total :]
        .reshape(local_rows, KEY_VALUE_HEADS, HEAD_DIMENSION)
        .astype(jnp.bfloat16)
    )
    head_queries, head_keys, head_values = (
        lax.all_to_all(queries, "seq", split_axis=1, concat_axis=0, tiled=True),
        lax.all_to_all(key_block_rows, "seq", split_axis=1, concat_axis=0, tiled=True),
        lax.all_to_all(value_block_rows, "seq", split_axis=1, concat_axis=0, tiled=True),
    )
    head_mixed, log_sums = attend_forward(
        head_queries,
        head_keys,
        head_values,
        pack_positions,
        pack_segments,
        pack_positions,
        pack_segments,
    )
    attended = lax.all_to_all(
        head_mixed.astype(jnp.bfloat16), "seq", split_axis=0, concat_axis=1, tiled=True
    )
    attended_flat = attended.reshape(local_rows, query_width_total)
    middle = inputs + jnp.dot(attended_flat, out_low, preferred_element_type=jnp.float32)
    second_scale = rms_scale(middle)
    normed_ffn = (middle * second_scale * ffn_gain).astype(jnp.bfloat16)
    logits = jnp.dot(
        normed_ffn.astype(jnp.float32), router_low.astype(jnp.float32), precision=PRECISE
    )
    highest = jnp.max(logits, axis=-1, keepdims=True)
    exponent = jnp.exp(logits - highest)
    router_probs = exponent / jnp.sum(exponent, axis=-1, keepdims=True)
    own_routes = route_ids[0]
    chosen = (own_routes[..., None] == jnp.arange(EXPERTS, dtype=jnp.int32)).astype(jnp.float32)
    gate_rows = jnp.sum(chosen * router_probs[:, None, :], axis=-1)
    targets, slot_owner = slot_tables(own_routes)
    model_width = inputs.shape[1]
    padded = jnp.concatenate([normed_ffn, jnp.zeros((1, model_width), jnp.bfloat16)], axis=0)
    picked = padded[slot_owner // TOPK].reshape(EXPERTS, CAP, model_width)
    joined = jnp.einsum("ecd,edf->ecf", picked, in_low, preferred_element_type=jnp.float32)
    hidden_units = joined.shape[-1] // 2
    gate_part = joined[..., :hidden_units]
    up_part = joined[..., hidden_units:]
    sigmoid_gate = jax.nn.sigmoid(gate_part)
    silu_gate = gate_part * sigmoid_gate
    activated = (silu_gate * up_part).astype(jnp.bfloat16)
    result = jnp.einsum("ecf,efd->ecd", activated, down_low, preferred_element_type=jnp.float32)
    per_route = result.reshape(EXPERTS * CAP, model_width)[targets].reshape(
        local_rows, TOPK, model_width
    )
    output = (middle + jnp.sum(gate_rows[..., None] * per_route, axis=1)).astype(jnp.bfloat16)
    back_in, back_down = (in_low, down_low)
    top_grad = cotangent[0].astype(jnp.float32)
    gate_grad = jnp.sum(per_route * top_grad[:, None, :], axis=-1)
    route_grad = (gate_rows[..., None] * top_grad[:, None, :]).reshape(
        local_rows * TOPK, model_width
    )
    slot_grad = (
        jnp.concatenate([route_grad, jnp.zeros((1, model_width), jnp.float32)], axis=0)[slot_owner]
        .reshape(EXPERTS, CAP, model_width)
        .astype(jnp.bfloat16)
    )
    down_grad = jnp.einsum("ecf,ecd->efd", activated, slot_grad, preferred_element_type=jnp.float32)
    act_grad = jnp.einsum("ecd,efd->ecf", slot_grad, back_down, preferred_element_type=jnp.float32)
    joined_grad = jnp.concatenate(
        [
            act_grad * up_part * sigmoid_gate * (1.0 + gate_part * (1.0 - sigmoid_gate)),
            act_grad * silu_gate,
        ],
        axis=-1,
    ).astype(jnp.bfloat16)
    in_grad = jnp.einsum("ecd,ecf->edf", picked, joined_grad, preferred_element_type=jnp.float32)
    picked_grad = jnp.einsum(
        "ecf,edf->ecd", joined_grad, back_in, preferred_element_type=jnp.float32
    ).reshape(EXPERTS * CAP, model_width)
    ffn_grad = jnp.sum(picked_grad[targets].reshape(local_rows, TOPK, model_width), axis=1)
    prob_grad = jnp.sum(chosen * gate_grad[..., None], axis=1)
    logit_grad = router_probs * (
        prob_grad - jnp.sum(router_probs * prob_grad, axis=-1, keepdims=True)
    )
    router_grad = jnp.dot(normed_ffn.astype(jnp.float32).T, logit_grad, precision=PRECISE)
    ffn_grad = ffn_grad + jnp.dot(logit_grad, router_low.astype(jnp.float32).T, precision=PRECISE)
    middle_grad, ffn_gain_grad = norm_backward(middle, second_scale, ffn_gain, ffn_grad)
    middle_grad = middle_grad + top_grad
    branch_grad = middle_grad.astype(jnp.bfloat16)
    out_grad = jnp.dot(attended_flat.T, branch_grad, preferred_element_type=jnp.float32)
    attended_grad = (
        jnp.dot(branch_grad, out_low.T, preferred_element_type=jnp.float32)
        .reshape(local_rows, QUERY_HEADS, HEAD_DIMENSION)
        .astype(jnp.bfloat16)
    )
    head_grad = lax.all_to_all(attended_grad, "seq", split_axis=1, concat_axis=0, tiled=True)
    query_grad, key_grad, value_grad = attend_backward(
        head_queries,
        head_keys,
        head_values,
        pack_positions,
        pack_segments,
        pack_positions,
        pack_segments,
        log_sums,
        head_grad,
    )
    query_grad, key_grad, value_grad = (
        lax.all_to_all(
            query_grad.astype(jnp.bfloat16), "seq", split_axis=0, concat_axis=1, tiled=True
        ),
        lax.all_to_all(
            key_grad.astype(jnp.bfloat16), "seq", split_axis=0, concat_axis=1, tiled=True
        ),
        lax.all_to_all(
            value_grad.astype(jnp.bfloat16), "seq", split_axis=0, concat_axis=1, tiled=True
        ),
    )
    mixed_grad = jnp.concatenate(
        [
            rotation_embedding(query_grad.astype(jnp.float32), -rotation_positions).reshape(
                local_rows, query_width_total
            ),
            rotation_embedding(key_grad.astype(jnp.float32), -rotation_positions).reshape(
                local_rows, key_width_total
            ),
            value_grad.astype(jnp.float32).reshape(local_rows, key_width_total),
        ],
        axis=1,
    ).astype(jnp.bfloat16)
    qkv_grad = jnp.dot(normed.T, mixed_grad, preferred_element_type=jnp.float32)
    normed_grad = jnp.dot(mixed_grad, qkv_low.T, preferred_element_type=jnp.float32)
    input_grad, attn_gain_grad = norm_backward(inputs, first_scale, attn_gain, normed_grad)
    input_grad = input_grad + middle_grad
    gains_grad = jnp.stack([attn_gain_grad, ffn_gain_grad], axis=1)
    qkv_sum, out_sum, router_sum, gains_sum = (
        lax.psum_scatter(qkv_grad, ("seq", "fsdp"), scatter_dimension=0, tiled=True),
        lax.psum_scatter(out_grad, ("seq", "fsdp"), scatter_dimension=0, tiled=True),
        lax.psum_scatter(router_grad, ("seq", "fsdp"), scatter_dimension=0, tiled=True),
        lax.psum_scatter(gains_grad, ("seq", "fsdp"), scatter_dimension=0, tiled=True),
    )
    in_sum, down_sum = (
        lax.psum_scatter(in_grad, ("seq", "fsdp"), scatter_dimension=1, tiled=True),
        lax.psum_scatter(down_grad, ("seq", "fsdp"), scatter_dimension=1, tiled=True),
    )
    square_total = (
        jnp.sum(qkv_sum * qkv_sum)
        + jnp.sum(out_sum * out_sum)
        + jnp.sum(router_sum * router_sum)
        + jnp.sum(in_sum * in_sum)
        + jnp.sum(down_sum * down_sum)
        + jnp.sum(gains_sum * gains_sum)
    )
    grad_norm = jnp.sqrt(lax.psum(square_total, ("seq", "fsdp")))
    factor = CLIP_NORM / jnp.maximum(grad_norm, CLIP_NORM)
    new_weights, new_moments, new_seconds = update_all(
        (query_key_value_weight, out_weight, router_weight, expert_in, expert_down, norm_gains),
        (qkv_sum, out_sum, router_sum, in_sum, down_sum, gains_sum),
        (query_key_value_moment, out_moment, router_moment, in_moment, down_moment, gains_moment),
        (query_key_value_second, out_second, router_second, in_second, down_second, gains_second),
        factor,
    )
    qkv_new, out_new, router_new, in_new, down_new, gains_new = new_weights
    (
        qkv_moment_new,
        out_moment_new,
        router_moment_new,
        in_moment_new,
        down_moment_new,
        gains_moment_new,
    ) = new_moments
    (
        qkv_second_new,
        out_second_new,
        router_second_new,
        in_second_new,
        down_second_new,
        gains_second_new,
    ) = new_seconds
    return (
        output[None],
        input_grad.astype(jnp.bfloat16)[None],
        grad_norm,
        qkv_new,
        out_new,
        router_new,
        in_new,
        down_new,
        gains_new,
        qkv_moment_new,
        out_moment_new,
        router_moment_new,
        in_moment_new,
        down_moment_new,
        gains_moment_new,
        qkv_second_new,
        out_second_new,
        router_second_new,
        in_second_new,
        down_second_new,
        gains_second_new,
    )


def solution(mesh):
    placed = (
        P("fsdp", "seq", None),
        P("fsdp", "seq", None),
        P("fsdp", "seq"),
        P("fsdp", "seq", None),
        P(("seq", "fsdp"), None),
        P(("seq", "fsdp"), None),
        P(("seq", "fsdp"), None),
        P(None, ("seq", "fsdp"), None),
        P(None, ("seq", "fsdp"), None),
        P(("seq", "fsdp"), None),
        P(("seq", "fsdp"), None),
        P(("seq", "fsdp"), None),
        P(("seq", "fsdp"), None),
        P(None, ("seq", "fsdp"), None),
        P(None, ("seq", "fsdp"), None),
        P(("seq", "fsdp"), None),
        P(("seq", "fsdp"), None),
        P(("seq", "fsdp"), None),
        P(("seq", "fsdp"), None),
        P(None, ("seq", "fsdp"), None),
        P(None, ("seq", "fsdp"), None),
        P(("seq", "fsdp"), None),
    )
    return jax.shard_map(
        shards,
        mesh=mesh,
        in_specs=placed,
        out_specs=(
            P("fsdp", "seq", None),
            P("fsdp", "seq", None),
            P(),
            P(("seq", "fsdp"), None),
            P(("seq", "fsdp"), None),
            P(("seq", "fsdp"), None),
            P(None, ("seq", "fsdp"), None),
            P(None, ("seq", "fsdp"), None),
            P(("seq", "fsdp"), None),
            P(("seq", "fsdp"), None),
            P(("seq", "fsdp"), None),
            P(("seq", "fsdp"), None),
            P(None, ("seq", "fsdp"), None),
            P(None, ("seq", "fsdp"), None),
            P(("seq", "fsdp"), None),
            P(("seq", "fsdp"), None),
            P(("seq", "fsdp"), None),
            P(("seq", "fsdp"), None),
            P(None, ("seq", "fsdp"), None),
            P(None, ("seq", "fsdp"), None),
            P(("seq", "fsdp"), None),
        ),
        check_vma=False,
    )
```

profile of v0, /device:TPU:1, one launch (start us, length us, event | category | flops | bytes accessed | tf_op | source)
XLA Modules:
  0.0 2396.5 jit_solution(8841147424685123054)
XLA Ops:
  15.2 42.9 %all-gather.1 = bf16[32,48,2]{1,2,0:T(2,128)(2,1)S(1)} all-gather(bf16[1,48,2]{1,2,0:T(2,128)(2,1)S(1)} %convert_bitcast_fusion.3), channel_id=1, replica_groups=mesh['seq'=2,'fsdp'=16] {'seq','fsdp'}, dimensions={0}, use_global_device_ids=true | all-gather | bytes 6336 | tf_op jit(solution)/shard_map/all_gather | solution.py:259
  65.1 18.5 all-gather.8.cloned.1.call-done
  83.6 5.6 fusion.82
  113.5 19.8 all-to-all-done
  137.9 7.6 all-gather
  150.0 23.5 while.28
  183.0 43.8 %all-gather.2 = bf16[32,48,8]{1,2,0:T(8,128)(2,1)S(1)} all-gather(bf16[1,48,8]{1,2,0:T(8,128)(2,1)S(1)} %convert_bitcast_fusion.2), channel_id=1, replica_groups=mesh['seq'=2,'fsdp'=16] {'seq','fsdp'}, dimensions={0}, use_global_device_ids=true | all-gather | bytes 25344 | tf_op jit(solution)/shard_map/all_gather | solution.py:258
  227.0 7.8 mul.733
  234.8 14.9 mul.734
  249.8 8.5 scatter_custom_fusion
  261.2 5.3 multiply_reduce_fusion.4
  271.6 9.7 broadcast_multiply_fusion
  281.3 5.8 concatenate.33
  287.1 20.1 gather_fusion.2
  307.2 9.6 gather_fusion
  316.8 61.4 %all-gather.12.cloned.1.call-done = bf16[8,1536,1536]{2,1,0:T(8,128)(2,1)} async-done(((bf16[8,48,1536]{2,1,0:T(8,128)(2,1)}), bf16[8,1536,1536]{2,1,0:T(8,128)(2,1)}) %all-gather.12.cloned.1.call-update) | async-done | bytes 37748752 | tf_op jit(solution)/shard_map/all_gather | solution.py:262
  378.1 26.1 %fusion.114 = f32[8,320,1536]{2,1,0:T(8,128)} fusion(bf16[8,320,1536]{2,1,0:T(8,128)(2,1)} %bitcast.355, bf16[8,1536,1536]{2,1,0:T(8,128)(2,1)} %all-gather.12.cloned.1.call-done), kind=kOutput, calls=%fused_computation.224 | convolution fusion | flops 12079595520 | bytes 61341696 | tf_op jit(solution)/shard_map/ecd,edf->ecf/dot_general | solution.py:331
  404.3 100.1 %all-gather.14.cloned.1.call-done = bf16[8,768,1536]{2,1,0:T(8,128)(2,1)} async-done(((bf16[8,24,1536]{2,1,0:T(8,128)(2,1)}), bf16[8,768,1536]{2,1,0:T(8,128)(2,1)}) %all-gather.14.cloned.1.call-update) | async-done | bytes 18874384 | tf_op jit(solution)/shard_map/all_gather | solution.py:263
  504.4 19.6 multiply_convert_fusion.1
  524.0 17.4 fusion.115
  541.4 19.7 gather_fusion.1
  561.1 14.8 reshape.479
  576.0 17.4 multiply_reduce_fusion
  594.6 24.3 %fusion.61 = f32[8,320,1536]{2,1,0:T(8,128)} fusion(bf16[8,1536,1536]{2,1,0:T(8,128)(2,1)} %all-gather.12.cloned.1.call-done, bf16[8,320,768]{2,1,0:T(8,128)(2,1)} %get-tuple-element.286, bf16[8,320,768]{2,1,0:T(8,128)(2,1)} %get-tuple-element.285), kind=kOutput, calls=%fused_computation.87 | convolution fusion | flops 12095324160 | bytes 61341696 | tf_op jit(solution)/shard_map/ecf,edf->ecd/dot_general | solution.py:364
  618.9 19.7 gather_fusion.3
  638.6 14.7 reshape.481
  653.3 13.0 reduce_sum.204
  684.2 19.1 all-to-all-done.4
  707.7 68.9 %while.29 = (s32[]{:T(128)}, f32[1024,1,128]{0,2,1:T(8,128)S(1)}, f32[1024,1,128]{0,2,1:T(8,128)}, bf16[2,512,1,6,128]{4,1,0,3,2:T(8,128)(2,1)}, bf16[2,512,1,6,...) while((s32[]{:T(128)}, f32[1024,1,128]{0,2,1:T(8,128)S(1)}, ...), condition=%wide.region_21.22_spmd.clone, body=%wide.region_19.21_spmd.clone.sunk | while | flops 4076336128 | bytes 192262944 | solution.py:221
  710.2 7.3 fusion.174
  718.4 6.9 fusion.175
  734.7 7.3 fusion.177
  744.5 7.3 fusion.174
  752.8 6.9 fusion.175
  769.1 7.5 fusion.177
  804.0 16.9 all-to-all-done.5
  826.9 9.6 fusion.65
  838.0 6.6 fusion.78
  844.6 10.2 fusion.76
  854.8 20.8 fusion.116
  876.0 35.2 %fusion.60 = f32[8,1536,1536]{2,1,0:T(8,128)} fusion(bf16[8,320,1536]{2,1,0:T(8,128)(2,1)} %bitcast.356, bf16[8,320,768]{2,1,0:T(8,128)(2,1)} %get-tuple-element.286, bf16[8,320,768]{2,1,0:T(8,128)(2,1)} %get-tuple-element.285), kind=kOutput, calls=%fused_computation.86 | convolution fusion | flops 12095324160 | bytes 91226112 | tf_op jit(solution)/shard_map/ecd,ecf->edf/dot_general | solution.py:363
  912.7 88.7 %reduce-scatter.21.cloned.1.call-done = f32[48,2]{1,0:T(8,128)} async-done(((f32[1536,2]{1,0:T(8,128)}), f32[48,2]{1,0:T(8,128)}) %reduce-scatter.21.cloned.1.call-update) | async-done | bytes 400
  1002.8 138.9 %reduce-scatter.13.cloned.1.call-done = f32[48,1536]{1,0:T(8,128)} async-done(((f32[1536,1536]{1,0:T(8,128)}), f32[48,1536]{1,0:T(8,128)}) %reduce-scatter.13.cloned.1.call-update) | async-done | bytes 294928 | tf_op jit(solution)/shard_map/reduce_scatter | solution.py:425
  1143.3 160.5 %reduce-scatter.11.cloned.1.call-done = f32[48,2048]{1,0:T(8,128)} async-done(((f32[1536,2048]{1,0:T(8,128)}), f32[48,2048]{1,0:T(8,128)}) %reduce-scatter.11.cloned.1.call-update) | async-done | bytes 393232 | tf_op jit(solution)/shard_map/reduce_scatter | solution.py:424
  1307.5 349.2 %reduce-scatter.17.cloned.1.call-done = f32[8,24,1536]{2,1,0:T(8,128)} async-done(((f32[8,768,1536]{2,1,0:T(8,128)}), f32[8,24,1536]{2,1,0:T(8,128)}) %reduce-scatter.17.cloned.1.call-update) | async-done | bytes 1179664 | tf_op jit(solution)/shard_map/reduce_scatter | solution.py:431
  1658.8 664.2 %reduce-scatter.15.cloned.1.call-done = f32[8,48,1536]{2,1,0:T(8,128)} async-done(((f32[8,1536,1536]{2,1,0:T(8,128)}), f32[8,48,1536]{2,1,0:T(8,128)}) %reduce-scatter.15.cloned.1.call-update) | async-done | bytes 2359312 | tf_op jit(solution)/shard_map/reduce_scatter | solution.py:430
  2332.3 39.5 %psum.7 = f32[]{:T(128)} all-reduce(f32[]{:T(128)S(6)} %add.288), channel_id=1, replica_groups=mesh['seq'=2,'fsdp'=16] {'seq','fsdp'}, use_global_device_ids=true, to_apply=%region_37.38 | all-reduce | flops 1 | bytes 8 | tf_op jit(solution)/shard_map/psum | solution.py:441
  2379.6 6.1 multiply_subtract_fusion
  (373 shorter events, 197.5 us)
Async XLA Ops:
  7.2 76.4 %all-gather.8.cloned.1.call-start = ((), (), s32[]{:S(2)}) async-start(), calls=%async_computation.14 | async-start | bytes 6488064 | tf_op jit(solution)/shard_map/all_gather | solution.py:254
  9.1 252.2 %all-gather.10.cloned.1.call-start = ((), (), s32[]{:S(2)}) async-start(), calls=%async_computation.15 | async-start | bytes 4866048 | tf_op jit(solution)/shard_map/all_gather | solution.py:257
  10.8 367.3 %all-gather.12.cloned.1.call-start = ((), (), s32[]{:S(2)}) async-start(), calls=%async_computation.16 | async-start | bytes 38928384 | tf_op jit(solution)/shard_map/all_gather | solution.py:262
  13.7 50.5 %copy-start.25 = (bf16[1,512,1536]{2,1,0:T(8,128)(2,1)S(1)}, bf16[1,512,1536]{2,1,0:T(8,128)(2,1)}, u32[]{:S(2)}) copy-start(bf16[1,512,1536]{2,1,0:T(8,128)(2,1)} %param.26) | copy-start | bytes 4718596
  13.7 490.7 %all-gather.14.cloned.1.call-start = ((), (), s32[]{:S(2)}) async-start(), calls=%async_computation.17 | async-start | bytes 19464192 | tf_op jit(solution)/shard_map/all_gather | solution.py:263
  64.0 25.2 %copy-start.66 = (f32[1536]{0:T(1024)}, f32[1536]{0:T(1024)S(1)}, u32[]{:S(2)}) copy-start(f32[1536]{0:T(1024)S(1)} %get-tuple-element.216) | copy-start | bytes 18436
  65.1 24.1 %copy-start.79 = (f32[512]{0:T(512)}, f32[512]{0:T(512)S(1)}, u32[]{:S(2)}) copy-start(f32[512]{0:T(512)S(1)} %get-tuple-element.307) | copy-start | bytes 6148
  95.2 10.7 all-to-all-start.1
  105.9 27.3 %all-to-all-start = ((bf16[512,12,128]{0,2,1:T(8,128)(2,1)}), bf16[512,12,128]{0,2,1:T(8,128)(2,1)S(1)}, u32[]{:S(2)}, u32[]{:S(2)}) async-start(bf16[512,12,128]{0,2,1:T(8,128)(2,1)} %pad_maximum_fusion.4), calls=%async_computation | async-start | bytes 3145728 | tf_op jit(solution)/shard_map/all_to_all | solution.py:298
  109.6 28.2 %copy-start.83 = (s32[1,512]{1,0:T(1,128)S(1)}, s32[1,512]{1,0:T(1,128)}, u32[]{:S(2)}) copy-start(s32[1,512]{1,0:T(1,128)} %param.28) | copy-start | bytes 6148
  134.4 14.2 all-to-all-start.2
  178.1 80.1 %all-to-all-start.3 = ((bf16[1024,6,128]{2,1,0:T(8,128)(2,1)}), bf16[1024,6,128]{2,1,0:T(8,128)(2,1)}, u32[]{:S(2)}, u32[]{:S(2)}) async-start(bf16[1024,6,128]{2,1,0:T(8,128)(2,1)} %copy.222), calls=%async_computation.3 | async-start | bytes 4194304 | tf_op jit(solution)/shard_map/all_to_all | solution.py:311
  227.0 41.6 %copy-start.51 = (bf16[1536,8]{0,1:T(8,128)(2,1)}, bf16[1536,8]{0,1:T(8,128)(2,1)S(1)}, u32[]{:S(2)}) copy-start(bf16[1536,8]{0,1:T(8,128)(2,1)S(1)} %reshape.540) | copy-start | bytes 73732
  524.0 17.4 copy-start.15
  561.1 14.8 copy-start.6
  561.1 14.8 copy-start.30
  575.9 18.5 copy-start.61
  575.9 18.6 copy-start.50
  575.9 18.6 copy-start.65
  575.9 18.6 copy-start.72
  594.5 71.8 %copy-start.47 = (f32[512,8]{0,1:T(8,128)}, f32[512,8]{0,1:T(8,128)S(1)}, u32[]{:S(2)}) copy-start(f32[512,8]{0,1:T(8,128)S(1)} %select_reduce_fusion) | copy-start | bytes 49156
  594.6 71.8 %copy-start.73 = (f32[512]{0:T(512)}, f32[512]{0:T(512)S(1)}, u32[]{:S(2)}) copy-start(f32[512]{0:T(512)S(1)} %multiply_reduce_fusion.9) | copy-start | bytes 6148
  679.4 23.8 all-to-all-start.4
  684.1 23.6 copy-start.3
  684.1 23.6 copy-start.5
  684.1 23.5 copy-start.18
  684.1 23.5 copy-start.37
  684.1 23.5 copy-start.54
  684.1 23.5 copy-start.56
  684.2 23.5 copy-start.58
  776.6 13.5 copy-start.38
  776.6 13.7 copy-start.68
  778.9 7.5 all-to-all-start.6
  786.4 7.9 all-to-all-start.7
  794.3 26.7 %all-to-all-start.5 = ((bf16[1024,6,128]{2,1,0:T(8,128)(2,1)}), bf16[1024,6,128]{2,1,0:T(8,128)(2,1)}, u32[]{:S(2)}, u32[]{:S(2)}) async-start(bf16[1024,6,128]{2,1,0:T(8,128)(2,1)} %copy.235), calls=%async_computation.5 | async-start | bytes 4194304 | tf_op jit(solution)/shard_map/all_to_all | solution.py:396
  799.1 112.1 %reduce-scatter.19.cloned.1.call-start = ((), (), s32[]{:S(2)}) async-start(), calls=%async_computation.22 | async-start | bytes 811008
  801.9 199.5 %reduce-scatter.21.cloned.1.call-start = ((), (), s32[]{:S(2)}) async-start(), calls=%async_computation.23 | async-start | bytes 811008
  837.7 304.0 %reduce-scatter.13.cloned.1.call-start = ((), (), s32[]{:S(2)}) async-start(), calls=%async_computation.19 | async-start | bytes 9732096 | tf_op jit(solution)/shard_map/reduce_scatter | solution.py:425
  844.6 459.3 %reduce-scatter.11.cloned.1.call-start = ((), (), s32[]{:S(2)}) async-start(), calls=%async_computation.18 | async-start | bytes 12976128 | tf_op jit(solution)/shard_map/reduce_scatter | solution.py:424
  854.8 801.9 %reduce-scatter.17.cloned.1.call-start = ((), (), s32[]{:S(2)}) async-start(), calls=%async_computation.21 | async-start | bytes 38928384 | tf_op jit(solution)/shard_map/reduce_scatter | solution.py:431
  875.7 1447.3 %reduce-scatter.15.cloned.1.call-start = ((), (), s32[]{:S(2)}) async-start(), calls=%async_computation.20 | async-start | bytes 77856768 | tf_op jit(solution)/shard_map/reduce_scatter | solution.py:430
  911.2 1416.6 %copy-start.78 = (f32[512]{0:T(512)S(1)}, f32[512]{0:T(512)}, u32[]{:S(2)}) copy-start(f32[512]{0:T(512)} %get-tuple-element.306) | copy-start | bytes 6148
  2327.8 44.7 %copy-start.85 = (f32[48,2]{0,1:T(2,128)S(1)}, f32[48,2]{0,1:T(2,128)}, u32[]{:S(2)}) copy-start(f32[48,2]{0,1:T(2,128)} %param.35) | copy-start | bytes 1156
  2327.8 44.7 %copy-start.86 = (f32[48,2]{0,1:T(2,128)S(1)}, f32[48,2]{0,1:T(2,128)}, u32[]{:S(2)}) copy-start(f32[48,2]{0,1:T(2,128)} %param.41) | copy-start | bytes 1156
  2327.8 44.7 %copy-start.87 = (f32[48,2]{0,1:T(2,128)S(1)}, f32[48,2]{0,1:T(2,128)}, u32[]{:S(2)}) copy-start(f32[48,2]{0,1:T(2,128)} %param.47) | copy-start | bytes 1156
  2327.9 45.3 %copy-start.76 = (f32[48,8]{0,1:T(8,128)S(1)}, f32[48,8]{0,1:T(8,128)}, u32[]{:S(2)}) copy-start(f32[48,8]{0,1:T(8,128)} %param.32) | copy-start | bytes 4612
  2327.9 45.3 %copy-start.81 = (f32[48,8]{0,1:T(8,128)S(1)}, f32[48,8]{0,1:T(8,128)}, u32[]{:S(2)}) copy-start(f32[48,8]{0,1:T(8,128)} %param.38) | copy-start | bytes 4612
  2327.9 45.3 %copy-start.82 = (f32[48,8]{0,1:T(8,128)S(1)}, f32[48,8]{0,1:T(8,128)}, u32[]{:S(2)}) copy-start(f32[48,8]{0,1:T(8,128)} %param.44) | copy-start | bytes 4612
  (64 other events, 384.2 us)
Sparse Core Ops, SparseCore 0:
  11.5 72.0 all-gather.7
  87.1 66.8 all-gather.9
  157.6 220.5 all-gather.11
  381.5 122.7 all-gather.13
  805.3 95.8 reduce-scatter.18
  906.8 94.5 reduce-scatter.20
  1007.3 134.3 reduce-scatter.12
  1148.8 155.0 reduce-scatter.10
  1310.3 346.3 reduce-scatter.16
  1664.1 658.8 reduce-scatter.14
where the time goes:
time: 2410 us; the launch traced here: 2400 us
  waiting for transfers between devices  1640 us (68%)
  matrix products  252 us (10%)
  local copies, waits for them, and re-layouts  195 us (8%)
  blocking collectives  134 us (6%)
  other arithmetic  121 us (5%)
  starting transfers between devices  32.8 us (1%)
    reduce_scatter x1, waiting for transfers between devices, shards(): lax.psum_scatter(in_grad, ('seq', 'fsdp'), scatter_dimension=1, tiled=True)  664 us
    reduce_scatter x1, waiting for transfers between devices, shards(): lax.psum_scatter(down_grad, ('seq', 'fsdp'), scatter_dimension=1, tiled=T...  349 us
    reduce_scatter x1, waiting for transfers between devices, shards(): lax.psum_scatter(qkv_grad, ('seq', 'fsdp'), scatter_dimension=0, tiled=True)  161 us
    reduce_scatter x1, waiting for transfers between devices, shards(): lax.psum_scatter(out_grad, ('seq', 'fsdp'), scatter_dimension=0, tiled=True)  139 us
    all_gather x1, waiting for transfers between devices, shards(): lax.all_gather(expert_down.astype(jnp.bfloat16), ('seq', 'fsdp'), axis=1,...  100 us
    unnamed x12, waiting for transfers between devices  88.9 us
    all_gather x1, waiting for transfers between devices, shards(): lax.all_gather(expert_in.astype(jnp.bfloat16), ('seq', 'fsdp'), axis=1, t...  61.4 us
  transfers between devices with their start and end apart: 18, of which 12 were waited for; matrix products, arithmetic and copies ran while one was open for 12% of the time, Pallas kernels for 0%

commit v1 on v0

v1 whole, which is shorter than its diff:
```python
import functools
import itertools

import jax
import jax.numpy as jnp
from jax import lax
from jax.experimental import pallas as pl
from jax.experimental.pallas import tpu as pltpu
from jax.sharding import PartitionSpec as P

MODEL_DIMENSION = 1536
QUERY_HEADS = 12
KEY_VALUE_HEADS = 2
HEAD_DIMENSION = 128
F = 768
EXPERTS = 8
TOPK = 4
STEP = 10
CAP = 320


PRECISE = lax.Precision.HIGHEST
NORM_EPS = 1e-06
CLIP_NORM = 1.0
BETA_ONE = 0.9
BETA_TWO = 0.95
ADAM_EPS = 1e-08
DECAY_RATE = 0.1
ROPE_BASE = 10000.0
MASKED_SCORE = -1e30

F32 = jnp.float32
BF16 = jnp.bfloat16
ALL_AXES = ("x", "z", "y", "core")
ROWS = ("z", "y", "core")
SOURCES = 4
OWN_EXPERTS = EXPERTS // SOURCES
Z_STEPS = 4
LANES = 128
MIB = 1024 * 1024


def rms_scale(values):
    return lax.rsqrt(jnp.mean(values * values, axis=-1, keepdims=True) + NORM_EPS)


def step_sizes():
    return (
        MODEL_DIMENSION ** (-0.5),
        (QUERY_HEADS * HEAD_DIMENSION // 64) ** (-0.5),
        (4 * MODEL_DIMENSION) ** (-0.5),
        MODEL_DIMENSION ** (-0.5),
        (F // 64) ** (-0.5),
        0.3,
    )


def adam_step(weight, gradient, moment, second, step_size, decay_value):
    moment_new = BETA_ONE * moment + (1.0 - BETA_ONE) * gradient
    second_new = BETA_TWO * second + (1.0 - BETA_TWO) * gradient * gradient
    corrected = (
        moment_new
        / (1.0 - BETA_ONE**STEP)
        / (jnp.sqrt(second_new / (1.0 - BETA_TWO**STEP)) + ADAM_EPS)
    )
    return (weight - step_size * (corrected + decay_value * weight), moment_new, second_new)


def update_all(weights, gradients, moments, seconds, factor):
    sizes_list = step_sizes()
    decays = (DECAY_RATE, DECAY_RATE, DECAY_RATE, DECAY_RATE, DECAY_RATE, 0.0)
    new_weights = []
    new_moments = []
    new_seconds = []
    for position in range(6):
        weight_new, moment_new, second_new = adam_step(
            weights[position],
            gradients[position] * factor,
            moments[position],
            seconds[position],
            sizes_list[position],
            decays[position],
        )
        new_weights.append(weight_new)
        new_moments.append(moment_new)
        new_seconds.append(second_new)
    return (new_weights, new_moments, new_seconds)


def norm_value_grad(values, norm_scale, gain_row, upstream):
    scaled = gain_row * upstream
    return norm_scale * scaled - values * norm_scale**3 * jnp.mean(
        values * scaled, axis=-1, keepdims=True
    )


def dot_nt(a, b):
    return lax.dot_general(a, b, (((1,), (1,)), ((), ())), preferred_element_type=F32)


def dot_tn(a, b):
    return lax.dot_general(a, b, (((0,), (0,)), ((), ())), preferred_element_type=F32)


def swap(value, axis):
    return lax.ppermute(value, axis, [(0, 1), (1, 0)])


def rotate(value, step):
    size = lax.axis_size("z")
    return lax.ppermute(value, "z", [(i, (i + step) % size) for i in range(size)])


def hold(values, *others):
    count = len(values)
    spec = pl.BlockSpec(memory_space=pl.ANY)
    return pl.pallas_call(
        lambda *refs: None,
        in_specs=[spec] * (count + len(others)),
        out_specs=[spec] * count,
        out_shape=[jax.ShapeDtypeStruct(v.shape, v.dtype) for v in values],
        input_output_aliases={i: i for i in range(count)},
        name="hold",
    )(*values, *others)


def by_index(index, own, other):
    return jnp.where(index == 0, jnp.stack([own, other]), jnp.stack([other, own]))


def take_index(index, array, axis):
    return lax.dynamic_index_in_dim(array, index, axis=axis, keepdims=False)


def total_over(value):
    if lax.axis_size("z") != Z_STEPS:
        return lax.psum(value, ALL_AXES)
    value = jnp.broadcast_to(value, (8, LANES))
    value = value + sum(rotate(value, k) for k in range(1, Z_STEPS))
    for axis in ("x", "y", "core"):
        value = value + swap(value, axis)
    return value[0, 0]


def place():
    return jnp.stack([lax.axis_index(a) for a in ALL_AXES]).astype(jnp.int32)


def block_of(place_ref, rel_x, rel_z, rel_y):
    x = lax.rem(place_ref[0] + rel_x, 2)
    z = lax.rem(place_ref[1] + rel_z, Z_STEPS)
    y = lax.rem(place_ref[2] + rel_y, 2)
    return (x * Z_STEPS + z) * 2 + y


def row_blocks():
    return [
        (c, y, x, z) for c in range(2) for y in range(2) for x in range(2) for z in range(Z_STEPS)
    ]


def row_copies(place_ref, own_ref, other_ref, targets, sems, first):
    rows = own_ref.shape[-2]
    copies = []
    for c, y, x, z in row_blocks():
        core = lax.rem(place_ref[3] + c, 2)
        row = pl.multiple_of((block_of(place_ref, x, z, y) * 2 + core) * rows, rows)
        for start, width, ref, column in targets:
            copies.append(
                pltpu.make_async_copy(
                    (own_ref, other_ref)[c].at[y, x, z, :, pl.ds(start, width)],
                    ref.at[pl.ds(row, rows), pl.ds(column, width)],
                    sems.at[first + len(copies)],
                )
            )
    return copies


def gather_whole(shard):
    whole = lax.all_gather(shard, ALL_AXES, axis=0, tiled=True)
    blocks = whole.reshape(2, Z_STEPS, 2, 2, -1, whole.shape[1])
    blocks = jnp.transpose(blocks, (3, 2, 0, 1, 4, 5))
    return blocks[0], blocks[1]


def scatter_whole(keep, send):
    blocks = jnp.transpose(jnp.stack([keep, send]), (2, 3, 1, 0, 4, 5))
    return lax.psum_scatter(
        blocks.reshape(-1, blocks.shape[-1]), ALL_AXES, scatter_dimension=0, tiled=True
    ).astype(F32)


def grad_rows_kernel(count, has_extra, edges, place_ref, a_ref, *rest):
    rest = list(rest)
    b_refs = [rest.pop(0) for _ in range(count)]
    extra_ref = rest.pop(0) if has_extra else None
    outs = [(rest.pop(0), rest.pop(0)) for _ in edges[1:]]
    held, sems = rest
    rows = outs[0][0].shape[-2]

    @pl.loop(0, a_ref.shape[1] // 256)
    def _(i):
        tile = pl.ds(pl.multiple_of(i * 256, 256), 256)
        start = 0
        for b_ref in b_refs:
            grad = dot_tn(a_ref[:, tile], b_ref[...])
            held[tile, pl.ds(start, b_ref.shape[1])] = grad.astype(BF16)
            start += b_ref.shape[1]

    if has_extra:
        held[:, pl.ds(held.shape[1] - LANES, LANES)] = extra_ref[...].astype(BF16)
    copies = []
    for pair, start, end in zip(outs, edges, edges[1:]):
        for c, y, x, z in row_blocks():
            core = lax.rem(place_ref[3] + c, 2)
            row = pl.multiple_of((block_of(place_ref, x, z, y) * 2 + core) * rows, rows)
            copies.append(
                pltpu.make_async_copy(
                    held.at[pl.ds(row, rows), pl.ds(start, end - start)],
                    pair[c].at[y, x, z],
                    sems.at[len(copies)],
                )
            )
    for copy in copies:
        copy.start()
    for copy in copies:
        copy.wait()


def grad_rows(where, a, bs, extra, edges):
    model_rows = a.shape[1]
    rows = model_rows // (2 * Z_STEPS * 2 * 2)
    width = edges[-1]
    any_spec = pl.BlockSpec(memory_space=pl.ANY)
    vmem_spec = pl.BlockSpec(memory_space=pltpu.VMEM)
    operands = (a, *bs) + (() if extra is None else (extra,))
    parts = len(edges) - 1
    outs = pl.pallas_call(
        functools.partial(grad_rows_kernel, len(bs), extra is not None, edges),
        grid_spec=pltpu.PrefetchScalarGridSpec(
            num_scalar_prefetch=1,
            grid=(1,),
            in_specs=[vmem_spec] * len(operands),
            out_specs=[any_spec] * (2 * parts),
            scratch_shapes=[
                pltpu.VMEM((model_rows, width), BF16),
                pltpu.SemaphoreType.DMA((len(row_blocks()) * parts,)),
            ],
        ),
        out_shape=[
            jax.ShapeDtypeStruct((2, 2, Z_STEPS, rows, end - start), BF16)
            for start, end in zip(edges, edges[1:])
            for _ in range(2)
        ],
        compiler_params=pltpu.CompilerParams(vmem_limit_bytes=48 * MIB),
        cost_estimate=pl.CostEstimate(
            flops=4 * a.shape[0] * model_rows * width,
            bytes_accessed=4 * model_rows * width,
            transcendentals=0,
        ),
        name="grad_rows",
    )(where, *operands)
    return [(outs[2 * i], outs[2 * i + 1]) for i in range(parts)]


def kept_sent(blocks, axis):
    at = 0 if axis == "y" or blocks.ndim == 4 else 1
    return [lax.index_in_dim(blocks, i, axis=at, keepdims=False) for i in range(2)]


def fold(kept, sent, axis):
    return kept.astype(F32) + swap(sent.astype(BF16), axis).astype(F32)


def fold_z(blocks):
    total = blocks[0]
    for k in range(1, Z_STEPS):
        total = total + rotate(blocks[k].astype(BF16), k).astype(F32)
    return total


def rotated(values, cosine, sine):
    return values * cosine + pltpu.roll(values, HEAD_DIMENSION // 2, 1) * sine


def project_kernel(
    place_ref,
    x_ref,
    own,
    other,
    cos_ref,
    sin_ref,
    query_ref,
    kv_ref,
    normed_ref,
    weight_out,
    small_out,
    weight,
    small,
    sems,
    out_sems,
):
    step = pl.program_id(0)
    columns = weight.shape[1]
    keep = [
        pltpu.make_async_copy(weight, weight_out, out_sems.at[0]),
        pltpu.make_async_copy(small, small_out, out_sems.at[1]),
    ]

    @pl.when(step == 0)
    def _():
        copies = row_copies(
            place_ref,
            own,
            other,
            ((0, columns, weight, 0), (columns, LANES, small, 0)),
            sems,
            0,
        )
        for copy in copies:
            copy.start()
        for copy in copies:
            copy.wait()
        for copy in keep:
            copy.start()
        gain = small[...].astype(F32).T[EXPERTS : EXPERTS + 1, :]
        values = x_ref[...].astype(F32)
        normed_ref[...] = (values * rms_scale(values) * gain).astype(BF16)

    tile = KEY_VALUE_HEADS * HEAD_DIMENSION
    at = pl.ds(pl.multiple_of(step * tile, tile), tile)
    mixed = jnp.dot(normed_ref[...], weight[:, at], preferred_element_type=F32)
    query_steps = pl.num_programs(0) - 2

    def turned():
        return jnp.concatenate(
            [
                rotated(
                    mixed[:, h * HEAD_DIMENSION : (h + 1) * HEAD_DIMENSION],
                    cos_ref[...],
                    sin_ref[...],
                ).astype(BF16)
                for h in range(KEY_VALUE_HEADS)
            ],
            axis=1,
        )

    @pl.when(step < query_steps)
    def _():
        query_ref[...] = turned()

    @pl.when(step == query_steps)
    def _():
        kv_ref[...] = turned()

    @pl.when(step == query_steps + 1)
    def _():
        kv_ref[...] = mixed.astype(BF16)
        for copy in keep:
            copy.wait()


def project(where, x, pair, cosine, sine):
    rows, depth = x.shape
    columns = pair[0].shape[-1] - LANES
    tile = KEY_VALUE_HEADS * HEAD_DIMENSION
    query_steps = QUERY_HEADS // KEY_VALUE_HEADS
    whole = lambda i, *_: (0, 0)
    any_spec = pl.BlockSpec(memory_space=pl.ANY)
    turn = pl.BlockSpec((rows, HEAD_DIMENSION), whole)
    return pl.pallas_call(
        project_kernel,
        grid_spec=pltpu.PrefetchScalarGridSpec(
            num_scalar_prefetch=1,
            grid=(query_steps + 2,),
            in_specs=[pl.BlockSpec((rows, depth), whole)] + [any_spec] * 2 + [turn] * 2,
            out_specs=[
                pl.BlockSpec((rows, tile), lambda i, *_: (0, jnp.minimum(i, query_steps - 1))),
                pl.BlockSpec((rows, tile), lambda i, *_: (0, jnp.maximum(i - query_steps, 0))),
                pl.BlockSpec((rows, depth), whole),
                any_spec,
                any_spec,
            ],
            scratch_shapes=[
                pltpu.VMEM((depth, columns), BF16),
                pltpu.VMEM((depth, LANES), BF16),
                pltpu.SemaphoreType.DMA((2 * len(row_blocks()),)),
                pltpu.SemaphoreType.DMA((2,)),
            ],
        ),
        out_shape=[
            jax.ShapeDtypeStruct((rows, query_steps * tile), BF16),
            jax.ShapeDtypeStruct((rows, 2 * tile), BF16),
            jax.ShapeDtypeStruct((rows, depth), BF16),
            jax.ShapeDtypeStruct((depth, columns), BF16),
            jax.ShapeDtypeStruct((depth, LANES), BF16),
        ],
        compiler_params=pltpu.CompilerParams(vmem_limit_bytes=40 * MIB),
        cost_estimate=pl.CostEstimate(
            flops=6 * rows * depth * columns, bytes_accessed=20 * MIB, transcendentals=0
        ),
        name="project",
    )(where, x, *pair, cosine, sine)


def join_kernel(
    place_ref,
    attended_ref,
    x_ref,
    gain_ref,
    own,
    other,
    middle_ref,
    normed_ref,
    scale_ref,
    weight_out,
    weight,
    sems,
    out_sems,
):
    copies = row_copies(place_ref, own, other, ((0, weight.shape[1], weight, 0),), sems, 0)
    for copy in copies:
        copy.start()
    for copy in copies:
        copy.wait()
    keep = pltpu.make_async_copy(weight, weight_out, out_sems.at[0])
    keep.start()
    wide = 512
    width = weight.shape[1]

    def join(i, total):
        at = pl.ds(pl.multiple_of(i * wide, wide), wide)
        middle = x_ref[:, at].astype(F32) + jnp.dot(
            attended_ref[...], weight[:, at], preferred_element_type=F32
        )
        middle_ref[:, at] = middle
        return total + jnp.sum(middle * middle, axis=1, keepdims=True)

    total = lax.fori_loop(0, width // wide, join, jnp.zeros((x_ref.shape[0], 1), F32))
    scale = lax.rsqrt(total / width + NORM_EPS)
    scale_ref[...] = scale
    normed_ref[...] = (middle_ref[...] * scale * gain_ref[...]).astype(BF16)
    keep.wait()


def join(where, attended, x, gain, pair):
    rows, depth = attended.shape
    width = pair[0].shape[-1]
    any_spec = pl.BlockSpec(memory_space=pl.ANY)
    vmem_spec = pl.BlockSpec(memory_space=pltpu.VMEM)
    return pl.pallas_call(
        join_kernel,
        grid_spec=pltpu.PrefetchScalarGridSpec(
            num_scalar_prefetch=1,
            grid=(1,),
            in_specs=[vmem_spec] * 3 + [any_spec] * 2,
            out_specs=[vmem_spec] * 3 + [any_spec],
            scratch_shapes=[
                pltpu.VMEM((depth, width), BF16),
                pltpu.SemaphoreType.DMA((len(row_blocks()),)),
                pltpu.SemaphoreType.DMA((1,)),
            ],
        ),
        out_shape=[
            jax.ShapeDtypeStruct((rows, width), F32),
            jax.ShapeDtypeStruct((rows, width), BF16),
            jax.ShapeDtypeStruct((rows, 1), F32),
            jax.ShapeDtypeStruct((depth, width), BF16),
        ],
        compiler_params=pltpu.CompilerParams(vmem_limit_bytes=40 * MIB),
        cost_estimate=pl.CostEstimate(
            flops=4 * rows * depth * width, bytes_accessed=16 * MIB, transcendentals=0
        ),
        name="join",
    )(where, attended, x, gain, *pair)


def score_pair(q, ko_ref, kp_ref, seg_col, seg_own, seg_prev):
    scale = HEAD_DIMENSION ** (-0.5)
    own = dot_nt(q, ko_ref[...]) * scale
    query_at = lax.broadcasted_iota(jnp.int32, own.shape, 0)
    key_at = lax.broadcasted_iota(jnp.int32, own.shape, 1)
    own = jnp.where((seg_col == seg_own) & (key_at <= query_at), own, MASKED_SCORE)
    if kp_ref is None:
        return (own,)
    prev = dot_nt(q, kp_ref[...]) * scale
    return (own, jnp.where(seg_col == seg_prev, prev, MASKED_SCORE))


def attend_kernel(
    half_ref, q_ref, ko_ref, vo_ref, kp_ref, vp_ref, sc_ref, so_ref, sp_ref, out_ref, log_ref
):
    def run(with_previous):
        parts = score_pair(
            q_ref[...],
            ko_ref,
            kp_ref if with_previous else None,
            sc_ref[...],
            so_ref[...],
            sp_ref[...],
        )
        highest = jnp.max(parts[0], axis=-1, keepdims=True)
        for part in parts[1:]:
            highest = jnp.maximum(highest, jnp.max(part, axis=-1, keepdims=True))
        exponents = [jnp.exp(part - highest) for part in parts]
        total = sum(jnp.sum(part, axis=-1, keepdims=True) for part in exponents)
        scale = 1.0 / total
        mixed = sum(
            jnp.dot((part * scale).astype(BF16), ref[...], preferred_element_type=F32)
            for part, ref in zip(exponents, (vo_ref, vp_ref))
        )
        out_ref[...] = mixed.astype(BF16)
        log_ref[0] = highest + jnp.log(total)

    pl.when(half_ref[0] == 0)(lambda: run(False))
    pl.when(half_ref[0] != 0)(lambda: run(True))


def head_specs(rows):
    group = QUERY_HEADS // KEY_VALUE_HEADS
    query = pl.BlockSpec((rows, HEAD_DIMENSION), lambda h, *_: (0, h))
    key = pl.BlockSpec((rows, HEAD_DIMENSION), lambda h, *_: (0, h // group))
    value = pl.BlockSpec((rows, HEAD_DIMENSION), lambda h, *_: (0, KEY_VALUE_HEADS + h // group))
    col = pl.BlockSpec((rows, 1), lambda h, *_: (0, 0))
    row = pl.BlockSpec((1, rows), lambda h, *_: (0, 0))
    log = pl.BlockSpec((1, rows, 1), lambda h, *_: (h, 0, 0))
    return query, [query, key, value, key, value, col, row, row], log


def attend(queries, own, previous, seg_col, seg_own, seg_prev, half):
    rows = queries.shape[0]
    query, specs, log = head_specs(rows)
    return pl.pallas_call(
        attend_kernel,
        grid_spec=pltpu.PrefetchScalarGridSpec(
            num_scalar_prefetch=1,
            grid=(QUERY_HEADS,),
            in_specs=specs,
            out_specs=[query, log],
        ),
        out_shape=[
            jax.ShapeDtypeStruct((rows, QUERY_HEADS * HEAD_DIMENSION), BF16),
            jax.ShapeDtypeStruct((QUERY_HEADS, rows, 1), F32),
        ],
        compiler_params=pltpu.CompilerParams(vmem_limit_bytes=40 * MIB),
        cost_estimate=pl.CostEstimate(
            flops=8 * rows * rows * QUERY_HEADS * HEAD_DIMENSION,
            bytes_accessed=16 * MIB,
            transcendentals=2 * rows * rows * QUERY_HEADS,
        ),
        name="attend",
    )(half, queries, own, own, previous, previous, seg_col, seg_own, seg_prev)


def attend_back_kernel(
    half_ref,
    q_ref,
    ko_ref,
    vo_ref,
    kp_ref,
    vp_ref,
    sc_ref,
    so_ref,
    sp_ref,
    up_ref,
    log_ref,
    cos_ref,
    sin_ref,
    dq_ref,
    dko_ref,
    dvo_ref,
    dkp_ref,
    dvp_ref,
):
    scale = HEAD_DIMENSION ** (-0.5)
    first = lax.rem(pl.program_id(0), QUERY_HEADS // KEY_VALUE_HEADS) == 0

    @pl.when(first)
    def _():
        for ref in (dko_ref, dvo_ref, dkp_ref, dvp_ref):
            ref[...] = jnp.zeros_like(ref)

    def run(with_previous):
        q, up = q_ref[...], up_ref[...]
        parts = score_pair(
            q, ko_ref, kp_ref if with_previous else None, sc_ref[...], so_ref[...], sp_ref[...]
        )
        weights = [jnp.exp(part - log_ref[0]) for part in parts]
        grads = [dot_nt(up, ref[...]) for ref, _ in zip((vo_ref, vp_ref), parts)]
        inner = sum(
            jnp.sum(w * g, axis=-1, keepdims=True) for w, g in zip(weights, grads)
        )
        scores = [(w * (g - inner)).astype(BF16) for w, g in zip(weights, grads)]
        dq = sum(
            jnp.dot(s, ref[...], preferred_element_type=F32)
            for s, ref in zip(scores, (ko_ref, kp_ref))
        )
        dq = (dq * scale).astype(BF16).astype(F32)
        dq_ref[...] = rotated(dq, cos_ref[...], sin_ref[...]).astype(BF16)
        for s, w, dk_ref, dv_ref in zip(scores, weights, (dko_ref, dkp_ref), (dvo_ref, dvp_ref)):
            dk_ref[...] += dot_tn(s, q) * scale
            dv_ref[...] += dot_tn(w.astype(BF16), up)

    pl.when(half_ref[0] == 0)(lambda: run(False))
    pl.when(half_ref[0] != 0)(lambda: run(True))


def attend_back(queries, own, previous, seg_col, seg_own, seg_prev, half, up, log_sums, cosine, sine):
    rows = queries.shape[0]
    query, specs, log = head_specs(rows)
    group = QUERY_HEADS // KEY_VALUE_HEADS
    turn = pl.BlockSpec((rows, HEAD_DIMENSION), lambda h, *_: (0, 0))
    kv = pl.BlockSpec((rows, HEAD_DIMENSION), lambda h, *_: (0, h // group))
    kv_shape = jax.ShapeDtypeStruct((rows, KEY_VALUE_HEADS * HEAD_DIMENSION), F32)
    return pl.pallas_call(
        attend_back_kernel,
        grid_spec=pltpu.PrefetchScalarGridSpec(
            num_scalar_prefetch=1,
            grid=(QUERY_HEADS,),
            in_specs=specs + [query, log, turn, turn],
            out_specs=[query, kv, kv, kv, kv],
        ),
        out_shape=[jax.ShapeDtypeStruct((rows, QUERY_HEADS * HEAD_DIMENSION), BF16)]
        + [kv_shape] * 4,
        compiler_params=pltpu.CompilerParams(vmem_limit_bytes=48 * MIB),
        cost_estimate=pl.CostEstimate(
            flops=20 * rows * rows * QUERY_HEADS * HEAD_DIMENSION,
            bytes_accessed=24 * MIB,
            transcendentals=2 * rows * rows * QUERY_HEADS,
        ),
        name="attend_back",
    )(
        half,
        queries,
        own,
        own,
        previous,
        previous,
        seg_col,
        seg_own,
        seg_prev,
        up,
        log_sums,
        cosine,
        sine,
    )


def expert_kernel(has_before, place_ref, *refs):
    refs = list(refs)
    pieces = [refs.pop(0) for _ in range(2)]
    x_refs, t_refs = ([refs.pop(0) for _ in range(SOURCES)] for _ in range(2))
    rank_row_ref, rank_col_ref, router_ref = (refs.pop(0) for _ in range(3))
    before = [refs.pop(0) for _ in range(4)] if has_before else None
    mix_keep, mix_send, ffn_keep, ffn_send, gate_grad_ref = (refs.pop(0) for _ in range(5))
    grads = [refs.pop(0) for _ in range(2)]
    (
        in_w,
        down_w,
        picked,
        joined_grad,
        active,
        slot_grad,
        top,
        x_held,
        t_held,
        in_g,
        down_g,
        sems,
        token_sems,
    ) = refs
    source = pl.program_id(0)
    slot = lax.rem(source, 2)

    def token_copies(s):
        return [
            pltpu.make_async_copy(many[s], held.at[s % 2], token_sems.at[i, s % 2])
            for i, (many, held) in enumerate(((x_refs, x_held), (t_refs, t_held)))
        ]
    in_rows = in_w.shape[0] // (4 * Z_STEPS)
    down_rows = down_w.shape[0] // (4 * Z_STEPS)

    def block_copies(outward):
        copies = []
        for y, piece in enumerate(grads if outward else pieces):
            for z, x in itertools.product(range(Z_STEPS), range(2)):
                block = (x * Z_STEPS + z) * 2 + lax.rem(place_ref[2] + y, 2)
                for whole, rows, start in (
                    (in_g if outward else in_w, in_rows, 0),
                    (down_g if outward else down_w, down_rows, in_rows),
                ):
                    ends = (
                        piece.at[z, x, pl.ds(start, rows), :],
                        whole.at[pl.ds(pl.multiple_of(block * rows, rows), rows), :],
                    )
                    if outward:
                        ends = ends[::-1]
                    copies.append(pltpu.make_async_copy(*ends, sems.at[len(copies)]))
        return copies

    @pl.when(source == 0)
    def _():
        copies = token_copies(0) + block_copies(False)
        for copy in copies:
            copy.start()
        for copy in copies[2:]:
            copy.wait()

    for s in range(SOURCES):

        @pl.when(source == s)
        def _(s=s):
            for copy in token_copies(s):
                copy.wait()
            if s + 1 < SOURCES:
                for copy in token_copies(s + 1):
                    copy.start()

    slots = pl.ds(pl.multiple_of(source * CAP, CAP), CAP)
    tokens, width = x_refs[0].shape
    rank_row = rank_row_ref[0]
    expert_row = lax.broadcasted_iota(jnp.int32, (router_ref.shape[0], tokens), 0)
    logits = jnp.where(expert_row < EXPERTS, dot_nt(router_ref[...], x_held[slot]), MASKED_SCORE)
    exponent = jnp.exp(logits - jnp.max(logits, axis=0, keepdims=True))
    probs = exponent / jnp.sum(exponent, axis=0, keepdims=True)
    gate_row = jnp.sum(jnp.where(expert_row == place_ref[4], probs, 0.0), axis=0, keepdims=True)
    chosen = (
        lax.broadcasted_iota(jnp.int32, (CAP, tokens), 0) == rank_row
    ).astype(F32)
    gate = jnp.sum(chosen * gate_row, axis=1, keepdims=True)
    spread = (
        lax.broadcasted_iota(jnp.int32, (tokens, CAP), 1) == rank_col_ref[0]
    ).astype(F32).astype(BF16)
    pick = chosen.astype(BF16)
    wide = 512

    @pl.loop(0, width // wide, unroll=True)
    def _(i):
        at = pl.ds(pl.multiple_of(i * wide, wide), wide)
        picked[slots, at] = jnp.dot(
            pick, x_held[slot, :, at], preferred_element_type=F32
        ).astype(BF16)
        top_rows = jnp.dot(pick, t_held[slot, :, at], preferred_element_type=F32)
        top[:, at] = top_rows
        slot_grad[slots, at] = (gate * top_rows).astype(BF16)

    hidden = active.shape[1]
    narrow = 256

    @pl.loop(0, hidden // narrow, unroll=True)
    def _(i):
        at = pl.ds(pl.multiple_of(i * narrow, narrow), narrow)
        up_at = pl.ds(pl.multiple_of(hidden + i * narrow, narrow), narrow)
        rows = picked[slots, :]
        gate_part = jnp.dot(rows, in_w[:, at], preferred_element_type=F32)
        up_part = jnp.dot(rows, in_w[:, up_at], preferred_element_type=F32)
        act_grad = dot_nt(slot_grad[slots, :], down_w[at, :])
        sigmoid = jax.nn.sigmoid(gate_part)
        silu = gate_part * sigmoid
        active[slots, at] = (silu * up_part).astype(BF16)
        joined_grad[slots, at] = (
            act_grad * up_part * sigmoid * (1.0 + gate_part * (1.0 - sigmoid))
        ).astype(BF16)
        joined_grad[slots, up_at] = (act_grad * silu).astype(BF16)

    def results(i, total):
        at = pl.ds(pl.multiple_of(i * wide, wide), wide)
        result = jnp.dot(active[slots, :], down_w[:, at], preferred_element_type=F32)
        mix = jnp.dot(spread, (gate * result).astype(BF16), preferred_element_type=F32)
        back = dot_nt(joined_grad[slots, :], in_w[at, :])
        ffn = jnp.dot(spread, back.astype(BF16), preferred_element_type=F32)

        def put(mix_ref, ffn_ref, mix_before, ffn_before):
            if before is None:
                mix_ref[0, :, at] = mix.astype(BF16)
                ffn_ref[0, :, at] = ffn.astype(BF16)
            else:
                mix_ref[0, :, at] = (mix + mix_before[0, :, at].astype(F32)).astype(BF16)
                ffn_ref[0, :, at] = (ffn + ffn_before[0, :, at].astype(F32)).astype(BF16)

        earlier = before or [None] * 4
        pl.when(source < 2)(lambda: put(mix_keep, ffn_keep, earlier[0], earlier[2]))
        pl.when(source >= 2)(lambda: put(mix_send, ffn_send, earlier[1], earlier[3]))
        return total + jnp.sum(result * top[:, at], axis=1, keepdims=True)

    gate_grad = lax.fori_loop(
        0, width // wide, results, jnp.zeros((CAP, 1), F32), unroll=True
    )
    gate_grad_ref[0] = jnp.sum(chosen * gate_grad, axis=0, keepdims=True)

    @pl.when(source == SOURCES - 1)
    def _():
        @pl.loop(0, in_g.shape[0] // 256)
        def _(i):
            at = pl.ds(pl.multiple_of(i * 256, 256), 256)
            in_g[at, :] = dot_tn(picked[:, at], joined_grad[...]).astype(BF16)

        @pl.loop(0, down_g.shape[0] // 256)
        def _(i):
            at = pl.ds(pl.multiple_of(i * 256, 256), 256)
            down_g[at, :] = dot_tn(active[:, at], slot_grad[...]).astype(BF16)

        copies = block_copies(True)
        for copy in copies:
            copy.start()
        for copy in copies:
            copy.wait()


def expert_pass(where, pieces, x_all, t_all, rank_row, rank_col, router_rows, before):
    tokens, width = x_all[0].shape
    hidden = F
    any_spec = pl.BlockSpec(memory_space=pl.ANY)
    keep_at = lambda s, *_: (jnp.minimum(s, 1), 0, 0)
    send_at = lambda s, *_: (jnp.maximum(s - 2, 0), 0, 0)
    sum_specs = [pl.BlockSpec((1, tokens, width), at) for at in (keep_at, send_at)] * 2
    before_specs = [
        pl.BlockSpec((1, tokens, width), at, pipeline_mode=pl.Buffered(1))
        for at in (keep_at, send_at)
    ] * 2
    row_spec = pl.BlockSpec((1, 1, tokens), lambda s, *_: (s, 0, 0))
    col_spec = pl.BlockSpec((1, tokens, 1), lambda s, *_: (s, 0, 0))
    router_spec = pl.BlockSpec(router_rows.shape, lambda s, *_: (0, 0))
    piece_shape = jax.ShapeDtypeStruct(pieces[0].shape, BF16)
    sum_shape = jax.ShapeDtypeStruct((2, tokens, width), BF16)
    slots = SOURCES * CAP
    flops = 2 * slots * width * hidden * 9 + 8 * slots * tokens * width
    outs = pl.pallas_call(
        functools.partial(expert_kernel, before is not None),
        grid_spec=pltpu.PrefetchScalarGridSpec(
            num_scalar_prefetch=1,
            grid=(SOURCES,),
            in_specs=[any_spec] * (len(pieces) + 2 * SOURCES)
            + [row_spec, col_spec, router_spec]
            + ([] if before is None else before_specs),
            out_specs=sum_specs + [row_spec] + [any_spec] * len(pieces),
            scratch_shapes=[
                pltpu.VMEM((width, 2 * hidden), BF16),
                pltpu.VMEM((hidden, width), BF16),
                pltpu.VMEM((slots, width), BF16),
                pltpu.VMEM((slots, 2 * hidden), BF16),
                pltpu.VMEM((slots, hidden), BF16),
                pltpu.VMEM((slots, width), BF16),
                pltpu.VMEM((CAP, width), F32),
                pltpu.VMEM((2, tokens, width), BF16),
                pltpu.VMEM((2, tokens, width), BF16),
                pltpu.VMEM((width, 2 * hidden), BF16),
                pltpu.VMEM((hidden, width), BF16),
                pltpu.SemaphoreType.DMA((8 * Z_STEPS,)),
                pltpu.SemaphoreType.DMA((2, 2)),
            ],
        ),
        out_shape=[sum_shape] * 4
        + [jax.ShapeDtypeStruct((SOURCES, 1, tokens), F32)]
        + [piece_shape] * len(pieces),
        compiler_params=pltpu.CompilerParams(vmem_limit_bytes=60 * MIB),
        cost_estimate=pl.CostEstimate(
            flops=2 * flops, bytes_accessed=48 * MIB, transcendentals=slots * hidden
        ),
        name="expert",
    )(where, *pieces, *x_all, *t_all, rank_row, rank_col, router_rows, *(before or ()))
    return outs[:4], outs[4], outs[5:]


def expert_pairs(expert_in, expert_down):
    core = lax.axis_index("core")
    low = jnp.concatenate([expert_in.astype(BF16), expert_down.astype(BF16)], axis=1)
    low = low.reshape(2, 2, OWN_EXPERTS, *low.shape[1:])
    return by_index(core, take_index(core, low, 1), swap(take_index(1 - core, low, 1), "core"))


def expert_chunk(pair, number, in_rows):
    x = lax.axis_index("x")
    pair = pair[:, :, number]
    in_part = pair[:, :, :in_rows]
    down_part = pair[:, :, in_rows:]
    width = pair.shape[-1]
    both = jnp.concatenate(
        [
            jnp.swapaxes(in_part, 0, 1).reshape(2, -1, width),
            jnp.swapaxes(down_part, 0, 1).reshape(2, -1, width),
        ],
        axis=1,
    )
    return by_index(x, take_index(x, both, 0), swap(take_index(1 - x, both, 0), "x"))


def gather_expert(chunk):
    if lax.axis_size("z") == Z_STEPS:
        whole = lax.all_gather(chunk, "z")
        return whole, swap(whole, "y")
    whole = lax.all_gather(chunk, ("z", "y"))
    rows = chunk.shape[1] * 2 // 3
    width = chunk.shape[2]
    parts = [
        jnp.moveaxis(part, 0, 1).reshape(2, Z_STEPS, 2, -1, width)
        for part in (whole[:, :, :rows], whole[:, :, rows:])
    ]
    both = jnp.transpose(jnp.concatenate(parts, axis=3), (2, 1, 0, 3, 4))
    return both[0], both[1]


def scatter_expert_whole(kept, arrived):
    spots = lax.axis_size("z") * 2
    both = jnp.transpose(jnp.stack([kept, arrived]), (2, 1, 0, 3, 4))
    width = both.shape[-1]
    in_rows = both.shape[3] * 2 // 3
    parts = [
        part.reshape(2, spots, -1, width)
        for part in (both[:, :, :, :in_rows], both[:, :, :, in_rows:])
    ]
    both = jnp.moveaxis(jnp.concatenate(parts, axis=2), 1, 0)
    return lax.psum_scatter(both, ("z", "y"), scatter_dimension=0).astype(F32)


def cross_chunk(chunk):
    x = lax.axis_index("x")
    return take_index(x, chunk, 0), swap(take_index(1 - x, chunk, 0).astype(BF16), "x")


def scatter_chunks(pairs, in_rows, down_rows):
    x, core = lax.axis_index("x"), lax.axis_index("core")
    width = pairs[0][0].shape[-1]
    own, crossed = (jnp.stack([p[i].astype(F32) for p in pairs]) for i in range(2))
    both = by_index(x, own, crossed)
    split = jnp.concatenate(
        [
            both[:, :, : 2 * in_rows].reshape(2, OWN_EXPERTS, 2, in_rows, width),
            both[:, :, 2 * in_rows :].reshape(2, OWN_EXPERTS, 2, down_rows, width),
        ],
        axis=3,
    )
    other = swap(take_index(1 - core, split, 2).astype(BF16), "core").astype(F32)
    both = by_index(core, take_index(core, split, 2), other)
    both = jnp.swapaxes(both, 0, 1).reshape(EXPERTS, in_rows + down_rows, width)
    return both[:, :in_rows], both[:, in_rows:]


def shards(
    tokens,
    cotangent,
    segment_ids,
    route_ids,
    query_key_value_weight,
    out_weight,
    router_weight,
    expert_in,
    expert_down,
    norm_gains,
    query_key_value_moment,
    out_moment,
    router_moment,
    in_moment,
    down_moment,
    gains_moment,
    query_key_value_second,
    out_second,
    router_second,
    in_second,
    down_second,
    gains_second,
):
    local_rows = tokens.shape[1]
    model_width = tokens.shape[2]
    staged = lax.axis_size("z") == Z_STEPS
    x_index = lax.axis_index("x")
    shard_rows = query_key_value_weight.shape[0]
    in_rows, down_rows = expert_in.shape[1], expert_down.shape[1]
    key_width = KEY_VALUE_HEADS * HEAD_DIMENSION
    first_expert = (x_index * 2 + lax.axis_index("core")) * OWN_EXPERTS
    where = place() if staged else jnp.zeros((4,), jnp.int32)
    x_tokens, top = tokens[0], cotangent[0]

    own_gains = norm_gains.astype(BF16)
    small_part = jnp.concatenate(
        [
            router_weight.astype(BF16),
            own_gains,
            jnp.zeros((shard_rows, LANES - EXPERTS - 2), BF16),
        ],
        axis=1,
    )
    qkv_own = query_key_value_weight.astype(BF16)
    qkv_width = qkv_own.shape[1]
    half_width = qkv_width // 2
    attention_own = jnp.concatenate([qkv_own, small_part, out_weight.astype(BF16)], axis=1)
    attention_edges = (0, half_width, qkv_width + LANES, attention_own.shape[1])

    segments = segment_ids[0]
    seg_prev = swap(segments, "x")
    routes = route_ids[0].T
    routes_x = swap(routes, "x")
    routes_core = swap(jnp.stack([routes, routes_x]), "core")
    routes_all = jnp.stack([routes, routes_x, routes_core[0], routes_core[1]])
    top_x = swap(top, "x")

    pair = expert_pairs(expert_in, expert_down)
    if staged:
        attention_z = [rotate(attention_own, -k) for k in range(1, Z_STEPS)]
        first_held, second_held, out_held = (
            jnp.stack([part[:, start:end] for part in (attention_own, *attention_z)])
            for start, end in zip(attention_edges, attention_edges[1:])
        )
        first_x = swap(first_held, "x")
        second_y = swap(second_held, "y")
        chunk_one = expert_chunk(pair, 0, in_rows)
        pieces_one = gather_expert(chunk_one)
        first_held = jnp.stack([first_held, first_x])
        second_held = jnp.stack([second_held, second_y])
        first_y = swap(first_held, "y")
        second_x = swap(second_held, "x")
        first_held = jnp.stack([first_held, first_y])
        second_held = jnp.stack([second_held, second_x], axis=1)
        qkv_held = jnp.concatenate([first_held, second_held], axis=-1)
        (out_held,) = hold((out_held,), first_y, second_x)
        out_x = swap(out_held, "x")
        qkv_core = swap(qkv_held, "core")
        qkv_pair = (qkv_held, qkv_core)
        out_held = jnp.stack([out_held, out_x])
    else:
        qkv_pair, out_pair = (
            gather_whole(part)
            for part in (
                attention_own[:, : qkv_width + LANES],
                attention_own[:, qkv_width + LANES :],
            )
        )
        pieces_one, pieces_two = (
            gather_expert(expert_chunk(pair, i, in_rows)) for i in range(2)
        )

    half_size = HEAD_DIMENSION // 2
    positions = (x_index * local_rows + jnp.arange(local_rows, dtype=jnp.int32)).astype(F32)
    frequency = ROPE_BASE ** (-2.0 * jnp.arange(half_size, dtype=F32) / HEAD_DIMENSION)
    angles = positions[:, None] * frequency[None, :]
    cosine, sine = jnp.cos(angles), jnp.sin(angles)
    cosine = jnp.concatenate([cosine, cosine], axis=1)
    sine_forward = jnp.concatenate([-sine, sine], axis=1)
    half = x_index.astype(jnp.int32).reshape(1)

    experts_here = first_expert + jnp.arange(OWN_EXPERTS, dtype=jnp.int32)
    member = jnp.any(routes_all[None] == experts_here[:, None, None, None], axis=2)
    earlier = (
        lax.broadcasted_iota(jnp.int32, (local_rows, local_rows), 0)
        < lax.broadcasted_iota(jnp.int32, (local_rows, local_rows), 1)
    ).astype(BF16)
    rank = jnp.dot(
        member.astype(BF16).reshape(-1, local_rows), earlier, preferred_element_type=F32
    ).reshape(member.shape)
    rank = jnp.where(member, rank.astype(jnp.int32), -1)

    queries, kv_own, normed, qkv_low, small_low = project(
        where, x_tokens, qkv_pair, cosine, sine_forward
    )
    kv_prev = swap(kv_own, "x")
    attn_gain = small_low[:, EXPERTS].astype(F32)
    ffn_gain = small_low[:, EXPERTS + 1].astype(F32)
    router_rows = small_low.T[:16]
    if staged:
        out_y = swap(out_held, "y")
        out_held = jnp.stack([out_held, out_y])
        (pair,) = hold((pair,), kv_prev)
        pieces_two = gather_expert(expert_chunk(pair, 1, in_rows))
        out_core = swap(out_held, "core")
        out_pair = (out_held, out_core)
    segs = (segments[:, None], segments[None, :], seg_prev[None, :])
    attended, log_sums = attend(queries, kv_own, kv_prev, *segs, half)
    top_both = swap(jnp.stack([top, top_x]), "core")
    middle, normed_ffn, second_scale, out_low = join(
        where, attended, x_tokens, ffn_gain[None, :], out_pair
    )

    ffn_core = swap(normed_ffn, "core")
    ffn_x = swap(normed_ffn, "x")
    ffn_both = swap(ffn_x, "core")
    x_all = (normed_ffn, ffn_x, ffn_core, ffn_both)
    t_all = (top, top_x, top_both[0], top_both[1])
    places = [jnp.concatenate([where, first_expert[None] + i]) for i in range(OWN_EXPERTS)]

    def expert(i, pieces, before):
        ranks = (rank[i][:, None, :], rank[i][:, :, None])
        return expert_pass(places[i], pieces, x_all, t_all, *ranks, router_rows, before)

    before, gates_one, grads_one = expert(0, pieces_one, None)
    sums, gates_two, grads_two = expert(1, pieces_two, before)
    mix_keep, mix_send, ffn_keep, ffn_send = sums

    if staged:
        back_one = swap(grads_one[1], "y")
        (ffn_send,) = hold((ffn_send,), back_one)
        total_one = (grads_one[0].astype(F32) + back_one.astype(F32)).astype(BF16)
        chunk_sum_one = lax.psum_scatter(total_one, "z", scatter_dimension=0)
        back_two = swap(grads_two[1], "y")
    else:
        chunk_sum_one, chunk_sum_two = (
            scatter_expert_whole(*grads) for grads in (grads_one, grads_two)
        )
    gate_grad = jnp.concatenate([gates_one, gates_two], axis=1)
    spread = lax.dynamic_update_slice_in_dim(
        jnp.zeros((SOURCES, EXPERTS, local_rows), F32), gate_grad, first_expert, axis=1
    )
    spread_core = swap(spread[2:], "core")
    ffn_other = swap(ffn_send, "core").astype(F32)
    spread_x = swap(spread[1] + spread_core[1], "x")
    prob_grad = (spread[0] + spread_core[0] + spread_x).T
    ffn_crossed = swap((ffn_keep[1].astype(F32) + ffn_other[1]).astype(BF16), "x")
    if staged:
        (ffn_crossed,) = hold((ffn_crossed,), total_one)
    (mix_send,) = hold((mix_send,), ffn_crossed)
    mix_other = swap(mix_send, "core").astype(F32)
    mix_crossed = swap((mix_keep[1].astype(F32) + mix_other[1]).astype(BF16), "x")
    ffn_grad = ffn_keep[0].astype(F32) + ffn_other[0] + ffn_crossed.astype(F32)

    logits = jnp.dot(normed_ffn, small_low[:, :EXPERTS], preferred_element_type=F32)
    exponent = jnp.exp(logits - jnp.max(logits, axis=-1, keepdims=True))
    router_probs = exponent / jnp.sum(exponent, axis=-1, keepdims=True)
    logit_grad = router_probs * (
        prob_grad - jnp.sum(router_probs * prob_grad, axis=-1, keepdims=True)
    )
    router_grad = jnp.dot(normed_ffn.astype(F32).T, logit_grad, precision=PRECISE)
    ffn_grad = ffn_grad + jnp.dot(
        logit_grad, small_low[:, :EXPERTS].astype(F32).T, precision=PRECISE
    )
    ffn_gain_grad = jnp.sum(middle * second_scale * ffn_grad, axis=0)
    middle_grad = top.astype(F32) + norm_value_grad(middle, second_scale, ffn_gain, ffn_grad)
    branch_grad = middle_grad.astype(BF16)
    attended_grad = dot_nt(branch_grad, out_low).astype(BF16)
    small_grad = jnp.concatenate(
        [
            router_grad,
            ffn_gain_grad[:, None],
            jnp.zeros((model_width, LANES - EXPERTS - 1), F32),
        ],
        axis=1,
    )
    (out_blocks,) = grad_rows(
        where, attended, (branch_grad,), small_grad, (0, model_width + LANES)
    )
    if staged:
        attended_grad, chunk_sum_one = hold(
            (attended_grad, chunk_sum_one), out_blocks[1], back_two
        )
        total_two = (grads_two[0].astype(F32) + back_two.astype(F32)).astype(BF16)
        out_sum = fold(*out_blocks, "core")
        out_sent = swap(kept_sent(out_sum, "x")[1].astype(BF16), "x")
    query_grad, key_own, value_own, key_prev, value_prev = attend_back(
        queries, kv_own, kv_prev, *segs, half, attended_grad, log_sums, cosine, -sine_forward
    )
    crossed = swap(jnp.concatenate([key_prev, value_prev], axis=1).astype(BF16), "x").astype(F32)
    if staged:
        out_sent, query_grad = hold((out_sent, query_grad), total_two)
        chunk_sum_two = lax.psum_scatter(total_two, "z", scatter_dimension=0)
        out_sum = kept_sent(out_sum, "x")[0] + out_sent.astype(F32)
        out_sum = fold(*kept_sent(out_sum, "y"), "y")
    key_grad = (key_own + crossed[:, :key_width]).astype(BF16).astype(F32)
    value_grad = value_own + crossed[:, key_width:]
    key_grad = key_grad.reshape(local_rows, KEY_VALUE_HEADS, HEAD_DIMENSION)
    key_grad = key_grad * cosine[:, None, :] - jnp.roll(key_grad, half_size, axis=2) * sine_forward[
        :, None, :
    ]
    kv_grad = jnp.concatenate(
        [key_grad.reshape(local_rows, key_width).astype(BF16), value_grad.astype(BF16)], axis=1
    )
    kv_grad, chunk_sum_one = hold((kv_grad, chunk_sum_one), mix_crossed)
    qkv_blocks = grad_rows(
        where, normed, (query_grad, kv_grad), None, (0, half_width, 2 * half_width)
    )
    out_rows = fold_z(out_sum) if staged else scatter_whole(*out_blocks)
    if staged:
        pair_one = cross_chunk(chunk_sum_one)
        first = fold(*qkv_blocks[0], "core")
        second = fold(*qkv_blocks[1], "core")
        first_kept, first_sent = kept_sent(first, "y")
        second_kept, second_sent = kept_sent(second, "x")
        first_come = swap(first_sent.astype(BF16), "y")
        second_come = swap(second_sent.astype(BF16), "x")
        (chunk_sum_two,) = hold((chunk_sum_two,), first_come, second_come)
        first = fold(*kept_sent(first_kept + first_come.astype(F32), "x"), "x")
        second = fold(*kept_sent(second_kept + second_come.astype(F32), "y"), "y")
        qkv_sum = jnp.concatenate([fold_z(first), fold_z(second)], axis=1)
    else:
        pair_one = cross_chunk(chunk_sum_one)
        qkv_sum = jnp.concatenate([scatter_whole(*blocks) for blocks in qkv_blocks], axis=1)
    in_sum, down_sum = scatter_chunks(
        [pair_one, cross_chunk(chunk_sum_two)], in_rows, down_rows
    )
    mixture = mix_keep[0].astype(F32) + mix_other[0] + mix_crossed.astype(F32)
    output = (middle + mixture).astype(BF16)
    mixed_grad = jnp.concatenate([query_grad, kv_grad], axis=1)
    inputs = x_tokens.astype(F32)
    input_grad = middle_grad + norm_value_grad(
        inputs, rms_scale(inputs), attn_gain, dot_nt(mixed_grad, qkv_low)
    )

    out_sum = out_rows[:, :model_width]
    router_sum = out_rows[:, model_width : model_width + EXPERTS]
    attn_gain_sum = jnp.sum(qkv_sum * qkv_own.astype(F32), axis=1) / own_gains[:, 0].astype(F32)
    gains_sum = jnp.stack([attn_gain_sum, out_rows[:, model_width + EXPERTS]], axis=1)

    square_total = (
        jnp.sum(qkv_sum * qkv_sum)
        + jnp.sum(out_sum * out_sum)
        + jnp.sum(router_sum * router_sum)
        + jnp.sum(in_sum * in_sum)
        + jnp.sum(down_sum * down_sum)
        + jnp.sum(gains_sum * gains_sum)
    )
    grad_norm = jnp.sqrt(total_over(square_total))
    factor = CLIP_NORM / jnp.maximum(grad_norm, CLIP_NORM)
    new_weights, new_moments, new_seconds = update_all(
        (query_key_value_weight, out_weight, router_weight, expert_in, expert_down, norm_gains),
        (qkv_sum, out_sum, router_sum, in_sum, down_sum, gains_sum),
        (query_key_value_moment, out_moment, router_moment, in_moment, down_moment, gains_moment),
        (query_key_value_second, out_second, router_second, in_second, down_second, gains_second),
        factor,
    )
    return (
        output[None],
        input_grad.astype(BF16)[None],
        grad_norm,
        *new_weights,
        *new_moments,
        *new_seconds,
    )


def solution(mesh):
    mesh = jax.sharding.Mesh(
        mesh.devices.reshape(mesh.shape["seq"], mesh.shape["fsdp"] // 4, 2, 2), ALL_AXES
    )
    token_spec = P(ROWS, "x", None)
    row_spec = P(ALL_AXES, None)
    expert_spec = P(None, ALL_AXES, None)
    state_specs = (row_spec, row_spec, row_spec, expert_spec, expert_spec, row_spec)
    return jax.shard_map(
        shards,
        mesh=mesh,
        in_specs=(token_spec, token_spec, P(ROWS, "x"), token_spec) + state_specs * 3,
        out_specs=(token_spec, token_spec, P()) + state_specs * 3,
        check_vma=False,
    )
```

time: 2410 us -> 831 us (0.34)
  waiting for transfers between devices: 1640 us -> 320 us
  matrix products: 252 us -> 22 us
  Pallas kernels: 0 us -> 200 us
  blocking collectives: 134 us -> 0 us
  local copies, waits for them, and re-layouts: 195 us -> 71.7 us
  starting transfers between devices: 32.8 us -> 93.8 us
  other arithmetic: 121 us -> 93.4 us
    reduce_scatter x4 -> x2, waiting for transfers between devices: 1310 us -> 0.01 us  [the longest x1 0.01 us: shards(): chunk_sum_one = lax.psum_scatter(total_one, 'z', scatter_dimension=0)]
    ppermute x0 -> x61, waiting for transfers between devices: none -> 320 us  [the longest x46 274 us: swap(): return lax.ppermute(value, axis, [(0, 1), (1, 0)])]
    dot_general x28 -> x6, matrix products: 250 us -> 22 us  [the longest x2 12.5 us: dot_nt(): lax.dot_general(a, b, (((1,), (1,)), ((), ())), preferred_element_type=F32)]
    pallas_call x0 -> x17, Pallas kernels: none -> 200 us  [the longest x2 130 us: expert_pass(): pl.pallas_call(functools.partial(expert_kernel, before is not None), grid...]
    all_gather x4 -> x2, waiting for transfers between devices: 180 us -> 0.01 us  [gather_expert(): whole = lax.all_gather(chunk, 'z')]
    all_gather x3 -> x0, blocking collectives: 94.4 us -> none  [the longest x1 43.8 us: shards(): lax.all_gather(router_weight.astype(jnp.bfloat16), ('seq', 'fsdp'), axis=...]
    ppermute x0 -> x61, starting transfers between devices: none -> 93.2 us  [the longest x46 72.5 us: swap(): return lax.ppermute(value, axis, [(0, 1), (1, 0)])]
    unnamed x12 -> x4, waiting for transfers between devices: 88.9 us -> 0.07 us
  transfers between devices with their start and end apart: 18 -> 65, of which waited for: 12 -> 29; matrix products, arithmetic and copies ran while one was open for 12% -> 16% of each run, Pallas kernels for 0% -> 24%
where the time goes in v1:
time: 831 us; the launch traced here: 822 us
  waiting for transfers between devices  320 us (39%)
  Pallas kernels  200 us (24%)
  starting transfers between devices  93.8 us (11%)
  other arithmetic  93.4 us (11%)
  local copies, waits for them, and re-layouts  71.7 us (9%)
  matrix products  22 us (3%)
  between operations  21.4 us (3%)
    ppermute x46, waiting for transfers between devices, swap(): return lax.ppermute(value, axis, [(0, 1), (1, 0)])  274 us
    pallas_call x2, Pallas kernels, expert_pass(): pl.pallas_call(functools.partial(expert_kernel, before is not None), grid...  130 us
    ppermute x46, starting transfers between devices, swap(): return lax.ppermute(value, axis, [(0, 1), (1, 0)])  72.5 us
    ppermute x15, waiting for transfers between devices, rotate(): lax.ppermute(value, 'z', [(i, (i + step) % size) for i in range(size)])  46.6 us
    unnamed x183, local copies, waits for them, and re-layouts  24.2 us
    ppermute x15, starting transfers between devices, rotate(): lax.ppermute(value, 'z', [(i, (i + step) % size) for i in range(size)])  20.7 us
    pallas_call x1, Pallas kernels, attend_back(): pl.pallas_call(attend_back_kernel, grid_spec=pltpu.PrefetchScalarGridSpec...  16.7 us
  transfers between devices with their start and end apart: 65, of which 29 were waited for; matrix products, arithmetic and copies ran while one was open for 16% of the time, Pallas kernels for 24%

profile of v1, /device:TPU:1, one launch (start us, length us, event | category | flops | bytes accessed | tf_op | source)
XLA Modules:
  0.0 822.4 jit_solution(8450953542298449376)
XLA Ops:
  30.2 15.1 %collective-permute-done.1 = bf16[48,3712]{1,0:T(8,128)(2,1)} collective-permute-done((bf16[48,3712]{1,0:T(8,128)(2,1)}, bf16[48,3712]{1,0:T(8,128)(2,1)}, u32[]{:S(2)}, u32[]{:S(2)}) %collective-permute-start.1) | collective-permute-done | bytes 356384 | tf_op jit(solution)/shard_map/ppermute | solution.py:111
  53.4 5.0 collective-permute-done.5
  63.3 14.1 %collective-permute-done.4.refs_1_ = bf16[2,4,48,1024]{3,2,1,0:T(8,128)(2,1)S(1)} collective-permute-done((bf16[2,4,48,1024]{3,2,1,0:T(8,128)(2,1)S(1)}, bf16[2,4,48,1024]{3,2,1,0:T(8,128)(2,1)S(1)}, u32[]{:S(2)}, u32[]{:S(2)}) %collective-permute-start.4) | collective-permute-done | bytes 786464 | tf_op jit(solution)/shard_map/ppermute | solution.py:106
  85.4 10.6 %collective-permute-done.23 = bf16[144,1536]{1,0:T(8,128)(2,1)S(1)} collective-permute-done((bf16[144,1536]{1,0:T(8,128)(2,1)S(1)}, bf16[144,1536]{1,0:T(8,128)(2,1)S(1)}, u32[]{:S(2)}, u32[]{:S(2)}) %collective-permute-start.23) | collective-permute-done | bytes 442400 | tf_op jit(solution)/shard_map/ppermute | solution.py:106
  100.7 3.9 copy.231.own
  108.3 10.8 %project.1 = (bf16[512,1536]{1,0:T(8,128)(2,1)S(1)}, bf16[512,512]{1,0:T(8,128)(2,1)S(1)}, bf16[512,1536]{1,0:T(8,128)(2,1)S(1)}, bf16[1536,2048]{1,0:T(8,128)(2,1)}, bf16[1536,128]{1,0:T(8,128)(2,1)S(1)}) custom-call(s32[4]{0:T(128)S(1)} %pad_add_fusion.2.place_ref, bf16[512,1536]{1,0:T(8,128)(2,1)S(1)} %bitcast.287, ...), custom_call_target="tpu_custom_call" | custom-call | flops 9663676416 | bytes 20971520 | tf_op jit(solution)/shard_map/project/pallas_call | solution.py:371
  123.1 10.0 %collective-permute-done.8.kp_ref.vp_ref.refs_1_ = bf16[512,512]{1,0:T(8,128)(2,1)S(1)} collective-permute-done((bf16[512,512]{1,0:T(8,128)(2,1)S(1)}, bf16[512,512]{1,0:T(8,128)(2,1)S(1)}, u32[]{:S(2)}, u32[]{:S(2)}) %collective-permute-start.8) | collective-permute-done | bytes 524320 | tf_op jit(solution)/shard_map/ppermute | solution.py:106
  136.4 13.2 %collective-permute-done.11 = bf16[2,4,48,1536]{3,2,1,0:T(8,128)(2,1)} collective-permute-done((bf16[2,4,48,1536]{3,2,1,0:T(8,128)(2,1)}, bf16[2,4,48,1536]{3,2,1,0:T(8,128)(2,1)}, u32[]{:S(2)}, u32[]{:S(2)}) %collective-permute-start.11) | collective-permute-done | bytes 1179680 | tf_op jit(solution)/shard_map/ppermute | solution.py:106
  156.2 33.2 %collective-permute-done.19.refs_7_ = bf16[512,1536]{1,0:T(8,128)(2,1)} collective-permute-done((bf16[512,1536]{1,0:T(8,128)(2,1)}, bf16[512,1536]{1,0:T(8,128)(2,1)}, u32[]{:S(2)}, u32[]{:S(2)}) %collective-permute-start.19) | collective-permute-done | bytes 1572896 | tf_op jit(solution)/shard_map/ppermute | solution.py:106
  189.4 4.0 pad_maximum_fusion
  195.9 14.4 %attend.1 = (bf16[512,1536]{1,0:T(8,128)(2,1)S(1)}, f32[12,512,1]{2,1,0:T(8,128)S(1)}) custom-call(s32[1]{0:T(128)} %bitcast.half_ref, bf16[512,1536]{1,0:T(8,128)(2,1)S(1)} %copy-done.30, bf16[512,512]{1,0:T(8,128)(2,1)S(1)} %copy-done.26, bf16[512,512]{1,0:T(8,128)(2,1)S(1)} %copy-done.26, bf16[512,512]{1,0:T(8,128)(2,1)S(1)} %copy-done.18, ...), custom_call_target="tpu_custom_call" | custom-call | flops 3221225472 | bytes 16777216 | tf_op jit(solution)/shard_map/attend/pallas_call | solution.py:533
  218.0 10.9 %join.1 = (f32[512,1536]{1,0:T(8,128)S(1)}, bf16[512,1536]{1,0:T(8,128)(2,1)}, f32[512,1]{1,0:T(8,128)S(1)}, bf16[1536,1536]{1,0:T(8,128)(2,1)}) custom-call(s32[4]{0:T(128)S(1)} %pad_add_fusion.2.place_ref, bf16[512,1536]{1,0:T(8,128)(2,1)S(1)} %copy-done.32, bf16[512,1536]{1,0:T(8,128)(2,1)S(1)} %bitcast.288, f32[1,1536]{1,0:T(1,128)S(1)} %reshape.298.gain_ref, ...), custom_call_target="tpu_custom_call" | custom-call | flops 4831838208 | bytes 16777216 | tf_op jit(solution)/shard_map/join/pallas_call | solution.py:451
  229.6 8.2 collective-permute-start.16
  238.4 34.3 %collective-permute-done.16.refs_3_ = bf16[512,1536]{1,0:T(8,128)(2,1)} collective-permute-done((bf16[512,1536]{1,0:T(8,128)(2,1)}, bf16[512,1536]{1,0:T(8,128)(2,1)}, u32[]{:S(2)}, u32[]{:S(2)}) %collective-permute-start.16) | collective-permute-done | bytes 1572896 | tf_op jit(solution)/shard_map/ppermute | solution.py:106
  285.4 3.7 slice_bitcast_fusion.3
  292.8 60.7 %expert.2 = (bf16[2,512,1536]{2,1,0:T(8,128)(2,1)}, bf16[2,512,1536]{2,1,0:T(8,128)(2,1)}, bf16[2,512,1536]{2,1,0:T(8,128)(2,1)}, bf16[2,512,1536]{2,1,0:T(8,128...) custom-call(s32[5]{0:T(128)} %concatenate.94.place_ref, ...), custom_call_target="tpu_custom_call" | custom-call | flops 70464307200 | bytes 50331648 | tf_op jit(solution)/shard_map/expert/pallas_call | solution.py:828
  353.8 16.2 %collective-permute-done.15.refs_1_ = bf16[4,2,144,1536]{3,2,1,0:T(8,128)(2,1)} collective-permute-done((bf16[4,2,144,1536]{3,2,1,0:T(8,128)(2,1)}, bf16[4,2,144,1536]{3,2,1,0:T(8,128)(2,1)}, u32[]{:S(2)}, u32[]{:S(2)}) %collective-permute-start.15) | collective-permute-done | bytes 3538976 | tf_op jit(solution)/shard_map/ppermute | solution.py:106
  370.0 69.7 %expert.3 = (bf16[2,512,1536]{2,1,0:T(8,128)(2,1)}, bf16[2,512,1536]{2,1,0:T(8,128)(2,1)}, bf16[2,512,1536]{2,1,0:T(8,128)(2,1)}, bf16[2,512,1536]{2,1,0:T(8,128...) custom-call(s32[5]{0:T(128)} %concatenate.91.place_ref, ...), custom_call_target="tpu_custom_call" | custom-call | flops 70464307200 | bytes 50331648 | tf_op jit(solution)/shard_map/expert/pallas_call | solution.py:828
  439.7 6.2 collective-permute-done.25.refs_1_
  446.6 5.5 collective-permute-done.26
  456.9 5.7 collective-permute-start.27
  462.6 4.6 add_convert_fusion.1.refs_1_
  467.2 30.2 %collective-permute-done.27.refs_0_ = bf16[512,1536]{1,0:T(8,128)(2,1)} collective-permute-done((bf16[512,1536]{1,0:T(8,128)(2,1)}, bf16[512,1536]{1,0:T(8,128)(2,1)}, u32[]{:S(2)}, u32[]{:S(2)}) %collective-permute-start.27) | collective-permute-done | bytes 1572896 | tf_op jit(solution)/shard_map/ppermute | solution.py:106
  506.3 2.9 convert_element_type.314
  511.3 3.2 fusion.87
  514.5 4.3 multiply_reduce_fusion
  519.3 24.8 %collective-permute-done.29.refs_2_ = bf16[512,1536]{1,0:T(8,128)(2,1)S(1)} collective-permute-done((bf16[512,1536]{1,0:T(8,128)(2,1)S(1)}, bf16[512,1536]{1,0:T(8,128)(2,1)S(1)}, u32[]{:S(2)}, u32[]{:S(2)}) %collective-permute-start.29) | collective-permute-done | bytes 1572896 | tf_op jit(solution)/shard_map/ppermute | solution.py:106
  544.1 4.9 fusion.111
  549.1 6.8 grad_rows.2
  555.9 3.5 copy.248
  562.2 6.1 convolution_convert_fusion.refs_0_
  568.2 14.8 %collective-permute-done.34.refs_3_ = bf16[4,2,144,1536]{3,2,1,0:T(8,128)(2,1)} collective-permute-done((bf16[4,2,144,1536]{3,2,1,0:T(8,128)(2,1)}, bf16[4,2,144,1536]{3,2,1,0:T(8,128)(2,1)}, u32[]{:S(2)}, u32[]{:S(2)}) %collective-permute-start.34) | collective-permute-done | bytes 3538976 | tf_op jit(solution)/shard_map/ppermute | solution.py:106
  584.5 16.7 %attend_back.1 = (bf16[512,1536]{1,0:T(8,128)(2,1)S(1)}, f32[512,256]{1,0:T(8,128)S(1)}, f32[512,256]{1,0:T(8,128)S(1)}, f32[512,256]{1,0:T(8,128)S(1)}, f32[512,256]{1,0:T(8,128)S(1)}) custom-call(s32[1]{0:T(128)} %bitcast.half_ref, bf16[512,1536]{1,0:T(8,128)(2,1)} %copy-done.29, bf16[512,512]{1,0:T(8,128)(2,1)S(1)} %copy-done.27, ...), custom_call_target="tpu_custom_call" | custom-call | flops 8053063680 | bytes 25165824 | tf_op jit(solution)/shard_map/attend_back/pallas_call | solution.py:615
  602.1 9.9 %collective-permute-start.35 = (bf16[512,512]{1,0:T(8,128)(2,1)}, bf16[512,512]{1,0:T(8,128)(2,1)S(1)}, u32[]{:S(2)}, u32[]{:S(2)}) collective-permute-start(bf16[512,512]{1,0:T(8,128)(2,1)} %pad_maximum_fusion.7), channel_id=1, source_target_pairs={{0,16},{16,0},{1,17},{17,1},{2,18},{18,2},{3,19},{19,3},{4,20},{20... | collective-permute-start | bytes 1572872 | tf_op jit(solution)/shard_map/ppermute | solution.py:106
  618.7 5.0 add_convert_fusion.refs_2_
  626.6 23.9 %collective-permute-done.33.refs_0_ = bf16[2,4,48,1664]{3,2,1,0:T(8,128)(2,1)S(1)} collective-permute-done((bf16[2,4,48,1664]{3,2,1,0:T(8,128)(2,1)}, bf16[2,4,48,1664]{3,2,1,0:T(8,128)(2,1)S(1)}, u32[]{:S(2)}, u32[]{:S(2)}) %collective-permute-start.33) | collective-permute-done | bytes 1277984 | tf_op jit(solution)/shard_map/ppermute | solution.py:106
  658.4 9.6 %grad_rows.3 = (bf16[2,2,4,48,1024]{4,3,2,1,0:T(8,128)(2,1)S(1)}, bf16[2,2,4,48,1024]{4,3,2,1,0:T(8,128)(2,1)}, bf16[2,2,4,48,1024]{4,3,2,1,0:T(8,128)(2,1)S(1)}, bf16[2,2,4,48,1024]{4,3,2,1,0:T(8,128)(2,1)}) custom-call(s32[4]{0:T(128)S(1)} %pad_add_fusion.2.place_ref, bf16[512,1536]{1,0:T(8,128)(2,1)} %copy-done.34, ...), custom_call_target="tpu_custom_call" | custom-call | flops 6442450944 | bytes 12582912 | tf_op jit(solution)/shard_map/grad_rows/pallas_call | solution.py:238
  674.5 8.5 %collective-permute-start.51 = (bf16[48,1664]{1,0:T(8,128)(2,1)S(1)}, bf16[48,1664]{1,0:T(8,128)(2,1)S(1)}, u32[]{:S(2)}, u32[]{:S(2)}) collective-permute-start(bf16[48,1664]{1,0:T(8,128)(2,1)S(1)} %get-tuple-element.272), channel_id=1, source_target_pairs={{0,12},{4,0},{8,4},{12,8},{1,13},{5,1},{9,5},{13,9},{2,14},{6,2},{... | collective-permute-start | bytes 479240 | tf_op jit(solution)/shard_map/ppermute | solution.py:111
  684.4 9.7 %collective-permute-done.51 = bf16[48,1664]{1,0:T(8,128)(2,1)S(1)} collective-permute-done((bf16[48,1664]{1,0:T(8,128)(2,1)S(1)}, bf16[48,1664]{1,0:T(8,128)(2,1)S(1)}, u32[]{:S(2)}, u32[]{:S(2)}) %collective-permute-start.51) | collective-permute-done | bytes 159776 | tf_op jit(solution)/shard_map/ppermute | solution.py:111
  695.6 13.5 %collective-permute-done.50 = bf16[48,1664]{1,0:T(8,128)(2,1)S(1)} collective-permute-done((bf16[48,1664]{1,0:T(8,128)(2,1)S(1)}, bf16[48,1664]{1,0:T(8,128)(2,1)S(1)}, u32[]{:S(2)}, u32[]{:S(2)}) %collective-permute-start.50) | collective-permute-done | bytes 159776 | tf_op jit(solution)/shard_map/ppermute | solution.py:111
  718.8 12.7 %collective-permute-done.43.refs_2_ = bf16[2,4,48,1024]{3,2,1,0:T(8,128)(2,1)S(1)} collective-permute-done((bf16[2,4,48,1024]{3,2,1,0:T(8,128)(2,1)S(1)}, bf16[2,4,48,1024]{3,2,1,0:T(8,128)(2,1)S(1)}, u32[]{:S(2)}, u32[]{:S(2)}) %collective-permute-start.43) | collective-permute-done | bytes 786464 | tf_op jit(solution)/shard_map/ppermute | solution.py:106
  739.4 3.5 collective-permute-done.44
  749.1 4.7 collective-permute-done.53
  756.5 3.0 collective-permute-start.54
  760.7 7.3 collective-permute-done.40
  779.8 6.4 fusion.1
  791.3 3.6 collective-permute-start.60
  803.7 7.5 multiply_subtract_fusion
  (458 shorter events, 193.9 us)
Async XLA Ops:
  7.2 206.0 %all-gather.5.cloned.1.call-start = ((), (), s32[]{:S(2)}) async-start(), calls=%async_computation.3 | async-start | bytes 4423680 | tf_op jit(solution)/shard_map/all_gather | solution.py:890
  16.7 12.6 %collective-permute-start.2 = (bf16[48,3712]{1,0:T(8,128)(2,1)}, bf16[48,3712]{1,0:T(8,128)(2,1)}, u32[]{:S(2)}, u32[]{:S(2)}) collective-permute-start(bf16[48,3712]{1,0:T(8,128)(2,1)} %concatenate.86), channel_id=1, source_target_pairs={{0,4},{4,8},{8,12},{12,0},{1,5},{5,9},{9,13},{13,1},{2,6},{6,10},{... | collective-permute-start | bytes 1069064 | tf_op jit(solution)/shard_map/ppermute | solution.py:111
  18.8 26.4 %collective-permute-start.1 = (bf16[48,3712]{1,0:T(8,128)(2,1)}, bf16[48,3712]{1,0:T(8,128)(2,1)}, u32[]{:S(2)}, u32[]{:S(2)}) collective-permute-start(bf16[48,3712]{1,0:T(8,128)(2,1)} %concatenate.86), channel_id=1, source_target_pairs={{0,8},{4,12},{8,0},{12,4},{1,9},{5,13},{9,1},{13,5},{2,10},{6,14},... | collective-permute-start | bytes 1069064 | tf_op jit(solution)/shard_map/ppermute | solution.py:111
  21.1 25.0 %collective-permute-start = (bf16[48,3712]{1,0:T(8,128)(2,1)}, bf16[48,3712]{1,0:T(8,128)(2,1)}, u32[]{:S(2)}, u32[]{:S(2)}) collective-permute-start(bf16[48,3712]{1,0:T(8,128)(2,1)} %concatenate.86), channel_id=1, source_target_pairs={{0,12},{4,0},{8,4},{12,8},{1,13},{5,1},{9,5},{13,9},{2,14},{6,2},{... | collective-permute-start | bytes 1069064 | tf_op jit(solution)/shard_map/ppermute | solution.py:111
  25.5 36.0 %collective-permute-start.13 = (bf16[2,2,72,1536]{3,2,1,0:T(8,128)(2,1)}, bf16[2,2,72,1536]{3,2,1,0:T(8,128)(2,1)}, u32[]{:S(2)}, u32[]{:S(2)}) collective-permute-start(bf16[2,2,72,1536]{3,2,1,0:T(8,128)(2,1)} %get-tuple-element.254), channel_id=1, source_target_pairs={{0,1},{1,0},{2,3},{3,2},{4,5},{5,4},{6,7},{7,6},{8,9},{9,8},{10,11... | collective-permute-start | bytes 2654216 | tf_op jit(solution)/shard_map/ppermute | solution.py:106
  47.2 11.2 %collective-permute-start.5 = (bf16[4,48,1152]{2,1,0:T(8,128)(2,1)S(1)}, bf16[4,48,1152]{2,1,0:T(8,128)(2,1)S(1)}, u32[]{:S(2)}, u32[]{:S(2)}) collective-permute-start(bf16[4,48,1152]{2,1,0:T(8,128)(2,1)S(1)} %get-tuple-element.277), channel_id=1, source_target_pairs={{0,2},{2,0},{1,3},{3,1},{4,6},{6,4},{5,7},{7,5},{8,10},{10,8},{9,1... | collective-permute-start | bytes 1327112 | tf_op jit(solution)/shard_map/ppermute | solution.py:106
  58.5 21.8 %collective-permute-start.6 = (bf16[2,4,48,1152]{3,2,1,0:T(8,128)(2,1)S(1)}, bf16[2,4,48,1152]{3,2,1,0:T(8,128)(2,1)S(1)}, u32[]{:S(2)}, u32[]{:S(2)}) collective-permute-start(bf16[2,4,48,1152]{3,2,1,0:T(8,128)(2,1)S(1)} %get-tuple-element.268), channel_id=1, source_target_pairs={{0,16},{16,0},{1,17},{17,1},{2,18},{18,2},{3,19},{19,3},{4,20},{20... | collective-permute-start | bytes 2654216 | tf_op jit(solution)/shard_map/ppermute | solution.py:106
  61.2 16.2 %collective-permute-start.4 = (bf16[2,4,48,1024]{3,2,1,0:T(8,128)(2,1)S(1)}, bf16[2,4,48,1024]{3,2,1,0:T(8,128)(2,1)S(1)}, u32[]{:S(2)}, u32[]{:S(2)}) collective-permute-start(bf16[2,4,48,1024]{3,2,1,0:T(8,128)(2,1)S(1)} %get-tuple-element.270), channel_id=1, source_target_pairs={{0,2},{2,0},{1,3},{3,1},{4,6},{6,4},{5,7},{7,5},{8,10},{10,8},{9,1... | collective-permute-start | bytes 2359304 | tf_op jit(solution)/shard_map/ppermute | solution.py:106
  82.3 23.5 %collective-permute-start.7 = (bf16[2,2,4,48,2176]{4,3,2,0,1:T(8,128)(2,1)}, bf16[2,2,4,48,2176]{4,3,2,0,1:T(8,128)(2,1)}, u32[]{:S(2)}, u32[]{:S(2)}) collective-permute-start(bf16[2,2,4,48,2176]{4,3,2,0,1:T(8,128)(2,1)} %maximum_maximum_fusion), channel_id=1, source_target_pairs={{0,1},{1,0},{2,3},{3,2},{4,5},{5,4},{6,7},{7,6},{8,9},{9,8},{10,11... | collective-permute-start | bytes 10027016 | tf_op jit(solution)/shard_map/ppermute | solution.py:106
  84.1 11.9 %collective-permute-start.23 = (bf16[144,1536]{1,0:T(8,128)(2,1)S(1)}, bf16[144,1536]{1,0:T(8,128)(2,1)S(1)}, u32[]{:S(2)}, u32[]{:S(2)}) collective-permute-start(bf16[144,1536]{1,0:T(8,128)(2,1)S(1)} %get-tuple-element.264), channel_id=1, source_target_pairs={{0,16},{16,0},{1,17},{17,1},{2,18},{18,2},{3,19},{19,3},{4,20},{20... | collective-permute-start | bytes 1327112 | tf_op jit(solution)/shard_map/ppermute | solution.py:106
  97.0 194.5 %all-gather.3.cloned.1.call-start = ((), (), s32[]{:S(2)}) async-start(), calls=%async_computation.2 | async-start | bytes 4423680 | tf_op jit(solution)/shard_map/all_gather | solution.py:890
  104.6 16.6 %collective-permute-start.10 = (bf16[4,48,1536]{2,1,0:T(8,128)(2,1)}, bf16[4,48,1536]{2,1,0:T(8,128)(2,1)S(1)}, u32[]{:S(2)}, u32[]{:S(2)}) collective-permute-start(bf16[4,48,1536]{2,1,0:T(8,128)(2,1)} %hold.9), channel_id=1, source_target_pairs={{0,16},{16,0},{1,17},{17,1},{2,18},{18,2},{3,19},{19,3},{4,20},{20... | collective-permute-start | bytes 1769480 | tf_op jit(solution)/shard_map/ppermute | solution.py:106
  120.4 12.7 %collective-permute-start.8 = (bf16[512,512]{1,0:T(8,128)(2,1)S(1)}, bf16[512,512]{1,0:T(8,128)(2,1)S(1)}, u32[]{:S(2)}, u32[]{:S(2)}) collective-permute-start(bf16[512,512]{1,0:T(8,128)(2,1)S(1)} %get-tuple-element.64.ko_ref.vo_ref), channel_id=1, source_target_pairs={{0,16},{16,0},{1,17},{17,1},{2,18},{18,2},{3,19},{19,3},{4,20},{20... | collective-permute-start | bytes 1572872 | tf_op jit(solution)/shard_map/ppermute | solution.py:106
  122.8 26.7 %collective-permute-start.11 = (bf16[2,4,48,1536]{3,2,1,0:T(8,128)(2,1)}, bf16[2,4,48,1536]{3,2,1,0:T(8,128)(2,1)}, u32[]{:S(2)}, u32[]{:S(2)}) collective-permute-start(bf16[2,4,48,1536]{3,2,1,0:T(8,128)(2,1)} %get-tuple-element.256), channel_id=1, source_target_pairs={{0,2},{2,0},{1,3},{3,1},{4,6},{6,4},{5,7},{7,5},{8,10},{10,8},{9,1... | collective-permute-start | bytes 3538952 | tf_op jit(solution)/shard_map/ppermute | solution.py:106
  135.4 18.4 %collective-permute-start.14 = (bf16[144,1536]{1,0:T(8,128)(2,1)S(1)}, bf16[144,1536]{1,0:T(8,128)(2,1)S(1)}, u32[]{:S(2)}, u32[]{:S(2)}) collective-permute-start(bf16[144,1536]{1,0:T(8,128)(2,1)S(1)} %get-tuple-element.266), channel_id=1, source_target_pairs={{0,16},{16,0},{1,17},{17,1},{2,18},{18,2},{3,19},{19,3},{4,20},{20... | collective-permute-start | bytes 1327112 | tf_op jit(solution)/shard_map/ppermute | solution.py:106
  151.1 62.4 %collective-permute-start.12 = (bf16[2,2,4,48,1536]{4,3,2,1,0:T(8,128)(2,1)S(1)}, bf16[2,2,4,48,1536]{4,3,2,1,0:T(8,128)(2,1)}, u32[]{:S(2)}, u32[]{:S(2)}) collective-permute-start(bf16[2,2,4,48,1536]{4,3,2,1,0:T(8,128)(2,1)S(1)} %pad_maximum_fusion.1.own), channel_id=1, source_target_pairs={{0,1},{1,0},{2,3},{3,2},{4,5},{5,4},{6,7},{7,6},{8,9},{9,8},{10,11... | collective-permute-start | bytes 7077896 | tf_op jit(solution)/shard_map/ppermute | solution.py:106
  153.1 36.3 %collective-permute-start.19 = (bf16[512,1536]{1,0:T(8,128)(2,1)}, bf16[512,1536]{1,0:T(8,128)(2,1)}, u32[]{:S(2)}, u32[]{:S(2)}) collective-permute-start(bf16[512,1536]{1,0:T(8,128)(2,1)} %bitcast.46.refs_6_), channel_id=1, source_target_pairs={{0,16},{16,0},{1,17},{17,1},{2,18},{18,2},{3,19},{19,3},{4,20},{20... | collective-permute-start | bytes 4718600 | tf_op jit(solution)/shard_map/ppermute | solution.py:106
  154.9 428.1 %reduce-scatter.3.cloned.1.call-start = ((), (), s32[]{:S(2)}) async-start(), calls=%async_computation.4 | async-start | bytes 4423680 | tf_op jit(solution)/shard_map/reduce_scatter | solution.py:1092
  155.1 40.2 %collective-permute-start.9 = (s32[512]{0:T(512)S(1)}, s32[512]{0:T(512)}, u32[]{:S(2)}, u32[]{:S(2)}) collective-permute-start(s32[512]{0:T(512)S(1)} %bitcast.289), channel_id=1, source_target_pairs={{0,16},{16,0},{1,17},{17,1},{2,18},{18,2},{3,19},{19,3},{4,20},{20... | collective-permute-start | bytes 6152 | tf_op jit(solution)/shard_map/ppermute | solution.py:106
  193.4 92.0 %collective-permute-start.20 = (bf16[2,512,1536]{2,1,0:T(8,128)(2,1)}, bf16[2,512,1536]{2,1,0:T(8,128)(2,1)}, u32[]{:S(2)}, u32[]{:S(2)}) collective-permute-start(bf16[2,512,1536]{2,1,0:T(8,128)(2,1)} %pad_maximum_fusion), channel_id=1, source_target_pairs={{0,1},{1,0},{2,3},{3,2},{4,5},{5,4},{6,7},{7,6},{8,9},{9,8},{10,11... | collective-permute-start | bytes 9437192 | tf_op jit(solution)/shard_map/ppermute | solution.py:106
  213.3 79.5 %collective-permute-start.24 = (bf16[4,2,144,1536]{3,2,1,0:T(8,128)(2,1)}, bf16[4,2,144,1536]{3,2,1,0:T(8,128)(2,1)}, u32[]{:S(2)}, u32[]{:S(2)}) collective-permute-start(bf16[4,2,144,1536]{3,2,1,0:T(8,128)(2,1)} %all-gather.5.cloned.1.call-done.refs_0_), channel_id=1, source_target_pairs={{0,2},{2,0},{1,3},{3,1},{4,6},{6,4},{5,7},{7,5},{8,10},{10,8},{9,1... | collective-permute-start | bytes 10616840 | tf_op jit(solution)/shard_map/ppermute | solution.py:106
  229.6 43.1 %collective-permute-start.16 = (bf16[512,1536]{1,0:T(8,128)(2,1)}, bf16[512,1536]{1,0:T(8,128)(2,1)}, u32[]{:S(2)}, u32[]{:S(2)}) collective-permute-start(bf16[512,1536]{1,0:T(8,128)(2,1)} %get-tuple-element.68.refs_2_), channel_id=1, source_target_pairs={{0,16},{16,0},{1,17},{17,1},{2,18},{18,2},{3,19},{19,3},{4,20},{20... | collective-permute-start | bytes 4718600 | tf_op jit(solution)/shard_map/ppermute | solution.py:106
  237.8 54.9 %collective-permute-start.17 = (bf16[512,1536]{1,0:T(8,128)(2,1)}, bf16[512,1536]{1,0:T(8,128)(2,1)}, u32[]{:S(2)}, u32[]{:S(2)}) collective-permute-start(bf16[512,1536]{1,0:T(8,128)(2,1)} %get-tuple-element.68.refs_2_), channel_id=1, source_target_pairs={{0,1},{1,0},{2,3},{3,2},{4,5},{5,4},{6,7},{7,6},{8,9},{9,8},{10,11... | collective-permute-start | bytes 4718600 | tf_op jit(solution)/shard_map/ppermute | solution.py:106
  272.7 20.0 %collective-permute-start.18 = (bf16[512,1536]{1,0:T(8,128)(2,1)}, bf16[512,1536]{1,0:T(8,128)(2,1)}, u32[]{:S(2)}, u32[]{:S(2)}) collective-permute-start(bf16[512,1536]{1,0:T(8,128)(2,1)} %collective-permute-done.16.refs_3_), channel_id=1, source_target_pairs={{0,1},{1,0},{2,3},{3,2},{4,5},{5,4},{6,7},{7,6},{8,9},{9,8},{10,11... | collective-permute-start | bytes 4718600 | tf_op jit(solution)/shard_map/ppermute | solution.py:106
  291.5 78.5 %collective-permute-start.15 = (bf16[4,2,144,1536]{3,2,1,0:T(8,128)(2,1)}, bf16[4,2,144,1536]{3,2,1,0:T(8,128)(2,1)}, u32[]{:S(2)}, u32[]{:S(2)}) collective-permute-start(bf16[4,2,144,1536]{3,2,1,0:T(8,128)(2,1)} %all-gather.3.cloned.1.call-done.refs_0_), channel_id=1, source_target_pairs={{0,2},{2,0},{1,3},{3,1},{4,6},{6,4},{5,7},{7,5},{8,10},{10,8},{9,1... | collective-permute-start | bytes 10616840 | tf_op jit(solution)/shard_map/ppermute | solution.py:106
  353.5 92.3 %collective-permute-start.25 = (bf16[4,2,144,1536]{3,2,1,0:T(8,128)(2,1)}, bf16[4,2,144,1536]{3,2,1,0:T(8,128)(2,1)}, u32[]{:S(2)}, u32[]{:S(2)}) collective-permute-start(bf16[4,2,144,1536]{3,2,1,0:T(8,128)(2,1)} %get-tuple-element.77), channel_id=1, source_target_pairs={{0,2},{2,0},{1,3},{3,1},{4,6},{6,4},{5,7},{7,5},{8,10},{10,8},{9,1... | collective-permute-start | bytes 10616840 | tf_op jit(solution)/shard_map/ppermute | solution.py:106
  456.9 40.5 %collective-permute-start.27 = (bf16[512,1536]{1,0:T(8,128)(2,1)}, bf16[512,1536]{1,0:T(8,128)(2,1)}, u32[]{:S(2)}, u32[]{:S(2)}) collective-permute-start(bf16[512,1536]{1,0:T(8,128)(2,1)} %fusion.26), channel_id=1, source_target_pairs={{0,16},{16,0},{1,17},{17,1},{2,18},{18,2},{3,19},{19,3},{4,20},{20... | collective-permute-start | bytes 4718600 | tf_op jit(solution)/shard_map/ppermute | solution.py:106
  498.3 237.7 %reduce-scatter.5.cloned.1.call-start = ((), (), s32[]{:S(2)}) async-start(), calls=%async_computation.5 | async-start | bytes 4423680 | tf_op jit(solution)/shard_map/reduce_scatter | solution.py:1152
  505.2 77.9 %collective-permute-start.34 = (bf16[4,2,144,1536]{3,2,1,0:T(8,128)(2,1)}, bf16[4,2,144,1536]{3,2,1,0:T(8,128)(2,1)}, u32[]{:S(2)}, u32[]{:S(2)}) collective-permute-start(bf16[4,2,144,1536]{3,2,1,0:T(8,128)(2,1)} %get-tuple-element.85), channel_id=1, source_target_pairs={{0,2},{2,0},{1,3},{3,1},{4,6},{6,4},{5,7},{7,5},{8,10},{10,8},{9,1... | collective-permute-start | bytes 10616840 | tf_op jit(solution)/shard_map/ppermute | solution.py:106
  509.7 34.4 %collective-permute-start.29 = (bf16[512,1536]{1,0:T(8,128)(2,1)S(1)}, bf16[512,1536]{1,0:T(8,128)(2,1)S(1)}, u32[]{:S(2)}, u32[]{:S(2)}) collective-permute-start(bf16[512,1536]{1,0:T(8,128)(2,1)S(1)} %fusion.28), channel_id=1, source_target_pairs={{0,16},{16,0},{1,17},{17,1},{2,18},{18,2},{3,19},{19,3},{4,20},{20... | collective-permute-start | bytes 4718600 | tf_op jit(solution)/shard_map/ppermute | solution.py:106
  559.4 52.6 %collective-permute-start.32 = (bf16[2,2,4,48,1664]{4,3,2,0,1:T(8,128)(2,1)}, bf16[2,2,4,48,1664]{4,3,2,0,1:T(8,128)(2,1)}, u32[]{:S(2)}, u32[]{:S(2)}) collective-permute-start(bf16[2,2,4,48,1664]{4,3,2,0,1:T(8,128)(2,1)} %copy.248), channel_id=1, source_target_pairs={{0,1},{1,0},{2,3},{3,2},{4,5},{5,4},{6,7},{7,6},{8,9},{9,8},{10,11... | collective-permute-start | bytes 7667720 | tf_op jit(solution)/shard_map/ppermute | solution.py:106
  602.1 21.6 %collective-permute-start.35 = (bf16[512,512]{1,0:T(8,128)(2,1)}, bf16[512,512]{1,0:T(8,128)(2,1)S(1)}, u32[]{:S(2)}, u32[]{:S(2)}) collective-permute-start(bf16[512,512]{1,0:T(8,128)(2,1)} %pad_maximum_fusion.7), channel_id=1, source_target_pairs={{0,16},{16,0},{1,17},{17,1},{2,18},{18,2},{3,19},{19,3},{4,20},{20... | collective-permute-start | bytes 1572872 | tf_op jit(solution)/shard_map/ppermute | solution.py:106
  617.1 33.4 %collective-permute-start.33 = (bf16[2,4,48,1664]{3,2,1,0:T(8,128)(2,1)}, bf16[2,4,48,1664]{3,2,1,0:T(8,128)(2,1)S(1)}, u32[]{:S(2)}, u32[]{:S(2)}) collective-permute-start(bf16[2,4,48,1664]{3,2,1,0:T(8,128)(2,1)} %fusion.32), channel_id=1, source_target_pairs={{0,16},{16,0},{1,17},{17,1},{2,18},{18,2},{3,19},{19,3},{4,20},{20... | collective-permute-start | bytes 3833864 | tf_op jit(solution)/shard_map/ppermute | solution.py:106
  656.3 16.9 %collective-permute-start.48 = (bf16[4,48,1664]{2,1,0:T(8,128)(2,1)}, bf16[4,48,1664]{2,1,0:T(8,128)(2,1)}, u32[]{:S(2)}, u32[]{:S(2)}) collective-permute-start(bf16[4,48,1664]{2,1,0:T(8,128)(2,1)} %fusion.45), channel_id=1, source_target_pairs={{0,2},{2,0},{1,3},{3,1},{4,6},{6,4},{5,7},{7,5},{8,10},{10,8},{9,1... | collective-permute-start | bytes 1916936 | tf_op jit(solution)/shard_map/ppermute | solution.py:106
  670.9 39.8 %collective-permute-start.42 = (bf16[2,2,4,48,1024]{4,3,2,0,1:T(8,128)(2,1)}, bf16[2,2,4,48,1024]{4,3,2,0,1:T(8,128)(2,1)}, u32[]{:S(2)}, u32[]{:S(2)}) collective-permute-start(bf16[2,2,4,48,1024]{4,3,2,0,1:T(8,128)(2,1)} %copy.251), channel_id=1, source_target_pairs={{0,1},{1,0},{2,3},{3,2},{4,5},{5,4},{6,7},{7,6},{8,9},{9,8},{10,11... | collective-permute-start | bytes 4718600 | tf_op jit(solution)/shard_map/ppermute | solution.py:106
  673.2 40.9 %collective-permute-start.36 = (bf16[2,2,4,48,1024]{4,3,2,1,0:T(8,128)(2,1)}, bf16[2,2,4,48,1024]{4,3,2,1,0:T(8,128)(2,1)}, u32[]{:S(2)}, u32[]{:S(2)}) collective-permute-start(bf16[2,2,4,48,1024]{4,3,2,1,0:T(8,128)(2,1)} %get-tuple-element.100), channel_id=1, source_target_pairs={{0,1},{1,0},{2,3},{3,2},{4,5},{5,4},{6,7},{7,6},{8,9},{9,8},{10,11... | collective-permute-start | bytes 4718600 | tf_op jit(solution)/shard_map/ppermute | solution.py:106
  674.5 19.6 %collective-permute-start.51 = (bf16[48,1664]{1,0:T(8,128)(2,1)S(1)}, bf16[48,1664]{1,0:T(8,128)(2,1)S(1)}, u32[]{:S(2)}, u32[]{:S(2)}) collective-permute-start(bf16[48,1664]{1,0:T(8,128)(2,1)S(1)} %get-tuple-element.272), channel_id=1, source_target_pairs={{0,12},{4,0},{8,4},{12,8},{1,13},{5,1},{9,5},{13,9},{2,14},{6,2},{... | collective-permute-start | bytes 479240 | tf_op jit(solution)/shard_map/ppermute | solution.py:111
  683.1 26.0 %collective-permute-start.50 = (bf16[48,1664]{1,0:T(8,128)(2,1)S(1)}, bf16[48,1664]{1,0:T(8,128)(2,1)S(1)}, u32[]{:S(2)}, u32[]{:S(2)}) collective-permute-start(bf16[48,1664]{1,0:T(8,128)(2,1)S(1)} %get-tuple-element.273), channel_id=1, source_target_pairs={{0,8},{4,12},{8,0},{12,4},{1,9},{5,13},{9,1},{13,5},{2,10},{6,14},... | collective-permute-start | bytes 479240 | tf_op jit(solution)/shard_map/ppermute | solution.py:111
  683.4 25.7 %collective-permute-start.49 = (bf16[48,1664]{1,0:T(8,128)(2,1)S(1)}, bf16[48,1664]{1,0:T(8,128)(2,1)S(1)}, u32[]{:S(2)}, u32[]{:S(2)}) collective-permute-start(bf16[48,1664]{1,0:T(8,128)(2,1)S(1)} %get-tuple-element.271), channel_id=1, source_target_pairs={{0,4},{4,8},{8,12},{12,0},{1,5},{5,9},{9,13},{13,1},{2,6},{6,10},{... | collective-permute-start | bytes 479240 | tf_op jit(solution)/shard_map/ppermute | solution.py:111
  694.2 53.0 %collective-permute-start.52 = (bf16[144,1536]{1,0:T(8,128)(2,1)}, bf16[144,1536]{1,0:T(8,128)(2,1)}, u32[]{:S(2)}, u32[]{:S(2)}) collective-permute-start(bf16[144,1536]{1,0:T(8,128)(2,1)} %get-tuple-element.260), channel_id=1, source_target_pairs={{0,16},{16,0},{1,17},{17,1},{2,18},{18,2},{3,19},{19,3},{4,20},{20... | collective-permute-start | bytes 1327112 | tf_op jit(solution)/shard_map/ppermute | solution.py:106
  712.9 18.7 %collective-permute-start.43 = (bf16[2,4,48,1024]{3,2,1,0:T(8,128)(2,1)S(1)}, bf16[2,4,48,1024]{3,2,1,0:T(8,128)(2,1)S(1)}, u32[]{:S(2)}, u32[]{:S(2)}) collective-permute-start(bf16[2,4,48,1024]{3,2,1,0:T(8,128)(2,1)S(1)} %fusion.42), channel_id=1, source_target_pairs={{0,16},{16,0},{1,17},{17,1},{2,18},{18,2},{3,19},{19,3},{4,20},{20... | collective-permute-start | bytes 2359304 | tf_op jit(solution)/shard_map/ppermute | solution.py:106
  716.2 18.3 %collective-permute-start.37 = (bf16[2,4,48,1024]{3,2,1,0:T(8,128)(2,1)S(1)}, bf16[2,4,48,1024]{3,2,1,0:T(8,128)(2,1)S(1)}, u32[]{:S(2)}, u32[]{:S(2)}) collective-permute-start(bf16[2,4,48,1024]{3,2,1,0:T(8,128)(2,1)S(1)} %fusion.41), channel_id=1, source_target_pairs={{0,2},{2,0},{1,3},{3,1},{4,6},{6,4},{5,7},{7,5},{8,10},{10,8},{9,1... | collective-permute-start | bytes 2359304 | tf_op jit(solution)/shard_map/ppermute | solution.py:106
  737.2 16.6 %collective-permute-start.53 = (bf16[144,1536]{1,0:T(8,128)(2,1)S(1)}, bf16[144,1536]{1,0:T(8,128)(2,1)S(1)}, u32[]{:S(2)}, u32[]{:S(2)}) collective-permute-start(bf16[144,1536]{1,0:T(8,128)(2,1)S(1)} %get-tuple-element.262), channel_id=1, source_target_pairs={{0,16},{16,0},{1,17},{17,1},{2,18},{18,2},{3,19},{19,3},{4,20},{20... | collective-permute-start | bytes 1327112 | tf_op jit(solution)/shard_map/ppermute | solution.py:106
  744.1 15.6 %collective-permute-start.47 = (bf16[48,1024]{1,0:T(8,128)(2,1)S(1)}, bf16[48,1024]{1,0:T(8,128)(2,1)S(1)}, u32[]{:S(2)}, u32[]{:S(2)}) collective-permute-start(bf16[48,1024]{1,0:T(8,128)(2,1)S(1)} %get-tuple-element.282), channel_id=1, source_target_pairs={{0,12},{4,0},{8,4},{12,8},{1,13},{5,1},{9,5},{13,9},{2,14},{6,2},{... | collective-permute-start | bytes 294920 | tf_op jit(solution)/shard_map/ppermute | solution.py:111
  744.1 16.2 %collective-permute-start.46 = (bf16[48,1024]{1,0:T(8,128)(2,1)S(1)}, bf16[48,1024]{1,0:T(8,128)(2,1)S(1)}, u32[]{:S(2)}, u32[]{:S(2)}) collective-permute-start(bf16[48,1024]{1,0:T(8,128)(2,1)S(1)} %get-tuple-element.283), channel_id=1, source_target_pairs={{0,8},{4,12},{8,0},{12,4},{1,9},{5,13},{9,1},{13,5},{2,10},{6,14},... | collective-permute-start | bytes 294920 | tf_op jit(solution)/shard_map/ppermute | solution.py:111
  744.6 16.0 %collective-permute-start.45 = (bf16[48,1024]{1,0:T(8,128)(2,1)S(1)}, bf16[48,1024]{1,0:T(8,128)(2,1)S(1)}, u32[]{:S(2)}, u32[]{:S(2)}) collective-permute-start(bf16[48,1024]{1,0:T(8,128)(2,1)S(1)} %get-tuple-element.281), channel_id=1, source_target_pairs={{0,4},{4,8},{8,12},{12,0},{1,5},{5,9},{9,13},{13,1},{2,6},{6,10},{... | collective-permute-start | bytes 294920 | tf_op jit(solution)/shard_map/ppermute | solution.py:111
  747.2 13.5 %collective-permute-start.41 = (bf16[48,1024]{1,0:T(8,128)(2,1)S(1)}, bf16[48,1024]{1,0:T(8,128)(2,1)S(1)}, u32[]{:S(2)}, u32[]{:S(2)}) collective-permute-start(bf16[48,1024]{1,0:T(8,128)(2,1)S(1)} %get-tuple-element.279), channel_id=1, source_target_pairs={{0,12},{4,0},{8,4},{12,8},{1,13},{5,1},{9,5},{13,9},{2,14},{6,2},{... | collective-permute-start | bytes 294920 | tf_op jit(solution)/shard_map/ppermute | solution.py:111
  756.5 15.0 %collective-permute-start.54 = (bf16[2,2,72,1536]{3,2,1,0:T(8,128)(2,1)}, bf16[2,2,72,1536]{3,2,1,0:T(8,128)(2,1)}, u32[]{:S(2)}, u32[]{:S(2)}) collective-permute-start(bf16[2,2,72,1536]{3,2,1,0:T(8,128)(2,1)} %fusion.38), channel_id=1, source_target_pairs={{0,1},{1,0},{2,3},{3,2},{4,5},{5,4},{6,7},{7,6},{8,9},{9,8},{10,11... | collective-permute-start | bytes 2654216 | tf_op jit(solution)/shard_map/ppermute | solution.py:106
  (106 other events, 924.0 us)
Sparse Core Ops, SparseCore 0:
  97.1 74.9 all-gather.4
  174.2 68.5 all-gather.2
  498.4 71.3 reduce-scatter.2
  623.8 81.3 reduce-scatter.4

commit v2 on v1

--- a/solution.py
+++ b/solution.py
@@ -38,6 +38,15 @@
 Z_STEPS = 4
 LANES = 128
 MIB = 1024 * 1024
+COST_SCALE = 4
+
+
+def cost(flops, bytes_accessed, transcendentals=0):
+    return pl.CostEstimate(
+        flops=flops // COST_SCALE,
+        bytes_accessed=bytes_accessed // COST_SCALE,
+        transcendentals=transcendentals // COST_SCALE,
+    )
 
 
 def rms_scale(values):
@@ -253,10 +262,8 @@
             for _ in range(2)
         ],
         compiler_params=pltpu.CompilerParams(vmem_limit_bytes=48 * MIB),
-        cost_estimate=pl.CostEstimate(
-            flops=4 * a.shape[0] * model_rows * width,
-            bytes_accessed=4 * model_rows * width,
-            transcendentals=0,
+        cost_estimate=cost(
+            4 * a.shape[0] * model_rows * width, 4 * model_rows * width
         ),
         name="grad_rows",
     )(where, *operands)
@@ -270,13 +277,6 @@
 
 def fold(kept, sent, axis):
     return kept.astype(F32) + swap(sent.astype(BF16), axis).astype(F32)
-
-
-def fold_z(blocks):
-    total = blocks[0]
-    for k in range(1, Z_STEPS):
-        total = total + rotate(blocks[k].astype(BF16), k).astype(F32)
-    return total
 
 
 def rotated(values, cosine, sine):
@@ -396,8 +396,8 @@
             jax.ShapeDtypeStruct((depth, LANES), BF16),
         ],
         compiler_params=pltpu.CompilerParams(vmem_limit_bytes=40 * MIB),
-        cost_estimate=pl.CostEstimate(
-            flops=6 * rows * depth * columns, bytes_accessed=20 * MIB, transcendentals=0
+        cost_estimate=cost(
+            6 * rows * depth * columns, 20 * MIB
         ),
         name="project",
     )(where, x, *pair, cosine, sine)
@@ -468,8 +468,8 @@
             jax.ShapeDtypeStruct((depth, width), BF16),
         ],
         compiler_params=pltpu.CompilerParams(vmem_limit_bytes=40 * MIB),
-        cost_estimate=pl.CostEstimate(
-            flops=4 * rows * depth * width, bytes_accessed=16 * MIB, transcendentals=0
+        cost_estimate=cost(
+            4 * rows * depth * width, 16 * MIB
         ),
         name="join",
     )(where, attended, x, gain, *pair)
@@ -543,10 +543,8 @@
             jax.ShapeDtypeStruct((QUERY_HEADS, rows, 1), F32),
         ],
         compiler_params=pltpu.CompilerParams(vmem_limit_bytes=40 * MIB),
-        cost_estimate=pl.CostEstimate(
-            flops=8 * rows * rows * QUERY_HEADS * HEAD_DIMENSION,
-            bytes_accessed=16 * MIB,
-            transcendentals=2 * rows * rows * QUERY_HEADS,
+        cost_estimate=cost(
+            8 * rows * rows * QUERY_HEADS * HEAD_DIMENSION, 16 * MIB, 2 * rows * rows * QUERY_HEADS
         ),
         name="attend",
     )(half, queries, own, own, previous, previous, seg_col, seg_own, seg_prev)
@@ -623,10 +621,8 @@
         out_shape=[jax.ShapeDtypeStruct((rows, QUERY_HEADS * HEAD_DIMENSION), BF16)]
         + [kv_shape] * 4,
         compiler_params=pltpu.CompilerParams(vmem_limit_bytes=48 * MIB),
-        cost_estimate=pl.CostEstimate(
-            flops=20 * rows * rows * QUERY_HEADS * HEAD_DIMENSION,
-            bytes_accessed=24 * MIB,
-            transcendentals=2 * rows * rows * QUERY_HEADS,
+        cost_estimate=cost(
+            20 * rows * rows * QUERY_HEADS * HEAD_DIMENSION, 24 * MIB, 2 * rows * rows * QUERY_HEADS
         ),
         name="attend_back",
     )(
@@ -646,14 +642,17 @@
     )
 
 
-def expert_kernel(has_before, place_ref, *refs):
+def expert_kernel(count, given, gives, grads_too, place_ref, *refs):
     refs = list(refs)
-    pieces = [refs.pop(0) for _ in range(2)]
-    x_refs, t_refs = ([refs.pop(0) for _ in range(SOURCES)] for _ in range(2))
-    rank_row_ref, rank_col_ref, router_ref = (refs.pop(0) for _ in range(3))
-    before = [refs.pop(0) for _ in range(4)] if has_before else None
-    mix_keep, mix_send, ffn_keep, ffn_send, gate_grad_ref = (refs.pop(0) for _ in range(5))
-    grads = [refs.pop(0) for _ in range(2)]
+    pop = lambda n: [refs.pop(0) for _ in range(n)]
+    pieces = pop(4)
+    x_refs, t_refs = pop(count), pop(count)
+    rank_row_ref, rank_col_ref, router_ref = pop(3)
+    given_refs = pop(4) if given else []
+    mix_refs, ffn_refs = pop(count), pop(count)
+    (gate_grad_ref,) = pop(1)
+    gives_refs = pop(4) if gives else []
+    grads = pop(4) if grads_too else []
     (
         in_w,
         down_w,
@@ -662,204 +661,216 @@
         active,
         slot_grad,
         top,
+        spread,
+        gates,
         x_held,
         t_held,
-        in_g,
-        down_g,
         sems,
         token_sems,
+        given_sems,
     ) = refs
-    source = pl.program_id(0)
-    slot = lax.rem(source, 2)
+    in_rows = in_w.shape[0] // (4 * Z_STEPS)
+    down_rows = down_w.shape[0] // (4 * Z_STEPS)
+    tokens, width = x_refs[0].shape
+    hidden = active.shape[1]
+    slots = count * CAP
+    own_slots = pl.ds(0, slots)
+    wide, narrow = 512, 256
+
+    def block_copies(outward, which):
+        copies = []
+        for (y, x), piece in zip(
+            itertools.product(range(2), range(2)), grads if outward else pieces
+        ):
+            for z in range(Z_STEPS):
+                block = (lax.rem(place_ref[0] + x, 2) * Z_STEPS + z) * 2 + lax.rem(
+                    place_ref[2] + y, 2
+                )
+                whole, rows, start = (
+                    (in_w, in_rows, 0) if which == 0 else (down_w, down_rows, in_rows)
+                )
+                ends = (
+                    piece.at[z, pl.ds(start, rows), :],
+                    whole.at[pl.ds(pl.multiple_of(block * rows, rows), rows), :],
+                )
+                if outward:
+                    ends = ends[::-1]
+                copies.append(pltpu.make_async_copy(*ends, sems.at[which, len(copies)]))
+        return copies
 
     def token_copies(s):
         return [
             pltpu.make_async_copy(many[s], held.at[s % 2], token_sems.at[i, s % 2])
             for i, (many, held) in enumerate(((x_refs, x_held), (t_refs, t_held)))
         ]
-    in_rows = in_w.shape[0] // (4 * Z_STEPS)
-    down_rows = down_w.shape[0] // (4 * Z_STEPS)
-
-    def block_copies(outward):
-        copies = []
-        for y, piece in enumerate(grads if outward else pieces):
-            for z, x in itertools.product(range(Z_STEPS), range(2)):
-                block = (x * Z_STEPS + z) * 2 + lax.rem(place_ref[2] + y, 2)
-                for whole, rows, start in (
-                    (in_g if outward else in_w, in_rows, 0),
-                    (down_g if outward else down_w, down_rows, in_rows),
-                ):
-                    ends = (
-                        piece.at[z, x, pl.ds(start, rows), :],
-                        whole.at[pl.ds(pl.multiple_of(block * rows, rows), rows), :],
-                    )
-                    if outward:
-                        ends = ends[::-1]
-                    copies.append(pltpu.make_async_copy(*ends, sems.at[len(copies)]))
-        return copies
-
-    @pl.when(source == 0)
-    def _():
-        copies = token_copies(0) + block_copies(False)
-        for copy in copies:
-            copy.start()
-        for copy in copies[2:]:
+
+    kept = (picked, joined_grad, active, slot_grad)
+    arriving = [
+        pltpu.make_async_copy(
+            ref, held.at[pl.ds(slots, held.shape[0] - slots), :], given_sems.at[i]
+        )
+        for i, (ref, held) in enumerate(zip(given_refs, kept))
+    ]
+    leaving = [
+        pltpu.make_async_copy(held.at[own_slots, :], ref, given_sems.at[i])
+        for i, (ref, held) in enumerate(zip(gives_refs, kept))
+    ]
+    weight_copies = block_copies(False, 0) + block_copies(False, 1)
+    for copy in token_copies(0) + weight_copies + arriving:
+        copy.start()
+
+    for s in range(count):
+        for copy in token_copies(s):
             copy.wait()
-
-    for s in range(SOURCES):
-
-        @pl.when(source == s)
-        def _(s=s):
-            for copy in token_copies(s):
-                copy.wait()
-            if s + 1 < SOURCES:
-                for copy in token_copies(s + 1):
-                    copy.start()
-
-    slots = pl.ds(pl.multiple_of(source * CAP, CAP), CAP)
-    tokens, width = x_refs[0].shape
-    rank_row = rank_row_ref[0]
-    expert_row = lax.broadcasted_iota(jnp.int32, (router_ref.shape[0], tokens), 0)
-    logits = jnp.where(expert_row < EXPERTS, dot_nt(router_ref[...], x_held[slot]), MASKED_SCORE)
-    exponent = jnp.exp(logits - jnp.max(logits, axis=0, keepdims=True))
-    probs = exponent / jnp.sum(exponent, axis=0, keepdims=True)
-    gate_row = jnp.sum(jnp.where(expert_row == place_ref[4], probs, 0.0), axis=0, keepdims=True)
-    chosen = (
-        lax.broadcasted_iota(jnp.int32, (CAP, tokens), 0) == rank_row
-    ).astype(F32)
-    gate = jnp.sum(chosen * gate_row, axis=1, keepdims=True)
-    spread = (
-        lax.broadcasted_iota(jnp.int32, (tokens, CAP), 1) == rank_col_ref[0]
-    ).astype(F32).astype(BF16)
-    pick = chosen.astype(BF16)
-    wide = 512
-
-    @pl.loop(0, width // wide, unroll=True)
-    def _(i):
-        at = pl.ds(pl.multiple_of(i * wide, wide), wide)
-        picked[slots, at] = jnp.dot(
-            pick, x_held[slot, :, at], preferred_element_type=F32
-        ).astype(BF16)
-        top_rows = jnp.dot(pick, t_held[slot, :, at], preferred_element_type=F32)
-        top[:, at] = top_rows
-        slot_grad[slots, at] = (gate * top_rows).astype(BF16)
-
-    hidden = active.shape[1]
-    narrow = 256
-
-    @pl.loop(0, hidden // narrow, unroll=True)
+        if s + 1 < count:
+            for copy in token_copies(s + 1):
+                copy.start()
+        at_slots = slice(s * CAP, (s + 1) * CAP)
+        chosen = (
+            lax.broadcasted_iota(jnp.int32, (CAP, tokens), 0) == rank_row_ref[s]
+        ).astype(F32)
+        spread[s] = (
+            (lax.broadcasted_iota(jnp.int32, (tokens, CAP), 1) == rank_col_ref[s])
+            .astype(F32)
+            .astype(BF16)
+        )
+        expert_row = lax.broadcasted_iota(jnp.int32, (router_ref.shape[0], tokens), 0)
+        logits = jnp.where(
+            expert_row < EXPERTS, dot_nt(router_ref[...], x_held[s % 2]), MASKED_SCORE
+        )
+        exponent = jnp.exp(logits - jnp.max(logits, axis=0, keepdims=True))
+        probs = exponent / jnp.sum(exponent, axis=0, keepdims=True)
+        gate_row = jnp.sum(
+            jnp.where(expert_row == place_ref[4], probs, 0.0), axis=0, keepdims=True
+        )
+        gate = jnp.sum(chosen * gate_row, axis=1, keepdims=True)
+        gates[at_slots, :] = gate
+        pick = chosen.astype(BF16)
+
+        @pl.loop(0, width // wide)
+        def _(i, s=s, pick=pick, gate=gate, at_slots=at_slots):
+            at = pl.ds(pl.multiple_of(i * wide, wide), wide)
+            picked[at_slots, at] = jnp.dot(
+                pick, x_held[s % 2, :, at], preferred_element_type=F32
+            ).astype(BF16)
+            top_rows = jnp.dot(pick, t_held[s % 2, :, at], preferred_element_type=F32)
+            top[at_slots, at] = top_rows.astype(BF16)
+            slot_grad[at_slots, at] = (gate * top_rows).astype(BF16)
+
+    for copy in weight_copies:
+        copy.wait()
+
+    @pl.loop(0, hidden // narrow)
     def _(i):
         at = pl.ds(pl.multiple_of(i * narrow, narrow), narrow)
         up_at = pl.ds(pl.multiple_of(hidden + i * narrow, narrow), narrow)
-        rows = picked[slots, :]
+        rows = picked[own_slots, :]
         gate_part = jnp.dot(rows, in_w[:, at], preferred_element_type=F32)
         up_part = jnp.dot(rows, in_w[:, up_at], preferred_element_type=F32)
-        act_grad = dot_nt(slot_grad[slots, :], down_w[at, :])
+        act_grad = dot_nt(slot_grad[own_slots, :], down_w[at, :])
         sigmoid = jax.nn.sigmoid(gate_part)
         silu = gate_part * sigmoid
-        active[slots, at] = (silu * up_part).astype(BF16)
-        joined_grad[slots, at] = (
+        active[own_slots, at] = (silu * up_part).astype(BF16)
+        joined_grad[own_slots, at] = (
             act_grad * up_part * sigmoid * (1.0 + gate_part * (1.0 - sigmoid))
         ).astype(BF16)
-        joined_grad[slots, up_at] = (act_grad * silu).astype(BF16)
+        joined_grad[own_slots, up_at] = (act_grad * silu).astype(BF16)
+
+    for copy in leaving:
+        copy.start()
 
     def results(i, total):
         at = pl.ds(pl.multiple_of(i * wide, wide), wide)
-        result = jnp.dot(active[slots, :], down_w[:, at], preferred_element_type=F32)
-        mix = jnp.dot(spread, (gate * result).astype(BF16), preferred_element_type=F32)
-        back = dot_nt(joined_grad[slots, :], in_w[at, :])
-        ffn = jnp.dot(spread, back.astype(BF16), preferred_element_type=F32)
-
-        def put(mix_ref, ffn_ref, mix_before, ffn_before):
-            if before is None:
-                mix_ref[0, :, at] = mix.astype(BF16)
-                ffn_ref[0, :, at] = ffn.astype(BF16)
-            else:
-                mix_ref[0, :, at] = (mix + mix_before[0, :, at].astype(F32)).astype(BF16)
-                ffn_ref[0, :, at] = (ffn + ffn_before[0, :, at].astype(F32)).astype(BF16)
-
-        earlier = before or [None] * 4
-        pl.when(source < 2)(lambda: put(mix_keep, ffn_keep, earlier[0], earlier[2]))
-        pl.when(source >= 2)(lambda: put(mix_send, ffn_send, earlier[1], earlier[3]))
-        return total + jnp.sum(result * top[:, at], axis=1, keepdims=True)
-
-    gate_grad = lax.fori_loop(
-        0, width // wide, results, jnp.zeros((CAP, 1), F32), unroll=True
-    )
-    gate_grad_ref[0] = jnp.sum(chosen * gate_grad, axis=0, keepdims=True)
-
-    @pl.when(source == SOURCES - 1)
-    def _():
-        @pl.loop(0, in_g.shape[0] // 256)
+        result = jnp.dot(active[own_slots, :], down_w[:, at], preferred_element_type=F32)
+        mix = (gates[...] * result).astype(BF16)
+        back = dot_nt(joined_grad[own_slots, :], in_w[at, :]).astype(BF16)
+        for s in range(count):
+            at_slots = slice(s * CAP, (s + 1) * CAP)
+            for rows, out in ((mix, mix_refs[s]), (back, ffn_refs[s])):
+                out[:, at] = jnp.dot(
+                    spread[s], rows[at_slots], preferred_element_type=F32
+                ).astype(BF16)
+        return total + jnp.sum(result * top[:, at].astype(F32), axis=1, keepdims=True)
+
+    gate_grad = lax.fori_loop(0, width // wide, results, jnp.zeros((slots, 1), F32))
+    for s in range(count):
+        chosen = lax.broadcasted_iota(jnp.int32, (CAP, tokens), 0) == rank_row_ref[s]
+        gate_grad_ref[s] = jnp.sum(
+            jnp.where(chosen, gate_grad[s * CAP : (s + 1) * CAP], 0.0), axis=0, keepdims=True
+        )
+    for copy in arriving + leaving:
+        copy.wait()
+
+    if grads_too:
+        down_w[...] = dot_tn(active[...], slot_grad[...]).astype(BF16)
+
+        down_copies = block_copies(True, 1)
+        for copy in down_copies:
+            copy.start()
+
+        @pl.loop(0, width // hidden)
         def _(i):
-            at = pl.ds(pl.multiple_of(i * 256, 256), 256)
-            in_g[at, :] = dot_tn(picked[:, at], joined_grad[...]).astype(BF16)
-
-        @pl.loop(0, down_g.shape[0] // 256)
-        def _(i):
-            at = pl.ds(pl.multiple_of(i * 256, 256), 256)
-            down_g[at, :] = dot_tn(active[:, at], slot_grad[...]).astype(BF16)
-
-        copies = block_copies(True)
-        for copy in copies:
+            at = pl.ds(pl.multiple_of(i * hidden, hidden), hidden)
+            in_w[at, :] = dot_tn(picked[:, at], joined_grad[...]).astype(BF16)
+
+        in_copies = block_copies(True, 0)
+        for copy in in_copies:
             copy.start()
-        for copy in copies:
+        for copy in down_copies + in_copies:
             copy.wait()
 
 
-def expert_pass(where, pieces, x_all, t_all, rank_row, rank_col, router_rows, before):
-    tokens, width = x_all[0].shape
+def expert_pass(where, pieces, x_some, t_some, rank, router_rows, given, gives, grads_too):
+    count = len(x_some)
+    tokens, width = x_some[0].shape
     hidden = F
+    slots = count * CAP
+    held_slots = slots + (given[0].shape[0] if given else 0)
     any_spec = pl.BlockSpec(memory_space=pl.ANY)
-    keep_at = lambda s, *_: (jnp.minimum(s, 1), 0, 0)
-    send_at = lambda s, *_: (jnp.maximum(s - 2, 0), 0, 0)
-    sum_specs = [pl.BlockSpec((1, tokens, width), at) for at in (keep_at, send_at)] * 2
-    before_specs = [
-        pl.BlockSpec((1, tokens, width), at, pipeline_mode=pl.Buffered(1))
-        for at in (keep_at, send_at)
-    ] * 2
-    row_spec = pl.BlockSpec((1, 1, tokens), lambda s, *_: (s, 0, 0))
-    col_spec = pl.BlockSpec((1, tokens, 1), lambda s, *_: (s, 0, 0))
-    router_spec = pl.BlockSpec(router_rows.shape, lambda s, *_: (0, 0))
-    piece_shape = jax.ShapeDtypeStruct(pieces[0].shape, BF16)
-    sum_shape = jax.ShapeDtypeStruct((2, tokens, width), BF16)
-    slots = SOURCES * CAP
+    vmem_spec = pl.BlockSpec(memory_space=pltpu.VMEM)
+    token_shape = jax.ShapeDtypeStruct((tokens, width), BF16)
+    kept_widths = (width, 2 * hidden, hidden, width)
     flops = 2 * slots * width * hidden * 9 + 8 * slots * tokens * width
     outs = pl.pallas_call(
-        functools.partial(expert_kernel, before is not None),
+        functools.partial(expert_kernel, count, bool(given), gives, grads_too),
         grid_spec=pltpu.PrefetchScalarGridSpec(
             num_scalar_prefetch=1,
-            grid=(SOURCES,),
-            in_specs=[any_spec] * (len(pieces) + 2 * SOURCES)
-            + [row_spec, col_spec, router_spec]
-            + ([] if before is None else before_specs),
-            out_specs=sum_specs + [row_spec] + [any_spec] * len(pieces),
+            grid=(1,),
+            in_specs=[any_spec] * (len(pieces) + 2 * count)
+            + [vmem_spec] * 3
+            + [any_spec] * len(given),
+            out_specs=[vmem_spec] * (2 * count + 1)
+            + [any_spec] * (4 * gives + 4 * grads_too),
             scratch_shapes=[
                 pltpu.VMEM((width, 2 * hidden), BF16),
                 pltpu.VMEM((hidden, width), BF16),
+                pltpu.VMEM((held_slots, width), BF16),
+                pltpu.VMEM((held_slots, 2 * hidden), BF16),
+                pltpu.VMEM((held_slots, hidden), BF16),
+                pltpu.VMEM((held_slots, width), BF16),
                 pltpu.VMEM((slots, width), BF16),
-                pltpu.VMEM((slots, 2 * hidden), BF16),
-                pltpu.VMEM((slots, hidden), BF16),
-                pltpu.VMEM((slots, width), BF16),
-                pltpu.VMEM((CAP, width), F32),
+                pltpu.VMEM((count, tokens, CAP), BF16),
+                pltpu.VMEM((slots, 1), F32),
                 pltpu.VMEM((2, tokens, width), BF16),
                 pltpu.VMEM((2, tokens, width), BF16),
-                pltpu.VMEM((width, 2 * hidden), BF16),
-                pltpu.VMEM((hidden, width), BF16),
-                pltpu.SemaphoreType.DMA((8 * Z_STEPS,)),
+                pltpu.SemaphoreType.DMA((2, 4 * Z_STEPS)),
                 pltpu.SemaphoreType.DMA((2, 2)),
+                pltpu.SemaphoreType.DMA((4,)),
             ],
         ),
-        out_shape=[sum_shape] * 4
-        + [jax.ShapeDtypeStruct((SOURCES, 1, tokens), F32)]
-        + [piece_shape] * len(pieces),
+        out_shape=[token_shape] * (2 * count)
+        + [jax.ShapeDtypeStruct((count, 1, tokens), F32)]
+        + [jax.ShapeDtypeStruct((slots, w), BF16) for w in kept_widths if gives]
+        + [jax.ShapeDtypeStruct(p.shape, BF16) for p in pieces if grads_too],
         compiler_params=pltpu.CompilerParams(vmem_limit_bytes=60 * MIB),
-        cost_estimate=pl.CostEstimate(
-            flops=2 * flops, bytes_accessed=48 * MIB, transcendentals=slots * hidden
+        cost_estimate=cost(
+            8 * flops, 96 * MIB, slots * hidden
         ),
         name="expert",
-    )(where, *pieces, *x_all, *t_all, rank_row, rank_col, router_rows, *(before or ()))
-    return outs[:4], outs[4], outs[5:]
+    )(where, *pieces, *x_some, *t_some, *rank, router_rows, *given)
+    rest = list(outs[2 * count + 1 :])
+    kept = [rest.pop(0) for _ in range(4 * gives)]
+    return outs[:count], outs[count : 2 * count], outs[2 * count], kept, rest
 
 
 def expert_pairs(expert_in, expert_down):
@@ -869,26 +880,23 @@
     return by_index(core, take_index(core, low, 1), swap(take_index(1 - core, low, 1), "core"))
 
 
-def expert_chunk(pair, number, in_rows):
+def expert_halves(pair, number, in_rows):
     x = lax.axis_index("x")
     pair = pair[:, :, number]
-    in_part = pair[:, :, :in_rows]
-    down_part = pair[:, :, in_rows:]
     width = pair.shape[-1]
     both = jnp.concatenate(
         [
-            jnp.swapaxes(in_part, 0, 1).reshape(2, -1, width),
-            jnp.swapaxes(down_part, 0, 1).reshape(2, -1, width),
+            jnp.swapaxes(part, 0, 1).reshape(2, -1, width)
+            for part in (pair[:, :, :in_rows], pair[:, :, in_rows:])
         ],
         axis=1,
     )
-    return by_index(x, take_index(x, both, 0), swap(take_index(1 - x, both, 0), "x"))
-
-
-def gather_expert(chunk):
-    if lax.axis_size("z") == Z_STEPS:
-        whole = lax.all_gather(chunk, "z")
-        return whole, swap(whole, "y")
+    return take_index(x, both, 0), take_index(1 - x, both, 0)
+
+
+def gather_expert_whole(pair, number, in_rows):
+    own, sent = expert_halves(pair, number, in_rows)
+    chunk = by_index(lax.axis_index("x"), own, swap(sent, "x"))
     whole = lax.all_gather(chunk, ("z", "y"))
     rows = chunk.shape[1] * 2 // 3
     width = chunk.shape[2]
@@ -896,13 +904,14 @@
         jnp.moveaxis(part, 0, 1).reshape(2, Z_STEPS, 2, -1, width)
         for part in (whole[:, :, :rows], whole[:, :, rows:])
     ]
-    both = jnp.transpose(jnp.concatenate(parts, axis=3), (2, 1, 0, 3, 4))
-    return both[0], both[1]
-
-
-def scatter_expert_whole(kept, arrived):
+    both = jnp.concatenate(parts, axis=3)
+    return [both[x, :, y] for y in range(2) for x in range(2)]
+
+
+def scatter_expert_whole(grads):
     spots = lax.axis_size("z") * 2
-    both = jnp.transpose(jnp.stack([kept, arrived]), (2, 1, 0, 3, 4))
+    both = jnp.stack(grads).reshape((2, 2) + grads[0].shape)
+    both = jnp.transpose(both, (1, 2, 0, 3, 4))
     width = both.shape[-1]
     in_rows = both.shape[3] * 2 // 3
     parts = [
@@ -910,30 +919,25 @@
         for part in (both[:, :, :, :in_rows], both[:, :, :, in_rows:])
     ]
     both = jnp.moveaxis(jnp.concatenate(parts, axis=2), 1, 0)
-    return lax.psum_scatter(both, ("z", "y"), scatter_dimension=0).astype(F32)
-
-
-def cross_chunk(chunk):
+    total = lax.psum_scatter(both, ("z", "y"), scatter_dimension=0)
     x = lax.axis_index("x")
-    return take_index(x, chunk, 0), swap(take_index(1 - x, chunk, 0).astype(BF16), "x")
-
-
-def scatter_chunks(pairs, in_rows, down_rows):
+    return take_index(x, total, 0), take_index(1 - x, total, 0)
+
+
+def finish_expert(sums, in_rows):
     x, core = lax.axis_index("x"), lax.axis_index("core")
-    width = pairs[0][0].shape[-1]
-    own, crossed = (jnp.stack([p[i].astype(F32) for p in pairs]) for i in range(2))
-    both = by_index(x, own, crossed)
+    width = sums[0].shape[-1]
+    both = by_index(x, sums[0], swap(sums[1], "x"))
     split = jnp.concatenate(
         [
-            both[:, :, : 2 * in_rows].reshape(2, OWN_EXPERTS, 2, in_rows, width),
-            both[:, :, 2 * in_rows :].reshape(2, OWN_EXPERTS, 2, down_rows, width),
+            both[:, : 2 * in_rows].reshape(2, 2, in_rows, width),
+            both[:, 2 * in_rows :].reshape(2, 2, -1, width),
         ],
-        axis=3,
-    )
-    other = swap(take_index(1 - core, split, 2).astype(BF16), "core").astype(F32)
-    both = by_index(core, take_index(core, split, 2), other)
-    both = jnp.swapaxes(both, 0, 1).reshape(EXPERTS, in_rows + down_rows, width)
-    return both[:, :in_rows], both[:, in_rows:]
+        axis=2,
+    )
+    other = swap(take_index(1 - core, split, 1), "core")
+    both = jnp.swapaxes(by_index(core, take_index(core, split, 1), other), 0, 1).astype(F32)
+    return both[:, :, :in_rows], both[:, :, in_rows:]
 
 
 def shards(
@@ -987,36 +991,45 @@
     attention_edges = (0, half_width, qkv_width + LANES, attention_own.shape[1])
 
     segments = segment_ids[0]
-    seg_prev = swap(segments, "x")
-    routes = route_ids[0].T
-    routes_x = swap(routes, "x")
-    routes_core = swap(jnp.stack([routes, routes_x]), "core")
-    routes_all = jnp.stack([routes, routes_x, routes_core[0], routes_core[1]])
-    top_x = swap(top, "x")
+    named = jnp.concatenate([route_ids[0].T, segments[None]])
+    named_x = swap(named, "x")
+    named_core = swap(jnp.stack([named, named_x]), "core")
+    routes_all = jnp.stack([part[:TOPK] for part in (named, named_x, *named_core)])
+    seg_prev = named_x[TOPK]
+    (top_sent,) = hold((top,), named_x) if staged else (top,)
+    top_x = swap(top_sent, "x")
 
     pair = expert_pairs(expert_in, expert_down)
+    gather_z = lambda half: lax.all_gather(half, "z")
     if staged:
         attention_z = [rotate(attention_own, -k) for k in range(1, Z_STEPS)]
+        own_one, sent_one = expert_halves(pair, 0, in_rows)
         first_held, second_held, out_held = (
             jnp.stack([part[:, start:end] for part in (attention_own, *attention_z)])
             for start, end in zip(attention_edges, attention_edges[1:])
         )
+        first_held, second_held, own_one, seg_prev, routes_all = hold(
+            (first_held, second_held, own_one, seg_prev, routes_all), sent_one
+        )
+        one_own = gather_z(own_one)
         first_x = swap(first_held, "x")
         second_y = swap(second_held, "y")
-        chunk_one = expert_chunk(pair, 0, in_rows)
-        pieces_one = gather_expert(chunk_one)
+        other_one = swap(sent_one, "x")
         first_held = jnp.stack([first_held, first_x])
         second_held = jnp.stack([second_held, second_y])
+        first_held, other_one, top_x = hold((first_held, other_one, top_x))
         first_y = swap(first_held, "y")
         second_x = swap(second_held, "x")
+        one_other = gather_z(other_one)
         first_held = jnp.stack([first_held, first_y])
         second_held = jnp.stack([second_held, second_x], axis=1)
         qkv_held = jnp.concatenate([first_held, second_held], axis=-1)
         (out_held,) = hold((out_held,), first_y, second_x)
+        qkv_held, one_own = hold((qkv_held, one_own))
         out_x = swap(out_held, "x")
         qkv_core = swap(qkv_held, "core")
+        one_own_y = swap(one_own, "y")
         qkv_pair = (qkv_held, qkv_core)
-        out_held = jnp.stack([out_held, out_x])
     else:
         qkv_pair, out_pair = (
             gather_whole(part)
@@ -1025,9 +1038,7 @@
                 attention_own[:, qkv_width + LANES :],
             )
         )
-        pieces_one, pieces_two = (
-            gather_expert(expert_chunk(pair, i, in_rows)) for i in range(2)
-        )
+        pieces_one, pieces_two = (gather_expert_whole(pair, i, in_rows) for i in range(2))
 
     half_size = HEAD_DIMENSION // 2
     positions = (x_index * local_rows + jnp.arange(local_rows, dtype=jnp.int32)).astype(F32)
@@ -1057,59 +1068,93 @@
     ffn_gain = small_low[:, EXPERTS + 1].astype(F32)
     router_rows = small_low.T[:16]
     if staged:
+        own_two, sent_two = expert_halves(pair, 1, in_rows)
+        kv_prev, out_x, one_own_y, one_other, own_two, sent_two = hold(
+            (kv_prev, out_x, one_own_y, one_other, own_two, sent_two)
+        )
+        out_held = jnp.stack([out_held, out_x])
         out_y = swap(out_held, "y")
-        out_held = jnp.stack([out_held, out_y])
-        (pair,) = hold((pair,), kv_prev)
-        pieces_two = gather_expert(expert_chunk(pair, 1, in_rows))
-        out_core = swap(out_held, "core")
-        out_pair = (out_held, out_core)
+        other_two = swap(sent_two, "x")
+        two_own = gather_z(own_two)
     segs = (segments[:, None], segments[None, :], seg_prev[None, :])
     attended, log_sums = attend(queries, kv_own, kv_prev, *segs, half)
-    top_both = swap(jnp.stack([top, top_x]), "core")
+    top_core, top_both = swap(top, "core"), swap(top_x, "core")
+    if staged:
+        attended, out_y, other_two = hold((attended, out_y, other_two))
+        out_held = jnp.stack([out_held, out_y])
+        out_pair = (out_held, swap(out_held, "core"))
+        one_other_y = swap(one_other, "y")
+        two_other = gather_z(other_two)
     middle, normed_ffn, second_scale, out_low = join(
         where, attended, x_tokens, ffn_gain[None, :], out_pair
     )
 
     ffn_core = swap(normed_ffn, "core")
     ffn_x = swap(normed_ffn, "x")
+    if staged:
+        ffn_x, two_own = hold((ffn_x, two_own))
+        two_own_y = swap(two_own, "y")
     ffn_both = swap(ffn_x, "core")
     x_all = (normed_ffn, ffn_x, ffn_core, ffn_both)
-    t_all = (top, top_x, top_both[0], top_both[1])
+    t_all = (top, top_x, top_core, top_both)
     places = [jnp.concatenate([where, first_expert[None] + i]) for i in range(OWN_EXPERTS)]
-
-    def expert(i, pieces, before):
-        ranks = (rank[i][:, None, :], rank[i][:, :, None])
-        return expert_pass(places[i], pieces, x_all, t_all, *ranks, router_rows, before)
-
-    before, gates_one, grads_one = expert(0, pieces_one, None)
-    sums, gates_two, grads_two = expert(1, pieces_two, before)
-    mix_keep, mix_send, ffn_keep, ffn_send = sums
-
     if staged:
-        back_one = swap(grads_one[1], "y")
-        (ffn_send,) = hold((ffn_send,), back_one)
-        total_one = (grads_one[0].astype(F32) + back_one.astype(F32)).astype(BF16)
-        chunk_sum_one = lax.psum_scatter(total_one, "z", scatter_dimension=0)
-        back_two = swap(grads_two[1], "y")
+        two_other, ffn_both = hold((two_other, ffn_both))
+        x_all = (normed_ffn, ffn_x, ffn_core, ffn_both)
+        pieces_one = (one_own, one_other, one_own_y, one_other_y)
+        pieces_two = (two_own, two_other, two_own_y, swap(two_other, "y"))
+
+    def expert(i, pieces, sources, given, gives, grads_too):
+        some = lambda parts: [parts[s] for s in sources]
+        ranks = (
+            jnp.stack(some(rank[i]))[:, None, :],
+            jnp.stack(some(rank[i]))[:, :, None],
+        )
+        return expert_pass(
+            places[i], pieces, some(x_all), some(t_all), ranks, router_rows, given, gives, grads_too
+        )
+
+    mix_one, ffn_one, gates_one, _, grads_one = expert(
+        0, pieces_one, (0, 1, 2, 3), (), False, True
+    )
+    if staged:
+        back_one = [swap(part, "y") for part in grads_one[2:]]
+        pieces_two = hold(pieces_two, gates_one)
+    mix_far, ffn_far, gates_far, kept_far, _ = expert(1, pieces_two, (1, 3), (), True, False)
+    add = lambda *parts: sum(part.astype(F32) for part in parts)
+    ffn_come = swap(add(ffn_one[3], ffn_far[1]).astype(BF16), "core")
+    ffn_crossed = swap(add(ffn_one[1], ffn_far[0], ffn_come).astype(BF16), "x")
+    if staged:
+        total_one = [add(grads_one[0], back_one[0]).astype(BF16)]
+        kept_far[0], total_one[0] = hold((kept_far[0], total_one[0]), ffn_come)
+        sums_one = [lax.psum_scatter(total_one[0], "z", scatter_dimension=0)]
+    mix_near, ffn_near, gates_near, _, grads_two = expert(
+        1, pieces_two, (0, 2), tuple(kept_far), False, True
+    )
+    gates_two = jnp.stack([gates_near[0], gates_far[0], gates_near[1], gates_far[1]])
+
+    if staged:
+        back_two = [swap(part, "y") for part in grads_two[2:]]
+        total_one.append(add(grads_one[1], back_one[1]).astype(BF16))
+        sums_one.append(lax.psum_scatter(total_one[1], "z", scatter_dimension=0))
     else:
-        chunk_sum_one, chunk_sum_two = (
-            scatter_expert_whole(*grads) for grads in (grads_one, grads_two)
-        )
+        sums_one, sums_two = (scatter_expert_whole(grads) for grads in (grads_one, grads_two))
+    ffn_back, ffn_crossed = hold((ffn_near[1], ffn_crossed))
+    ffn_arrived = swap(add(ffn_one[2], ffn_back).astype(BF16), "core")
     gate_grad = jnp.concatenate([gates_one, gates_two], axis=1)
     spread = lax.dynamic_update_slice_in_dim(
         jnp.zeros((SOURCES, EXPERTS, local_rows), F32), gate_grad, first_expert, axis=1
     )
     spread_core = swap(spread[2:], "core")
-    ffn_other = swap(ffn_send, "core").astype(F32)
     spread_x = swap(spread[1] + spread_core[1], "x")
     prob_grad = (spread[0] + spread_core[0] + spread_x).T
-    ffn_crossed = swap((ffn_keep[1].astype(F32) + ffn_other[1]).astype(BF16), "x")
     if staged:
-        (ffn_crossed,) = hold((ffn_crossed,), total_one)
-    (mix_send,) = hold((mix_send,), ffn_crossed)
-    mix_other = swap(mix_send, "core").astype(F32)
-    mix_crossed = swap((mix_keep[1].astype(F32) + mix_other[1]).astype(BF16), "x")
-    ffn_grad = ffn_keep[0].astype(F32) + ffn_other[0] + ffn_crossed.astype(F32)
+        ffn_crossed, sums_one[0] = hold((ffn_crossed, sums_one[0]), total_one[1])
+    ffn_grad = add(ffn_one[0], ffn_near[0], ffn_arrived, ffn_crossed)
+    (mix_sent,) = hold((mix_far[1],), ffn_crossed)
+    mix_come = swap(add(mix_one[3], mix_sent).astype(BF16), "core")
+    mix_arrived = swap(add(mix_one[2], mix_near[1]).astype(BF16), "core")
+    mix_crossed = swap(add(mix_one[1], mix_far[0], mix_come).astype(BF16), "x")
 
     logits = jnp.dot(normed_ffn, small_low[:, :EXPERTS], preferred_element_type=F32)
     exponent = jnp.exp(logits - jnp.max(logits, axis=-1, keepdims=True))
@@ -1134,24 +1179,28 @@
         axis=1,
     )
     (out_blocks,) = grad_rows(
-        where, attended, (branch_grad,), small_grad, (0, model_width + LANES)
+        where.at[1].set(0),
+        attended, (branch_grad,),
+        small_grad,
+        (0, model_width + LANES),
     )
     if staged:
-        attended_grad, chunk_sum_one = hold(
-            (attended_grad, chunk_sum_one), out_blocks[1], back_two
-        )
-        total_two = (grads_two[0].astype(F32) + back_two.astype(F32)).astype(BF16)
-        out_sum = fold(*out_blocks, "core")
-        out_sent = swap(kept_sent(out_sum, "x")[1].astype(BF16), "x")
+        attended_grad, back_two[0] = hold((attended_grad, back_two[0]), out_blocks[1])
+        total_two = [add(grads_two[0], back_two[0]).astype(BF16)]
+        sums_two = [lax.psum_scatter(total_two[0], "z", scatter_dimension=0)]
+        out_kept, out_sent = kept_sent(fold(*out_blocks, "core"), "y")
+        out_come = swap(out_sent.astype(BF16), "y")
     query_grad, key_own, value_own, key_prev, value_prev = attend_back(
         queries, kv_own, kv_prev, *segs, half, attended_grad, log_sums, cosine, -sine_forward
     )
-    crossed = swap(jnp.concatenate([key_prev, value_prev], axis=1).astype(BF16), "x").astype(F32)
+    crossed = swap(jnp.concatenate([key_prev, value_prev], axis=1).astype(BF16), "x")
     if staged:
-        out_sent, query_grad = hold((out_sent, query_grad), total_two)
-        chunk_sum_two = lax.psum_scatter(total_two, "z", scatter_dimension=0)
-        out_sum = kept_sent(out_sum, "x")[0] + out_sent.astype(F32)
-        out_sum = fold(*kept_sent(out_sum, "y"), "y")
+        crossed, back_two[1], mix_crossed = hold(
+            (crossed, back_two[1], mix_crossed), query_grad
+        )
+        total_two.append(add(grads_two[1], back_two[1]).astype(BF16))
+        sums_two.append(lax.psum_scatter(total_two[1], "z", scatter_dimension=0))
+    crossed = crossed.astype(F32)
     key_grad = (key_own + crossed[:, :key_width]).astype(BF16).astype(F32)
     value_grad = value_own + crossed[:, key_width:]
     key_grad = key_grad.reshape(local_rows, KEY_VALUE_HEADS, HEAD_DIMENSION)
@@ -1161,30 +1210,45 @@
     kv_grad = jnp.concatenate(
         [key_grad.reshape(local_rows, key_width).astype(BF16), value_grad.astype(BF16)], axis=1
     )
-    kv_grad, chunk_sum_one = hold((kv_grad, chunk_sum_one), mix_crossed)
+    if staged:
+        kv_grad, out_come, sums_one[1] = hold((kv_grad, out_come, sums_one[1]))
+        out_kept, out_sent = kept_sent(out_kept + out_come.astype(F32), "x")
+        out_come = swap(out_sent.astype(BF16), "x")
     qkv_blocks = grad_rows(
-        where, normed, (query_grad, kv_grad), None, (0, half_width, 2 * half_width)
-    )
-    out_rows = fold_z(out_sum) if staged else scatter_whole(*out_blocks)
+        where.at[1].set(0), normed, (query_grad, kv_grad), None, (0, half_width, 2 * half_width)
+    )
     if staged:
-        pair_one = cross_chunk(chunk_sum_one)
+        (out_come,) = hold((out_come,), qkv_blocks[0][1])
         first = fold(*qkv_blocks[0], "core")
         second = fold(*qkv_blocks[1], "core")
         first_kept, first_sent = kept_sent(first, "y")
         second_kept, second_sent = kept_sent(second, "x")
         first_come = swap(first_sent.astype(BF16), "y")
         second_come = swap(second_sent.astype(BF16), "x")
-        (chunk_sum_two,) = hold((chunk_sum_two,), first_come, second_come)
-        first = fold(*kept_sent(first_kept + first_come.astype(F32), "x"), "x")
-        second = fold(*kept_sent(second_kept + second_come.astype(F32), "y"), "y")
-        qkv_sum = jnp.concatenate([fold_z(first), fold_z(second)], axis=1)
+        first_kept, first_sent = kept_sent(first_kept + first_come.astype(F32), "x")
+        second_kept, second_sent = kept_sent(second_kept + second_come.astype(F32), "y")
+        *sums_one, sums_two[0], out_come = hold(
+            (*sums_one, sums_two[0], out_come), first_come, second_come, total_two[1]
+        )
+        out_total = (out_kept + out_come.astype(F32)).astype(BF16)
+        first_come = swap(first_sent.astype(BF16), "x")
+        second_come = swap(second_sent.astype(BF16), "y")
+        expert_sums = [finish_expert(sums_one, in_rows)]
+        sums_two = hold(sums_two, first_come, second_come)
+        expert_sums.append(finish_expert(sums_two, in_rows))
+        first = first_kept + first_come.astype(F32)
+        second = second_kept + second_come.astype(F32)
+        rows_total = jnp.concatenate([first.astype(BF16), second.astype(BF16), out_total], axis=-1)
+        rows_sum = lax.psum_scatter(rows_total, "z", scatter_dimension=0).astype(F32)
+        qkv_sum, out_rows = rows_sum[:, :qkv_width], rows_sum[:, qkv_width:]
     else:
-        pair_one = cross_chunk(chunk_sum_one)
+        expert_sums = [finish_expert(sums, in_rows) for sums in (sums_one, sums_two)]
+        out_rows = scatter_whole(*out_blocks)
         qkv_sum = jnp.concatenate([scatter_whole(*blocks) for blocks in qkv_blocks], axis=1)
-    in_sum, down_sum = scatter_chunks(
-        [pair_one, cross_chunk(chunk_sum_two)], in_rows, down_rows
-    )
-    mixture = mix_keep[0].astype(F32) + mix_other[0] + mix_crossed.astype(F32)
+    in_sum, down_sum = (jnp.stack(parts, axis=2) for parts in zip(*expert_sums))
+    in_sum = in_sum.reshape(expert_in.shape)
+    down_sum = down_sum.reshape(expert_down.shape)
+    mixture = add(mix_one[0], mix_near[0], mix_arrived, mix_crossed)
     output = (middle + mixture).astype(BF16)
     mixed_grad = jnp.concatenate([query_grad, kv_grad], axis=1)
     inputs = x_tokens.astype(F32)

time: 831 us -> 763 us (0.918)
  waiting for transfers between devices: 320 us -> 218 us
  local copies, waits for them, and re-layouts: 71.7 us -> 96.2 us
  other arithmetic: 93.4 us -> 117 us
  starting transfers between devices: 93.8 us -> 74.9 us
    ppermute x46 -> x53, waiting for transfers between devices: 274 us -> 164 us  [swap(): return lax.ppermute(value, axis, [(0, 1), (1, 0)])]
    ppermute x15 -> x6, waiting for transfers between devices: 46.6 us -> 7.7 us  [rotate(): lax.ppermute(value, 'z', [(i, (i + step) % size) for i in range(size)])]
    all_gather x2 -> x4, waiting for transfers between devices: 0.01 us -> 35.4 us  [shards(): gather_z = lambda half: lax.all_gather(half, 'z')]
    unnamed x183 -> x282, local copies, waits for them, and re-layouts: 24.2 us -> 47.4 us
    convert_element_type x8 -> x17, other arithmetic: 16.6 us -> 36.8 us  [the longest x1 4.13 us: shards(): ffn_crossed = swap(add(ffn_one[1], ffn_far[0], ffn_come).astype(BF16), 'x')]
    ppermute x15 -> x6, starting transfers between devices: 20.7 us -> 8.26 us  [rotate(): lax.ppermute(value, 'z', [(i, (i + step) % size) for i in range(size)])]
    reduce_scatter x2 -> x5, waiting for transfers between devices: 0.01 us -> 11.3 us  [the longest x1 11.3 us: shards(): lax.psum_scatter(rows_total, 'z', scatter_dimension=0).astype(F32)]
    another operation x10 -> x5, other arithmetic: 9.82 us -> 0.67 us  [the longest x1 0.61 us: shards(): jnp.stack([part[:TOPK] for part in (named, named_x, *named_core)])]
  transfers between devices with their start and end apart: 65 -> 68, of which waited for: 29 -> 27; matrix products, arithmetic and copies ran while one was open for 16% -> 21% of each run, Pallas kernels for 24% -> 27%
where the time goes in v2:
time: 763 us; the launch traced here: 751 us
  waiting for transfers between devices  218 us (29%)
  Pallas kernels  199 us (26%)
  other arithmetic  117 us (15%)
  local copies, waits for them, and re-layouts  96.2 us (13%)
  starting transfers between devices  74.9 us (10%)
  matrix products  23.5 us (3%)
  between operations  21.5 us (3%)
    ppermute x53, waiting for transfers between devices, swap(): return lax.ppermute(value, axis, [(0, 1), (1, 0)])  164 us
    pallas_call x3, Pallas kernels, expert_pass(): pl.pallas_call(functools.partial(expert_kernel, count, bool(given), gives...  127 us
    ppermute x53, starting transfers between devices, swap(): return lax.ppermute(value, axis, [(0, 1), (1, 0)])  65.3 us
    unnamed x282, local copies, waits for them, and re-layouts  47.4 us
    all_gather x4, waiting for transfers between devices, shards(): gather_z = lambda half: lax.all_gather(half, 'z')  35.4 us
    pallas_call x2, Pallas kernels, grad_rows(): pl.pallas_call(functools.partial(grad_rows_kernel, len(bs), extra is not...  17.2 us
    pallas_call x1, Pallas kernels, attend_back(): pl.pallas_call(attend_back_kernel, grid_spec=pltpu.PrefetchScalarGridSpec...  16.6 us
  transfers between devices with their start and end apart: 68, of which 27 were waited for; matrix products, arithmetic and copies ran while one was open for 21% of the time, Pallas kernels for 27%

profile of v2, /device:TPU:1, one launch (start us, length us, event | category | flops | bytes accessed | tf_op | source)
XLA Modules:
  0.0 750.8 jit_solution(6642017292786305633)
XLA Ops:
  33.3 7.7 %collective-permute-done.1 = bf16[48,3712]{1,0:T(8,128)(2,1)} collective-permute-done((bf16[48,3712]{1,0:T(8,128)(2,1)}, bf16[48,3712]{1,0:T(8,128)(2,1)}, u32[]{:S(2)}, u32[]{:S(2)}) %collective-permute-start.1) | collective-permute-done | bytes 356384 | tf_op jit(solution)/shard_map/ppermute | solution.py:120
  53.9 8.7 %collective-permute-done.10 = bf16[4,48,1152]{2,1,0:T(8,128)(2,1)S(1)} collective-permute-done((bf16[4,48,1152]{2,1,0:T(8,128)(2,1)}, bf16[4,48,1152]{2,1,0:T(8,128)(2,1)S(1)}, u32[]{:S(2)}, u32[]{:S(2)}) %collective-permute-start.10) | collective-permute-done | bytes 442400 | tf_op jit(solution)/shard_map/ppermute | solution.py:115
  65.9 9.3 %collective-permute-done.6 = bf16[4,48,1024]{2,1,0:T(8,128)(2,1)S(1)} collective-permute-done((bf16[4,48,1024]{2,1,0:T(8,128)(2,1)}, bf16[4,48,1024]{2,1,0:T(8,128)(2,1)S(1)}, u32[]{:S(2)}, u32[]{:S(2)}) %collective-permute-start.6) | collective-permute-done | bytes 393248 | tf_op jit(solution)/shard_map/ppermute | solution.py:115
  76.2 8.5 %collective-permute-done.7.refs_1_ = bf16[144,1536]{1,0:T(8,128)(2,1)S(1)} collective-permute-done((bf16[144,1536]{1,0:T(8,128)(2,1)S(1)}, bf16[144,1536]{1,0:T(8,128)(2,1)S(1)}, u32[]{:S(2)}, u32[]{:S(2)}) %collective-permute-start.7) | collective-permute-done | bytes 442400 | tf_op jit(solution)/shard_map/ppermute | solution.py:115
  86.7 16.9 %collective-permute-done.11.refs_2_ = bf16[2,4,48,1152]{3,2,1,0:T(8,128)(2,1)S(1)} collective-permute-done((bf16[2,4,48,1152]{3,2,1,0:T(8,128)(2,1)S(1)}, bf16[2,4,48,1152]{3,2,1,0:T(8,128)(2,1)S(1)}, u32[]{:S(2)}, u32[]{:S(2)}) %collective-permute-start.11) | collective-permute-done | bytes 884768 | tf_op jit(solution)/shard_map/ppermute | solution.py:115
  124.1 12.6 %project.1 = (bf16[512,1536]{1,0:T(8,128)(2,1)S(1)}, bf16[512,512]{1,0:T(8,128)(2,1)}, bf16[512,1536]{1,0:T(8,128)(2,1)S(1)}, bf16[1536,2048]{1,0:T(8,128)(2,1)}, bf16[1536,128]{1,0:T(8,128)(2,1)S(1)}) custom-call(s32[4]{0:T(128)S(1)} %pad_add_fusion.6.place_ref, bf16[512,1536]{1,0:T(8,128)(2,1)S(1)} %bitcast.252, bf16[2,2,4,48,2176]{4,3,2,1,0:T(8,128)(2,1)S(1)} %copy-done, ...), custom_call_target="tpu_custom_call" | custom-call | flops 2415919104 | bytes 5242880 | tf_op jit(solution)/shard_map/project/pallas_call | solution.py:371
  142.1 8.7 %all-gather.11.cloned.1.call-done = bf16[576,1536]{1,0:T(8,128)(2,1)} async-done(((bf16[144,1536]{1,0:T(8,128)(2,1)}), bf16[576,1536]{1,0:T(8,128)(2,1)}) %all-gather.11.cloned.1.call-update) | async-done | bytes 1769488 | tf_op jit(solution)/shard_map/all_gather | solution.py:1003
  150.8 5.2 collective-permute-done.15.refs_2_
  157.8 2.8 fusion.82
  162.3 14.7 %attend.1 = (bf16[512,1536]{1,0:T(8,128)(2,1)S(1)}, f32[12,512,1]{2,1,0:T(8,128)S(1)}) custom-call(s32[1]{0:T(128)} %bitcast.half_ref, bf16[512,1536]{1,0:T(8,128)(2,1)S(1)} %copy-done.15, bf16[512,512]{1,0:T(8,128)(2,1)} %get-tuple-element.147.ko_ref.vo_ref, bf16[512,512]{1,0:T(8,128)(2,1)} %get-tuple-element.147.ko_ref.vo_ref, ...), custom_call_target="tpu_custom_call" | custom-call | flops 805306368 | bytes 4194304 | tf_op jit(solution)/shard_map/attend/pallas_call | solution.py:533
  179.8 7.8 %collective-permute-done.16.refs_1_ = bf16[2,4,48,1536]{3,2,1,0:T(8,128)(2,1)} collective-permute-done((bf16[2,4,48,1536]{3,2,1,0:T(8,128)(2,1)}, bf16[2,4,48,1536]{3,2,1,0:T(8,128)(2,1)}, u32[]{:S(2)}, u32[]{:S(2)}) %collective-permute-start.16) | collective-permute-done | bytes 1179680 | tf_op jit(solution)/shard_map/ppermute | solution.py:115
  200.2 10.9 %join.1 = (f32[512,1536]{1,0:T(8,128)S(1)}, bf16[512,1536]{1,0:T(8,128)(2,1)}, f32[512,1]{1,0:T(8,128)S(1)}, bf16[1536,1536]{1,0:T(8,128)(2,1)}) custom-call(s32[4]{0:T(128)S(1)} %pad_add_fusion.6.place_ref, bf16[512,1536]{1,0:T(8,128)(2,1)S(1)} %copy-done.12, bf16[512,1536]{1,0:T(8,128)(2,1)S(1)} %bitcast.253, f32[1,1536]{1,0:T(1,128)S(1)} %reshape.221.gain_ref, ...), custom_call_target="tpu_custom_call" | custom-call | flops 1207959552 | bytes 4194304 | tf_op jit(solution)/shard_map/join/pallas_call | solution.py:451
  213.8 16.2 %all-gather.13.cloned.1.call-done = bf16[576,1536]{1,0:T(8,128)(2,1)} async-done(((bf16[144,1536]{1,0:T(8,128)(2,1)}), bf16[576,1536]{1,0:T(8,128)(2,1)}) %all-gather.13.cloned.1.call-update) | async-done | bytes 1769488 | tf_op jit(solution)/shard_map/all_gather | solution.py:1003
  230.1 17.7 %collective-permute-done.20.refs_0_ = bf16[512,1536]{1,0:T(8,128)(2,1)} collective-permute-done((bf16[512,1536]{1,0:T(8,128)(2,1)}, bf16[512,1536]{1,0:T(8,128)(2,1)}, u32[]{:S(2)}, u32[]{:S(2)}) %collective-permute-start.20) | collective-permute-done | bytes 1572896 | tf_op jit(solution)/shard_map/ppermute | solution.py:115
  260.9 10.4 %all-gather.15.cloned.1.call-done = bf16[576,1536]{1,0:T(8,128)(2,1)} async-done(((bf16[144,1536]{1,0:T(8,128)(2,1)}), bf16[576,1536]{1,0:T(8,128)(2,1)}) %all-gather.15.cloned.1.call-update) | async-done | bytes 1769488 | tf_op jit(solution)/shard_map/all_gather | solution.py:1003
  272.5 59.2 %expert.3 = (bf16[512,1536]{1,0:T(8,128)(2,1)}, bf16[512,1536]{1,0:T(8,128)(2,1)}, bf16[512,1536]{1,0:T(8,128)(2,1)}, bf16[512,1536]{1,0:T(8,128)(2,1)}, bf16[51...) custom-call(s32[5]{0:T(128)} %concatenate.76.place_ref, ...), custom_call_target="tpu_custom_call" | custom-call | flops 70464307200 | bytes 25165824 | tf_op jit(solution)/shard_map/expert/pallas_call | solution.py:834
  332.0 5.5 collective-permute-done.26.refs_3_
  337.5 27.4 %expert.4 = (bf16[512,1536]{1,0:T(8,128)(2,1)}, bf16[512,1536]{1,0:T(8,128)(2,1)}, bf16[512,1536]{1,0:T(8,128)(2,1)}, bf16[512,1536]{1,0:T(8,128)(2,1)}, f32[2,1...) custom-call(s32[5]{0:T(128)} %concatenate.77.place_ref, ...), custom_call_target="tpu_custom_call" | custom-call | flops 35232153600 | bytes 25165824 | tf_op jit(solution)/shard_map/expert/pallas_call | solution.py:834
  365.0 3.4 add_convert_fusion.10
  382.0 3.1 add_convert_fusion.3.refs_1_
  385.4 4.1 add_convert_fusion.8
  389.7 40.7 %expert.5 = (bf16[512,1536]{1,0:T(8,128)(2,1)}, bf16[512,1536]{1,0:T(8,128)(2,1)}, bf16[512,1536]{1,0:T(8,128)(2,1)}, bf16[512,1536]{1,0:T(8,128)(2,1)}, f32[2,1...) custom-call(s32[5]{0:T(128)} %concatenate.77.place_ref, ...), custom_call_target="tpu_custom_call" | custom-call | flops 35232153600 | bytes 25165824 | tf_op jit(solution)/shard_map/expert/pallas_call | solution.py:834
  431.8 3.5 add_convert_fusion.7
  440.8 3.1 add_convert_fusion.2.refs_2_
  447.3 4.1 fusion.72
  452.1 6.2 multiply_reduce_fusion
  462.8 7.1 grad_rows.2
  472.5 3.7 convolution_convert_fusion.refs_0_
  476.2 8.2 %collective-permute-done.35.refs_1_ = bf16[4,144,1536]{2,1,0:T(8,128)(2,1)} collective-permute-done((bf16[4,144,1536]{2,1,0:T(8,128)(2,1)}, bf16[4,144,1536]{2,1,0:T(8,128)(2,1)}, u32[]{:S(2)}, u32[]{:S(2)}) %collective-permute-start.35) | collective-permute-done | bytes 1769504 | tf_op jit(solution)/shard_map/ppermute | solution.py:115
  487.4 16.6 %attend_back.1 = (bf16[512,1536]{1,0:T(8,128)(2,1)S(1)}, f32[512,256]{1,0:T(8,128)S(1)}, f32[512,256]{1,0:T(8,128)S(1)}, f32[512,256]{1,0:T(8,128)S(1)}, f32[512,256]{1,0:T(8,128)S(1)}) custom-call(s32[1]{0:T(128)} %bitcast.half_ref, bf16[512,1536]{1,0:T(8,128)(2,1)} %copy-done.14, bf16[512,512]{1,0:T(8,128)(2,1)} %get-tuple-element.147.ko_ref.vo_ref, ...), custom_call_target="tpu_custom_call" | custom-call | flops 2013265920 | bytes 6291456 | tf_op jit(solution)/shard_map/attend_back/pallas_call | solution.py:613
  506.8 10.2 %collective-permute-start.36 = (bf16[512,512]{1,0:T(8,128)(2,1)}, bf16[512,512]{1,0:T(8,128)(2,1)}, u32[]{:S(2)}, u32[]{:S(2)}) collective-permute-start(bf16[512,512]{1,0:T(8,128)(2,1)} %pad_maximum_fusion.9), channel_id=1, source_target_pairs={{0,16},{16,0},{1,17},{17,1},{2,18},{18,2},{3,19},{19,3},{4,20},{20... | collective-permute-start | bytes 1572872 | tf_op jit(solution)/shard_map/ppermute | solution.py:115
  517.0 3.1 add_convert_fusion.1
  520.1 3.1 add_convert_fusion.5
  532.8 28.2 %collective-permute-done.39.refs_2_ = bf16[512,1536]{1,0:T(8,128)(2,1)} collective-permute-done((bf16[512,1536]{1,0:T(8,128)(2,1)S(1)}, bf16[512,1536]{1,0:T(8,128)(2,1)}, u32[]{:S(2)}, u32[]{:S(2)}) %collective-permute-start.39) | collective-permute-done | bytes 1572896 | tf_op jit(solution)/shard_map/ppermute | solution.py:115
  570.9 10.1 %grad_rows.3 = (bf16[2,2,4,48,1024]{4,3,2,1,0:T(8,128)(2,1)S(1)}, bf16[2,2,4,48,1024]{4,3,2,1,0:T(8,128)(2,1)S(1)}, bf16[2,2,4,48,1024]{4,3,2,1,0:T(8,128)(2,1)S(1)}, bf16[2,2,4,48,1024]{4,3,2,1,0:T(8,128)(2,1)}) custom-call(s32[4]{0:T(128)S(1)} %constant_dynamic-update-slice_fusion.place_ref, bf16[512,1536]{1,0:T(8,128)(2,1)} %copy-done.41, ...), custom_call_target="tpu_custom_call" | custom-call | flops 1610612736 | bytes 3145728 | tf_op jit(solution)/shard_map/grad_rows/pallas_call | solution.py:247
  584.5 2.9 copy.292
  587.4 2.8 collective-permute-start.45
  590.2 3.1 add_convert_fusion.refs_6_
  606.0 4.2 fusion.13
  611.6 16.8 %collective-permute-done.46.refs_5_ = bf16[2,4,48,1024]{3,2,1,0:T(8,128)(2,1)} collective-permute-done((bf16[2,4,48,1024]{3,2,1,0:T(8,128)(2,1)}, bf16[2,4,48,1024]{3,2,1,0:T(8,128)(2,1)}, u32[]{:S(2)}, u32[]{:S(2)}) %collective-permute-start.46) | collective-permute-done | bytes 786464 | tf_op jit(solution)/shard_map/ppermute | solution.py:115
  645.5 8.3 %collective-permute-done.49 = bf16[144,1536]{1,0:T(8,128)(2,1)S(1)} collective-permute-done((bf16[144,1536]{1,0:T(8,128)(2,1)S(1)}, bf16[144,1536]{1,0:T(8,128)(2,1)S(1)}, u32[]{:S(2)}, u32[]{:S(2)}) %collective-permute-start.49) | collective-permute-done | bytes 442400 | tf_op jit(solution)/shard_map/ppermute | solution.py:115
  661.7 8.4 %collective-permute-done.51 = bf16[144,1536]{1,0:T(8,128)(2,1)S(1)} collective-permute-done((bf16[144,1536]{1,0:T(8,128)(2,1)}, bf16[144,1536]{1,0:T(8,128)(2,1)S(1)}, u32[]{:S(2)}, u32[]{:S(2)}) %collective-permute-start.51) | collective-permute-done | bytes 442400 | tf_op jit(solution)/shard_map/ppermute | solution.py:115
  676.9 11.3 %reduce-scatter.12.cloned.1.call-done = bf16[1,48,3712]{2,1,0:T(8,128)(2,1)} async-done(((bf16[4,48,3712]{2,1,0:T(8,128)(2,1)}), bf16[1,48,3712]{2,1,0:T(8,128)(2,1)}) %reduce-scatter.12.cloned.1.call-update) | async-done | bytes 356368 | tf_op jit(solution)/shard_map/reduce_scatter | solution.py:1242
  700.0 6.6 fusion
  711.7 3.8 collective-permute-start.58
  723.4 3.3 copy.303
  731.9 3.9 multiply_subtract_fusion.1
  736.6 6.0 multiply_subtract_fusion
  (593 shorter events, 238.8 us)
Async XLA Ops:
  7.2 101.5 %all-gather.9.cloned.1.call-start = ((), (), s32[]{:S(2)}) async-start(), calls=%async_computation.10 | async-start | bytes 2211840 | tf_op jit(solution)/shard_map/all_gather | solution.py:1003
  12.4 19.1 %collective-permute-start.2 = (bf16[48,3712]{1,0:T(8,128)(2,1)}, bf16[48,3712]{1,0:T(8,128)(2,1)}, u32[]{:S(2)}, u32[]{:S(2)}) collective-permute-start(bf16[48,3712]{1,0:T(8,128)(2,1)} %concatenate.67), channel_id=1, source_target_pairs={{0,4},{4,8},{8,12},{12,0},{1,5},{5,9},{9,13},{13,1},{2,6},{6,10},{... | collective-permute-start | bytes 1069064 | tf_op jit(solution)/shard_map/ppermute | solution.py:120
  14.5 26.4 %collective-permute-start.1 = (bf16[48,3712]{1,0:T(8,128)(2,1)}, bf16[48,3712]{1,0:T(8,128)(2,1)}, u32[]{:S(2)}, u32[]{:S(2)}) collective-permute-start(bf16[48,3712]{1,0:T(8,128)(2,1)} %concatenate.67), channel_id=1, source_target_pairs={{0,8},{4,12},{8,0},{12,4},{1,9},{5,13},{9,1},{13,5},{2,10},{6,14},... | collective-permute-start | bytes 1069064 | tf_op jit(solution)/shard_map/ppermute | solution.py:120
  16.9 25.9 %collective-permute-start = (bf16[48,3712]{1,0:T(8,128)(2,1)}, bf16[48,3712]{1,0:T(8,128)(2,1)}, u32[]{:S(2)}, u32[]{:S(2)}) collective-permute-start(bf16[48,3712]{1,0:T(8,128)(2,1)} %concatenate.67), channel_id=1, source_target_pairs={{0,12},{4,0},{8,4},{12,8},{1,13},{5,1},{9,5},{13,9},{2,14},{6,2},{... | collective-permute-start | bytes 1069064 | tf_op jit(solution)/shard_map/ppermute | solution.py:120
  24.4 21.8 %collective-permute-start.3 = (bf16[2,2,72,1536]{3,2,1,0:T(8,128)(2,1)}, bf16[2,2,72,1536]{3,2,1,0:T(8,128)(2,1)S(1)}, u32[]{:S(2)}, u32[]{:S(2)}) collective-permute-start(bf16[2,2,72,1536]{3,2,1,0:T(8,128)(2,1)} %get-tuple-element.404), channel_id=1, source_target_pairs={{0,1},{1,0},{2,3},{3,2},{4,5},{5,4},{6,7},{7,6},{8,9},{9,8},{10,11... | collective-permute-start | bytes 2654216 | tf_op jit(solution)/shard_map/ppermute | solution.py:115
  30.6 54.1 %collective-permute-start.8 = (bf16[512,1536]{1,0:T(8,128)(2,1)}, bf16[512,1536]{1,0:T(8,128)(2,1)}, u32[]{:S(2)}, u32[]{:S(2)}) collective-permute-start(bf16[512,1536]{1,0:T(8,128)(2,1)} %hold.21), channel_id=1, source_target_pairs={{0,16},{16,0},{1,17},{17,1},{2,18},{18,2},{3,19},{19,3},{4,20},{20... | collective-permute-start | bytes 4718600 | tf_op jit(solution)/shard_map/ppermute | solution.py:115
  51.1 99.7 %all-gather.11.cloned.1.call-start = ((), (), s32[]{:S(2)}) async-start(), calls=%async_computation.11 | async-start | bytes 2211840 | tf_op jit(solution)/shard_map/all_gather | solution.py:1003
  52.5 22.8 %collective-permute-start.6 = (bf16[4,48,1024]{2,1,0:T(8,128)(2,1)}, bf16[4,48,1024]{2,1,0:T(8,128)(2,1)S(1)}, u32[]{:S(2)}, u32[]{:S(2)}) collective-permute-start(bf16[4,48,1024]{2,1,0:T(8,128)(2,1)} %get-tuple-element.141), channel_id=1, source_target_pairs={{0,16},{16,0},{1,17},{17,1},{2,18},{18,2},{3,19},{19,3},{4,20},{20... | collective-permute-start | bytes 1179656 | tf_op jit(solution)/shard_map/ppermute | solution.py:115
  53.7 31.0 %collective-permute-start.7 = (bf16[144,1536]{1,0:T(8,128)(2,1)S(1)}, bf16[144,1536]{1,0:T(8,128)(2,1)S(1)}, u32[]{:S(2)}, u32[]{:S(2)}) collective-permute-start(bf16[144,1536]{1,0:T(8,128)(2,1)S(1)} %copy-done.85), channel_id=1, source_target_pairs={{0,16},{16,0},{1,17},{17,1},{2,18},{18,2},{3,19},{19,3},{4,20},{20... | collective-permute-start | bytes 1327112 | tf_op jit(solution)/shard_map/ppermute | solution.py:115
  64.7 38.8 %collective-permute-start.11 = (bf16[2,4,48,1152]{3,2,1,0:T(8,128)(2,1)S(1)}, bf16[2,4,48,1152]{3,2,1,0:T(8,128)(2,1)S(1)}, u32[]{:S(2)}, u32[]{:S(2)}) collective-permute-start(bf16[2,4,48,1152]{3,2,1,0:T(8,128)(2,1)S(1)} %get-tuple-element.416), channel_id=1, source_target_pairs={{0,16},{16,0},{1,17},{17,1},{2,18},{18,2},{3,19},{19,3},{4,20},{20... | collective-permute-start | bytes 2654216 | tf_op jit(solution)/shard_map/ppermute | solution.py:115
  85.5 18.1 %collective-permute-start.9 = (bf16[2,4,48,1024]{3,2,1,0:T(8,128)(2,1)}, bf16[2,4,48,1024]{3,2,1,0:T(8,128)(2,1)S(1)}, u32[]{:S(2)}, u32[]{:S(2)}) collective-permute-start(bf16[2,4,48,1024]{3,2,1,0:T(8,128)(2,1)} %get-tuple-element.142), channel_id=1, source_target_pairs={{0,2},{2,0},{1,3},{3,1},{4,6},{6,4},{5,7},{7,5},{8,10},{10,8},{9,1... | collective-permute-start | bytes 2359304 | tf_op jit(solution)/shard_map/ppermute | solution.py:115
  113.4 116.6 %all-gather.13.cloned.1.call-start = ((), (), s32[]{:S(2)}) async-start(), calls=%async_computation.12 | async-start | bytes 2211840 | tf_op jit(solution)/shard_map/all_gather | solution.py:1003
  115.3 40.6 %collective-permute-start.15 = (bf16[4,144,1536]{2,1,0:T(8,128)(2,1)}, bf16[4,144,1536]{2,1,0:T(8,128)(2,1)}, u32[]{:S(2)}, u32[]{:S(2)}) collective-permute-start(bf16[4,144,1536]{2,1,0:T(8,128)(2,1)} %get-tuple-element.148.refs_0_), channel_id=1, source_target_pairs={{0,2},{2,0},{1,3},{3,1},{4,6},{6,4},{5,7},{7,5},{8,10},{10,8},{9,1... | collective-permute-start | bytes 5308424 | tf_op jit(solution)/shard_map/ppermute | solution.py:115
  119.4 22.7 %collective-permute-start.14 = (bf16[4,48,1536]{2,1,0:T(8,128)(2,1)}, bf16[4,48,1536]{2,1,0:T(8,128)(2,1)}, u32[]{:S(2)}, u32[]{:S(2)}) collective-permute-start(bf16[4,48,1536]{2,1,0:T(8,128)(2,1)} %hold.24), channel_id=1, source_target_pairs={{0,16},{16,0},{1,17},{17,1},{2,18},{18,2},{3,19},{19,3},{4,20},{20... | collective-permute-start | bytes 1769480 | tf_op jit(solution)/shard_map/ppermute | solution.py:115
  139.7 16.2 %collective-permute-start.13 = (bf16[512,512]{1,0:T(8,128)(2,1)}, bf16[512,512]{1,0:T(8,128)(2,1)S(1)}, u32[]{:S(2)}, u32[]{:S(2)}) collective-permute-start(bf16[512,512]{1,0:T(8,128)(2,1)} %get-tuple-element.147.ko_ref.vo_ref), channel_id=1, source_target_pairs={{0,16},{16,0},{1,17},{17,1},{2,18},{18,2},{3,19},{19,3},{4,20},{20... | collective-permute-start | bytes 1572872 | tf_op jit(solution)/shard_map/ppermute | solution.py:115
  160.6 27.0 %collective-permute-start.16 = (bf16[2,4,48,1536]{3,2,1,0:T(8,128)(2,1)}, bf16[2,4,48,1536]{3,2,1,0:T(8,128)(2,1)}, u32[]{:S(2)}, u32[]{:S(2)}) collective-permute-start(bf16[2,4,48,1536]{3,2,1,0:T(8,128)(2,1)} %get-tuple-element.406), channel_id=1, source_target_pairs={{0,2},{2,0},{1,3},{3,1},{4,6},{6,4},{5,7},{7,5},{8,10},{10,8},{9,1... | collective-permute-start | bytes 3538952 | tf_op jit(solution)/shard_map/ppermute | solution.py:115
  161.8 17.9 %collective-permute-start.17 = (bf16[144,1536]{1,0:T(8,128)(2,1)}, bf16[144,1536]{1,0:T(8,128)(2,1)S(1)}, u32[]{:S(2)}, u32[]{:S(2)}) collective-permute-start(bf16[144,1536]{1,0:T(8,128)(2,1)} %get-tuple-element.154), channel_id=1, source_target_pairs={{0,16},{16,0},{1,17},{17,1},{2,18},{18,2},{3,19},{19,3},{4,20},{20... | collective-permute-start | bytes 1327112 | tf_op jit(solution)/shard_map/ppermute | solution.py:115
  192.7 78.6 %all-gather.15.cloned.1.call-start = ((), (), s32[]{:S(2)}) async-start(), calls=%async_computation.13 | async-start | bytes 2211840 | tf_op jit(solution)/shard_map/all_gather | solution.py:1003
  211.8 35.9 %collective-permute-start.20 = (bf16[512,1536]{1,0:T(8,128)(2,1)}, bf16[512,1536]{1,0:T(8,128)(2,1)}, u32[]{:S(2)}, u32[]{:S(2)}) collective-permute-start(bf16[512,1536]{1,0:T(8,128)(2,1)} %get-tuple-element.161.refs_4_), channel_id=1, source_target_pairs={{0,16},{16,0},{1,17},{17,1},{2,18},{18,2},{3,19},{19,3},{4,20},{20... | collective-permute-start | bytes 4718600 | tf_op jit(solution)/shard_map/ppermute | solution.py:115
  213.1 238.3 %reduce-scatter.6.cloned.1.call-start = ((), (), s32[]{:S(2)}) async-start(), calls=%async_computation.5 | async-start | bytes 2211840 | tf_op jit(solution)/shard_map/reduce_scatter | solution.py:1130
  213.5 59.0 %collective-permute-start.19 = (bf16[4,144,1536]{2,1,0:T(8,128)(2,1)}, bf16[4,144,1536]{2,1,0:T(8,128)(2,1)}, u32[]{:S(2)}, u32[]{:S(2)}) collective-permute-start(bf16[4,144,1536]{2,1,0:T(8,128)(2,1)} %get-tuple-element.159.refs_1_), channel_id=1, source_target_pairs={{0,2},{2,0},{1,3},{3,1},{4,6},{6,4},{5,7},{7,5},{8,10},{10,8},{9,1... | collective-permute-start | bytes 5308424 | tf_op jit(solution)/shard_map/ppermute | solution.py:115
  249.0 22.3 %collective-permute-start.23 = (bf16[512,1536]{1,0:T(8,128)(2,1)}, bf16[512,1536]{1,0:T(8,128)(2,1)}, u32[]{:S(2)}, u32[]{:S(2)}) collective-permute-start(bf16[512,1536]{1,0:T(8,128)(2,1)} %bitcast.262), channel_id=1, source_target_pairs={{0,1},{1,0},{2,3},{3,2},{4,5},{5,4},{6,7},{7,6},{8,9},{9,8},{10,11... | collective-permute-start | bytes 4718600 | tf_op jit(solution)/shard_map/ppermute | solution.py:115
  249.0 23.5 %collective-permute-start.24 = (bf16[512,1536]{1,0:T(8,128)(2,1)}, bf16[512,1536]{1,0:T(8,128)(2,1)}, u32[]{:S(2)}, u32[]{:S(2)}) collective-permute-start(bf16[512,1536]{1,0:T(8,128)(2,1)} %get-tuple-element.166.refs_9_.refs_6_), channel_id=1, source_target_pairs={{0,1},{1,0},{2,3},{3,2},{4,5},{5,4},{6,7},{7,6},{8,9},{9,8},{10,11... | collective-permute-start | bytes 4718600 | tf_op jit(solution)/shard_map/ppermute | solution.py:115
  249.5 23.0 %collective-permute-start.21 = (bf16[512,1536]{1,0:T(8,128)(2,1)}, bf16[512,1536]{1,0:T(8,128)(2,1)}, u32[]{:S(2)}, u32[]{:S(2)}) collective-permute-start(bf16[512,1536]{1,0:T(8,128)(2,1)} %get-tuple-element.161.refs_4_), channel_id=1, source_target_pairs={{0,1},{1,0},{2,3},{3,2},{4,5},{5,4},{6,7},{7,6},{8,9},{9,8},{10,11... | collective-permute-start | bytes 4718600 | tf_op jit(solution)/shard_map/ppermute | solution.py:115
  259.6 72.4 %collective-permute-start.25 = (bf16[4,144,1536]{2,1,0:T(8,128)(2,1)}, bf16[4,144,1536]{2,1,0:T(8,128)(2,1)}, u32[]{:S(2)}, u32[]{:S(2)}) collective-permute-start(bf16[4,144,1536]{2,1,0:T(8,128)(2,1)} %get-tuple-element.169.refs_0_), channel_id=1, source_target_pairs={{0,2},{2,0},{1,3},{3,1},{4,6},{6,4},{5,7},{7,5},{8,10},{10,8},{9,1... | collective-permute-start | bytes 5308424 | tf_op jit(solution)/shard_map/ppermute | solution.py:115
  271.3 66.2 %collective-permute-start.26 = (bf16[4,144,1536]{2,1,0:T(8,128)(2,1)}, bf16[4,144,1536]{2,1,0:T(8,128)(2,1)}, u32[]{:S(2)}, u32[]{:S(2)}) collective-permute-start(bf16[4,144,1536]{2,1,0:T(8,128)(2,1)} %get-tuple-element.170.refs_1_), channel_id=1, source_target_pairs={{0,2},{2,0},{1,3},{3,1},{4,6},{6,4},{5,7},{7,5},{8,10},{10,8},{9,1... | collective-permute-start | bytes 5308424 | tf_op jit(solution)/shard_map/ppermute | solution.py:115
  331.7 50.3 %collective-permute-start.27 = (bf16[4,144,1536]{2,1,0:T(8,128)(2,1)}, bf16[4,144,1536]{2,1,0:T(8,128)(2,1)}, u32[]{:S(2)}, u32[]{:S(2)}) collective-permute-start(bf16[4,144,1536]{2,1,0:T(8,128)(2,1)} %get-tuple-element.178), channel_id=1, source_target_pairs={{0,2},{2,0},{1,3},{3,1},{4,6},{6,4},{5,7},{7,5},{8,10},{10,8},{9,1... | collective-permute-start | bytes 5308424 | tf_op jit(solution)/shard_map/ppermute | solution.py:115
  368.4 16.7 %collective-permute-start.28 = (bf16[512,1536]{1,0:T(8,128)(2,1)}, bf16[512,1536]{1,0:T(8,128)(2,1)}, u32[]{:S(2)}, u32[]{:S(2)}) collective-permute-start(bf16[512,1536]{1,0:T(8,128)(2,1)} %add_convert_fusion.10), channel_id=1, source_target_pairs={{0,1},{1,0},{2,3},{3,2},{4,5},{5,4},{6,7},{7,6},{8,9},{9,8},{10,11... | collective-permute-start | bytes 4718600 | tf_op jit(solution)/shard_map/ppermute | solution.py:115
  380.8 60.0 %collective-permute-start.32 = (bf16[4,144,1536]{2,1,0:T(8,128)(2,1)}, bf16[4,144,1536]{2,1,0:T(8,128)(2,1)}, u32[]{:S(2)}, u32[]{:S(2)}) collective-permute-start(bf16[4,144,1536]{2,1,0:T(8,128)(2,1)} %get-tuple-element.199), channel_id=1, source_target_pairs={{0,2},{2,0},{1,3},{3,1},{4,6},{6,4},{5,7},{7,5},{8,10},{10,8},{9,1... | collective-permute-start | bytes 5308424 | tf_op jit(solution)/shard_map/ppermute | solution.py:115
  385.1 184.7 %reduce-scatter.8.cloned.1.call-start = ((), (), s32[]{:S(2)}) async-start(), calls=%async_computation.6 | async-start | bytes 2211840 | tf_op jit(solution)/shard_map/reduce_scatter | solution.py:1139
  389.5 42.3 %collective-permute-start.30 = (bf16[512,1536]{1,0:T(8,128)(2,1)}, bf16[512,1536]{1,0:T(8,128)(2,1)}, u32[]{:S(2)}, u32[]{:S(2)}) collective-permute-start(bf16[512,1536]{1,0:T(8,128)(2,1)} %add_convert_fusion.8), channel_id=1, source_target_pairs={{0,16},{16,0},{1,17},{17,1},{2,18},{18,2},{3,19},{19,3},{4,20},{20... | collective-permute-start | bytes 4718600 | tf_op jit(solution)/shard_map/ppermute | solution.py:115
  435.4 16.1 %collective-permute-start.31 = (bf16[512,1536]{1,0:T(8,128)(2,1)}, bf16[512,1536]{1,0:T(8,128)(2,1)}, u32[]{:S(2)}, u32[]{:S(2)}) collective-permute-start(bf16[512,1536]{1,0:T(8,128)(2,1)} %add_convert_fusion.7), channel_id=1, source_target_pairs={{0,1},{1,0},{2,3},{3,2},{4,5},{5,4},{6,7},{7,6},{8,9},{9,8},{10,11... | collective-permute-start | bytes 4718600 | tf_op jit(solution)/shard_map/ppermute | solution.py:115
  443.9 192.7 %reduce-scatter.10.cloned.1.call-start = ((), (), s32[]{:S(2)}) async-start(), calls=%async_computation.7 | async-start | bytes 2211840 | tf_op jit(solution)/shard_map/reduce_scatter | solution.py:1190
  444.3 40.1 %collective-permute-start.35 = (bf16[4,144,1536]{2,1,0:T(8,128)(2,1)}, bf16[4,144,1536]{2,1,0:T(8,128)(2,1)}, u32[]{:S(2)}, u32[]{:S(2)}) collective-permute-start(bf16[4,144,1536]{2,1,0:T(8,128)(2,1)} %get-tuple-element.204), channel_id=1, source_target_pairs={{0,2},{2,0},{1,3},{3,1},{4,6},{6,4},{5,7},{7,5},{8,10},{10,8},{9,1... | collective-permute-start | bytes 5308424 | tf_op jit(solution)/shard_map/ppermute | solution.py:115
  444.6 88.2 %collective-permute-start.37 = (bf16[4,144,1536]{2,1,0:T(8,128)(2,1)}, bf16[4,144,1536]{2,1,0:T(8,128)(2,1)}, u32[]{:S(2)}, u32[]{:S(2)}) collective-permute-start(bf16[4,144,1536]{2,1,0:T(8,128)(2,1)} %get-tuple-element.210), channel_id=1, source_target_pairs={{0,2},{2,0},{1,3},{3,1},{4,6},{6,4},{5,7},{7,5},{8,10},{10,8},{9,1... | collective-permute-start | bytes 5308424 | tf_op jit(solution)/shard_map/ppermute | solution.py:115
  469.9 53.8 %collective-permute-start.40 = (bf16[2,2,4,48,1664]{4,3,2,1,0:T(8,128)(2,1)}, bf16[2,2,4,48,1664]{4,3,2,1,0:T(8,128)(2,1)}, u32[]{:S(2)}, u32[]{:S(2)}) collective-permute-start(bf16[2,2,4,48,1664]{4,3,2,1,0:T(8,128)(2,1)} %get-tuple-element.205.refs_2_), channel_id=1, source_target_pairs={{0,1},{1,0},{2,3},{3,2},{4,5},{5,4},{6,7},{7,6},{8,9},{9,8},{10,11... | collective-permute-start | bytes 7667720 | tf_op jit(solution)/shard_map/ppermute | solution.py:115
  472.5 47.7 %collective-permute-start.38 = (bf16[512,1536]{1,0:T(8,128)(2,1)}, bf16[512,1536]{1,0:T(8,128)(2,1)}, u32[]{:S(2)}, u32[]{:S(2)}) collective-permute-start(bf16[512,1536]{1,0:T(8,128)(2,1)} %add_convert_fusion.6), channel_id=1, source_target_pairs={{0,1},{1,0},{2,3},{3,2},{4,5},{5,4},{6,7},{7,6},{8,9},{9,8},{10,11... | collective-permute-start | bytes 4718600 | tf_op jit(solution)/shard_map/ppermute | solution.py:115
  506.8 26.0 %collective-permute-start.36 = (bf16[512,512]{1,0:T(8,128)(2,1)}, bf16[512,512]{1,0:T(8,128)(2,1)}, u32[]{:S(2)}, u32[]{:S(2)}) collective-permute-start(bf16[512,512]{1,0:T(8,128)(2,1)} %pad_maximum_fusion.9), channel_id=1, source_target_pairs={{0,16},{16,0},{1,17},{17,1},{2,18},{18,2},{3,19},{19,3},{4,20},{20... | collective-permute-start | bytes 1572872 | tf_op jit(solution)/shard_map/ppermute | solution.py:115
  520.1 137.9 %reduce-scatter.14.cloned.1.call-start = ((), (), s32[]{:S(2)}) async-start(), calls=%async_computation.9 | async-start | bytes 2211840 | tf_op jit(solution)/shard_map/reduce_scatter | solution.py:1202
  523.2 37.8 %collective-permute-start.39 = (bf16[512,1536]{1,0:T(8,128)(2,1)S(1)}, bf16[512,1536]{1,0:T(8,128)(2,1)}, u32[]{:S(2)}, u32[]{:S(2)}) collective-permute-start(bf16[512,1536]{1,0:T(8,128)(2,1)S(1)} %add_convert_fusion.5), channel_id=1, source_target_pairs={{0,16},{16,0},{1,17},{17,1},{2,18},{18,2},{3,19},{19,3},{4,20},{20... | collective-permute-start | bytes 4718600 | tf_op jit(solution)/shard_map/ppermute | solution.py:115
  527.2 42.6 %collective-permute-start.41 = (bf16[2,4,48,1664]{3,2,1,0:T(8,128)(2,1)}, bf16[2,4,48,1664]{3,2,1,0:T(8,128)(2,1)}, u32[]{:S(2)}, u32[]{:S(2)}) collective-permute-start(bf16[2,4,48,1664]{3,2,1,0:T(8,128)(2,1)} %fusion.17), channel_id=1, source_target_pairs={{0,2},{2,0},{1,3},{3,1},{4,6},{6,4},{5,7},{7,5},{8,10},{10,8},{9,1... | collective-permute-start | bytes 3833864 | tf_op jit(solution)/shard_map/ppermute | solution.py:115
  530.1 75.9 %collective-permute-start.29 = (bf16[512,1536]{1,0:T(8,128)(2,1)}, bf16[512,1536]{1,0:T(8,128)(2,1)}, u32[]{:S(2)}, u32[]{:S(2)}) collective-permute-start(bf16[512,1536]{1,0:T(8,128)(2,1)} %add_convert_fusion.9), channel_id=1, source_target_pairs={{0,1},{1,0},{2,3},{3,2},{4,5},{5,4},{6,7},{7,6},{8,9},{9,8},{10,11... | collective-permute-start | bytes 4718600 | tf_op jit(solution)/shard_map/ppermute | solution.py:115
  593.3 94.9 %reduce-scatter.12.cloned.1.call-start = ((), (), s32[]{:S(2)}) async-start(), calls=%async_computation.8 | async-start | bytes 1781760 | tf_op jit(solution)/shard_map/reduce_scatter | solution.py:1242
  595.9 15.6 %collective-permute-start.48 = (bf16[4,48,1664]{2,1,0:T(8,128)(2,1)S(1)}, bf16[4,48,1664]{2,1,0:T(8,128)(2,1)}, u32[]{:S(2)}, u32[]{:S(2)}) collective-permute-start(bf16[4,48,1664]{2,1,0:T(8,128)(2,1)S(1)} %fusion.32), channel_id=1, source_target_pairs={{0,16},{16,0},{1,17},{17,1},{2,18},{18,2},{3,19},{19,3},{4,20},{20... | collective-permute-start | bytes 1916936 | tf_op jit(solution)/shard_map/ppermute | solution.py:115
  600.6 27.9 %collective-permute-start.46 = (bf16[2,4,48,1024]{3,2,1,0:T(8,128)(2,1)}, bf16[2,4,48,1024]{3,2,1,0:T(8,128)(2,1)}, u32[]{:S(2)}, u32[]{:S(2)}) collective-permute-start(bf16[2,4,48,1024]{3,2,1,0:T(8,128)(2,1)} %fusion.27), channel_id=1, source_target_pairs={{0,16},{16,0},{1,17},{17,1},{2,18},{18,2},{3,19},{19,3},{4,20},{20... | collective-permute-start | bytes 2359304 | tf_op jit(solution)/shard_map/ppermute | solution.py:115
  604.7 27.7 %collective-permute-start.43 = (bf16[2,4,48,1024]{3,2,1,0:T(8,128)(2,1)}, bf16[2,4,48,1024]{3,2,1,0:T(8,128)(2,1)}, u32[]{:S(2)}, u32[]{:S(2)}) collective-permute-start(bf16[2,4,48,1024]{3,2,1,0:T(8,128)(2,1)} %fusion.26), channel_id=1, source_target_pairs={{0,2},{2,0},{1,3},{3,1},{4,6},{6,4},{5,7},{7,5},{8,10},{10,8},{9,1... | collective-permute-start | bytes 2359304 | tf_op jit(solution)/shard_map/ppermute | solution.py:115
  639.7 14.1 %collective-permute-start.49 = (bf16[144,1536]{1,0:T(8,128)(2,1)S(1)}, bf16[144,1536]{1,0:T(8,128)(2,1)S(1)}, u32[]{:S(2)}, u32[]{:S(2)}) collective-permute-start(bf16[144,1536]{1,0:T(8,128)(2,1)S(1)} %copy-done.91), channel_id=1, source_target_pairs={{0,16},{16,0},{1,17},{17,1},{2,18},{18,2},{3,19},{19,3},{4,20},{20... | collective-permute-start | bytes 1327112 | tf_op jit(solution)/shard_map/ppermute | solution.py:115
  658.0 12.2 %collective-permute-start.51 = (bf16[144,1536]{1,0:T(8,128)(2,1)}, bf16[144,1536]{1,0:T(8,128)(2,1)S(1)}, u32[]{:S(2)}, u32[]{:S(2)}) collective-permute-start(bf16[144,1536]{1,0:T(8,128)(2,1)} %get-tuple-element.240), channel_id=1, source_target_pairs={{0,16},{16,0},{1,17},{17,1},{2,18},{18,2},{3,19},{19,3},{4,20},{20... | collective-permute-start | bytes 1327112 | tf_op jit(solution)/shard_map/ppermute | solution.py:115
  (158 other events, 869.3 us)
Sparse Core Ops, SparseCore 0:
  51.2 46.9 all-gather.8
  113.6 37.1 all-gather.10
  192.8 37.2 all-gather.12
  232.1 39.1 all-gather.14
  385.2 35.2 reduce-scatter.5
  444.0 35.3 reduce-scatter.7
  520.2 37.4 reduce-scatter.9
  593.4 36.3 reduce-scatter.13
  658.1 30.1 reduce-scatter.11

commit v3 on v2

--- a/solution.py
+++ b/solution.py
@@ -1025,7 +1025,8 @@
         second_held = jnp.stack([second_held, second_x], axis=1)
         qkv_held = jnp.concatenate([first_held, second_held], axis=-1)
         (out_held,) = hold((out_held,), first_y, second_x)
-        qkv_held, one_own = hold((qkv_held, one_own))
+        own_two, sent_two = expert_halves(pair, 1, in_rows)
+        qkv_held, one_own, own_two = hold((qkv_held, one_own, own_two))
         out_x = swap(out_held, "x")
         qkv_core = swap(qkv_held, "core")
         one_own_y = swap(one_own, "y")
@@ -1068,9 +1069,8 @@
     ffn_gain = small_low[:, EXPERTS + 1].astype(F32)
     router_rows = small_low.T[:16]
     if staged:
-        own_two, sent_two = expert_halves(pair, 1, in_rows)
-        kv_prev, out_x, one_own_y, one_other, own_two, sent_two = hold(
-            (kv_prev, out_x, one_own_y, one_other, own_two, sent_two)
+        kv_prev, out_x, one_own_y, one_other, sent_two = hold(
+            (kv_prev, out_x, one_own_y, one_other, sent_two)
         )
         out_held = jnp.stack([out_held, out_x])
         out_y = swap(out_held, "y")
@@ -1080,7 +1080,7 @@
     attended, log_sums = attend(queries, kv_own, kv_prev, *segs, half)
     top_core, top_both = swap(top, "core"), swap(top_x, "core")
     if staged:
-        attended, out_y, other_two = hold((attended, out_y, other_two))
+        attended, out_y, two_own, other_two = hold((attended, out_y, two_own, other_two))
         out_held = jnp.stack([out_held, out_y])
         out_pair = (out_held, swap(out_held, "core"))
         one_other_y = swap(one_other, "y")
@@ -1092,7 +1092,6 @@
     ffn_core = swap(normed_ffn, "core")
     ffn_x = swap(normed_ffn, "x")
     if staged:
-        ffn_x, two_own = hold((ffn_x, two_own))
         two_own_y = swap(two_own, "y")
     ffn_both = swap(ffn_x, "core")
     x_all = (normed_ffn, ffn_x, ffn_core, ffn_both)
@@ -1195,9 +1194,7 @@
     )
     crossed = swap(jnp.concatenate([key_prev, value_prev], axis=1).astype(BF16), "x")
     if staged:
-        crossed, back_two[1], mix_crossed = hold(
-            (crossed, back_two[1], mix_crossed), query_grad
-        )
+        crossed, back_two[1] = hold((crossed, back_two[1]), query_grad)
         total_two.append(add(grads_two[1], back_two[1]).astype(BF16))
         sums_two.append(lax.psum_scatter(total_two[1], "z", scatter_dimension=0))
     crossed = crossed.astype(F32)
@@ -1211,7 +1208,9 @@
         [key_grad.reshape(local_rows, key_width).astype(BF16), value_grad.astype(BF16)], axis=1
     )
     if staged:
-        kv_grad, out_come, sums_one[1] = hold((kv_grad, out_come, sums_one[1]))
+        kv_grad, out_come, sums_one[1], mix_crossed = hold(
+            (kv_grad, out_come, sums_one[1], mix_crossed)
+        )
         out_kept, out_sent = kept_sent(out_kept + out_come.astype(F32), "x")
         out_come = swap(out_sent.astype(BF16), "x")
     qkv_blocks = grad_rows(
@@ -1227,15 +1226,14 @@
         second_come = swap(second_sent.astype(BF16), "x")
         first_kept, first_sent = kept_sent(first_kept + first_come.astype(F32), "x")
         second_kept, second_sent = kept_sent(second_kept + second_come.astype(F32), "y")
-        *sums_one, sums_two[0], out_come = hold(
-            (*sums_one, sums_two[0], out_come), first_come, second_come, total_two[1]
-        )
+        (out_come,) = hold((out_come,), first_come, second_come, total_two[1])
         out_total = (out_kept + out_come.astype(F32)).astype(BF16)
         first_come = swap(first_sent.astype(BF16), "x")
         second_come = swap(second_sent.astype(BF16), "y")
-        expert_sums = [finish_expert(sums_one, in_rows)]
-        sums_two = hold(sums_two, first_come, second_come)
-        expert_sums.append(finish_expert(sums_two, in_rows))
+        *sums_one, sums_two[0], sums_two[1] = hold(
+            (*sums_one, *sums_two), first_come, second_come
+        )
+        expert_sums = [finish_expert(sums, in_rows) for sums in (sums_one, sums_two)]
         first = first_kept + first_come.astype(F32)
         second = second_kept + second_come.astype(F32)
         rows_total = jnp.concatenate([first.astype(BF16), second.astype(BF16), out_total], axis=-1)

time: 763 us -> 731 us (0.958)
  waiting for transfers between devices: 218 us -> 196 us
    all_gather x4, waiting for transfers between devices: 35.4 us -> 2.79 us  [shards(): gather_z = lambda half: lax.all_gather(half, 'z')]
    ppermute x53, waiting for transfers between devices: 164 us -> 181 us  [swap(): return lax.ppermute(value, axis, [(0, 1), (1, 0)])]
    reduce_scatter x1, waiting for transfers between devices: 11.3 us -> 2.4 us  [shards(): lax.psum_scatter(rows_total, 'z', scatter_dimension=0).astype(F32)]
    unnamed x282 -> x300, local copies, waits for them, and re-layouts: 47.4 us -> 39.1 us
  transfers between devices with their start and end apart: 68 -> 68, of which waited for: 27 -> 24; matrix products, arithmetic and copies ran while one was open for 21% -> 25% of each run, Pallas kernels for 27% -> 26%
where the time goes in v3:
time: 731 us; the launch traced here: 724 us
  Pallas kernels  201 us (27%)
  waiting for transfers between devices  196 us (27%)
  other arithmetic  122 us (17%)
  local copies, waits for them, and re-layouts  89.5 us (12%)
  starting transfers between devices  69.3 us (9%)
  matrix products  25 us (3%)
  between operations  21.9 us (3%)
    ppermute x53, waiting for transfers between devices, swap(): return lax.ppermute(value, axis, [(0, 1), (1, 0)])  181 us
    pallas_call x3, Pallas kernels, expert_pass(): pl.pallas_call(functools.partial(expert_kernel, count, bool(given), gives...  128 us
    ppermute x53, starting transfers between devices, swap(): return lax.ppermute(value, axis, [(0, 1), (1, 0)])  58.4 us
    unnamed x300, local copies, waits for them, and re-layouts  39.1 us
    pallas_call x2, Pallas kernels, grad_rows(): pl.pallas_call(functools.partial(grad_rows_kernel, len(bs), extra is not...  16.6 us
    pallas_call x1, Pallas kernels, attend_back(): pl.pallas_call(attend_back_kernel, grid_spec=pltpu.PrefetchScalarGridSpec...  16.5 us
    pallas_call x1, Pallas kernels, attend(): pl.pallas_call(attend_kernel, grid_spec=pltpu.PrefetchScalarGridSpec(num_...  14.6 us
  transfers between devices with their start and end apart: 68, of which 24 were waited for; matrix products, arithmetic and copies ran while one was open for 25% of the time, Pallas kernels for 26%

profile of v3, /device:TPU:1, one launch (start us, length us, event | category | flops | bytes accessed | tf_op | source)
XLA Modules:
  0.0 724.1 jit_solution(4273746558407715301)
XLA Ops:
  31.3 9.6 %collective-permute-done.1 = bf16[48,3712]{1,0:T(8,128)(2,1)} collective-permute-done((bf16[48,3712]{1,0:T(8,128)(2,1)}, bf16[48,3712]{1,0:T(8,128)(2,1)}, u32[]{:S(2)}, u32[]{:S(2)}) %collective-permute-start.1) | collective-permute-done | bytes 356384 | tf_op jit(solution)/shard_map/ppermute | solution.py:120
  52.8 20.2 %collective-permute-done.6 = bf16[4,48,1024]{2,1,0:T(8,128)(2,1)S(1)} collective-permute-done((bf16[4,48,1024]{2,1,0:T(8,128)(2,1)}, bf16[4,48,1024]{2,1,0:T(8,128)(2,1)S(1)}, u32[]{:S(2)}, u32[]{:S(2)}) %collective-permute-start.6) | collective-permute-done | bytes 393248 | tf_op jit(solution)/shard_map/ppermute | solution.py:115
  76.5 6.0 collective-permute-done.7.refs_1_
  85.7 15.6 %collective-permute-done.11.refs_2_ = bf16[2,4,48,1152]{3,2,1,0:T(8,128)(2,1)S(1)} collective-permute-done((bf16[2,4,48,1152]{3,2,1,0:T(8,128)(2,1)}, bf16[2,4,48,1152]{3,2,1,0:T(8,128)(2,1)S(1)}, u32[]{:S(2)}, u32[]{:S(2)}) %collective-permute-start.11) | collective-permute-done | bytes 884768 | tf_op jit(solution)/shard_map/ppermute | solution.py:115
  122.8 12.5 %project.1 = (bf16[512,1536]{1,0:T(8,128)(2,1)S(1)}, bf16[512,512]{1,0:T(8,128)(2,1)}, bf16[512,1536]{1,0:T(8,128)(2,1)S(1)}, bf16[1536,2048]{1,0:T(8,128)(2,1)}, bf16[1536,128]{1,0:T(8,128)(2,1)S(1)}) custom-call(s32[4]{0:T(128)S(1)} %pad_add_fusion.6.place_ref, bf16[512,1536]{1,0:T(8,128)(2,1)S(1)} %bitcast.252, bf16[2,2,4,48,2176]{4,3,2,1,0:T(8,128)(2,1)S(1)} %copy-done, ...), custom_call_target="tpu_custom_call" | custom-call | flops 2415919104 | bytes 5242880 | tf_op jit(solution)/shard_map/project/pallas_call | solution.py:371
  139.7 13.8 %collective-permute-done.15.refs_2_ = bf16[4,144,1536]{2,1,0:T(8,128)(2,1)} collective-permute-done((bf16[4,144,1536]{2,1,0:T(8,128)(2,1)}, bf16[4,144,1536]{2,1,0:T(8,128)(2,1)}, u32[]{:S(2)}, u32[]{:S(2)}) %collective-permute-start.15) | collective-permute-done | bytes 1769504 | tf_op jit(solution)/shard_map/ppermute | solution.py:115
  159.7 14.6 %attend.1 = (bf16[512,1536]{1,0:T(8,128)(2,1)S(1)}, f32[12,512,1]{2,1,0:T(8,128)S(1)}) custom-call(s32[1]{0:T(128)} %bitcast.half_ref, bf16[512,1536]{1,0:T(8,128)(2,1)S(1)} %copy-done.11, bf16[512,512]{1,0:T(8,128)(2,1)} %get-tuple-element.144.ko_ref.vo_ref, bf16[512,512]{1,0:T(8,128)(2,1)} %get-tuple-element.144.ko_ref.vo_ref, ...), custom_call_target="tpu_custom_call" | custom-call | flops 805306368 | bytes 4194304 | tf_op jit(solution)/shard_map/attend/pallas_call | solution.py:533
  177.1 2.8 all-gather.13.cloned.1.call-done
  179.9 5.3 collective-permute-done.16.refs_1_
  190.9 3.1 collective-permute-done.18.other
  194.1 13.0 %join.1 = (f32[512,1536]{1,0:T(8,128)S(1)}, bf16[512,1536]{1,0:T(8,128)(2,1)}, f32[512,1]{1,0:T(8,128)S(1)}, bf16[1536,1536]{1,0:T(8,128)(2,1)}) custom-call(s32[4]{0:T(128)S(1)} %pad_add_fusion.6.place_ref, bf16[512,1536]{1,0:T(8,128)(2,1)S(1)} %copy-done.13, bf16[512,1536]{1,0:T(8,128)(2,1)S(1)} %bitcast.253, f32[1,1536]{1,0:T(1,128)S(1)} %reshape.221.gain_ref, ...), custom_call_target="tpu_custom_call" | custom-call | flops 1207959552 | bytes 4194304 | tf_op jit(solution)/shard_map/join/pallas_call | solution.py:451
  209.3 34.3 %collective-permute-done.20.refs_5_.refs_4_ = bf16[512,1536]{1,0:T(8,128)(2,1)} collective-permute-done((bf16[512,1536]{1,0:T(8,128)(2,1)}, bf16[512,1536]{1,0:T(8,128)(2,1)}, u32[]{:S(2)}, u32[]{:S(2)}) %collective-permute-start.20) | collective-permute-done | bytes 1572896 | tf_op jit(solution)/shard_map/ppermute | solution.py:115
  259.1 59.1 %expert.3 = (bf16[512,1536]{1,0:T(8,128)(2,1)}, bf16[512,1536]{1,0:T(8,128)(2,1)}, bf16[512,1536]{1,0:T(8,128)(2,1)}, bf16[512,1536]{1,0:T(8,128)(2,1)}, bf16[51...) custom-call(s32[5]{0:T(128)} %concatenate.76.place_ref, ...), custom_call_target="tpu_custom_call" | custom-call | flops 70464307200 | bytes 25165824 | tf_op jit(solution)/shard_map/expert/pallas_call | solution.py:834
  319.4 16.1 %collective-permute-done.26.refs_3_ = bf16[4,144,1536]{2,1,0:T(8,128)(2,1)} collective-permute-done((bf16[4,144,1536]{2,1,0:T(8,128)(2,1)}, bf16[4,144,1536]{2,1,0:T(8,128)(2,1)}, u32[]{:S(2)}, u32[]{:S(2)}) %collective-permute-start.26) | collective-permute-done | bytes 1769504 | tf_op jit(solution)/shard_map/ppermute | solution.py:115
  335.5 27.3 %expert.4 = (bf16[512,1536]{1,0:T(8,128)(2,1)}, bf16[512,1536]{1,0:T(8,128)(2,1)}, bf16[512,1536]{1,0:T(8,128)(2,1)}, bf16[512,1536]{1,0:T(8,128)(2,1)}, f32[2,1...) custom-call(s32[5]{0:T(128)} %concatenate.77.place_ref, ...), custom_call_target="tpu_custom_call" | custom-call | flops 35232153600 | bytes 25165824 | tf_op jit(solution)/shard_map/expert/pallas_call | solution.py:834
  362.8 3.4 add_convert_fusion.10
  378.0 3.3 add_convert_fusion.3.refs_1_
  381.3 3.2 add_convert_fusion.8
  384.7 41.3 %expert.5 = (bf16[512,1536]{1,0:T(8,128)(2,1)}, bf16[512,1536]{1,0:T(8,128)(2,1)}, bf16[512,1536]{1,0:T(8,128)(2,1)}, bf16[512,1536]{1,0:T(8,128)(2,1)}, f32[2,1...) custom-call(s32[5]{0:T(128)} %concatenate.77.place_ref, ...), custom_call_target="tpu_custom_call" | custom-call | flops 35232153600 | bytes 25165824 | tf_op jit(solution)/shard_map/expert/pallas_call | solution.py:834
  427.3 3.5 add_convert_fusion.7
  436.3 3.1 add_convert_fusion.2.refs_2_
  442.7 4.0 fusion.72
  447.4 5.9 multiply_reduce_fusion
  457.6 7.1 grad_rows.2
  467.3 3.7 convolution_convert_fusion.refs_0_
  471.1 8.7 %collective-permute-done.35.refs_1_ = bf16[4,144,1536]{2,1,0:T(8,128)(2,1)} collective-permute-done((bf16[4,144,1536]{2,1,0:T(8,128)(2,1)}, bf16[4,144,1536]{2,1,0:T(8,128)(2,1)}, u32[]{:S(2)}, u32[]{:S(2)}) %collective-permute-start.35) | collective-permute-done | bytes 1769504 | tf_op jit(solution)/shard_map/ppermute | solution.py:115
  482.8 16.5 %attend_back.1 = (bf16[512,1536]{1,0:T(8,128)(2,1)S(1)}, f32[512,256]{1,0:T(8,128)S(1)}, f32[512,256]{1,0:T(8,128)S(1)}, f32[512,256]{1,0:T(8,128)S(1)}, f32[512,256]{1,0:T(8,128)S(1)}) custom-call(s32[1]{0:T(128)} %bitcast.half_ref, bf16[512,1536]{1,0:T(8,128)(2,1)} %copy-done.10, bf16[512,512]{1,0:T(8,128)(2,1)} %get-tuple-element.144.ko_ref.vo_ref, ...), custom_call_target="tpu_custom_call" | custom-call | flops 2013265920 | bytes 6291456 | tf_op jit(solution)/shard_map/attend_back/pallas_call | solution.py:613
  502.0 9.9 %collective-permute-start.36 = (bf16[512,512]{1,0:T(8,128)(2,1)}, bf16[512,512]{1,0:T(8,128)(2,1)}, u32[]{:S(2)}, u32[]{:S(2)}) collective-permute-start(bf16[512,512]{1,0:T(8,128)(2,1)} %pad_maximum_fusion.9), channel_id=1, source_target_pairs={{0,16},{16,0},{1,17},{17,1},{2,18},{18,2},{3,19},{19,3},{4,20},{20... | collective-permute-start | bytes 1572872 | tf_op jit(solution)/shard_map/ppermute | solution.py:115
  511.9 3.1 add_convert_fusion
  515.1 4.2 add_convert_fusion.5
  519.7 4.7 convert_add_fusion
  524.4 2.9 fusion.17
  539.0 17.1 %collective-permute-done.41.refs_3_ = bf16[512,1536]{1,0:T(8,128)(2,1)} collective-permute-done((bf16[512,1536]{1,0:T(8,128)(2,1)}, bf16[512,1536]{1,0:T(8,128)(2,1)}, u32[]{:S(2)}, u32[]{:S(2)}) %collective-permute-start.41) | collective-permute-done | bytes 1572896 | tf_op jit(solution)/shard_map/ppermute | solution.py:115
  557.2 9.6 %grad_rows.3 = (bf16[2,2,4,48,1024]{4,3,2,1,0:T(8,128)(2,1)S(1)}, bf16[2,2,4,48,1024]{4,3,2,1,0:T(8,128)(2,1)}, bf16[2,2,4,48,1024]{4,3,2,1,0:T(8,128)(2,1)S(1)}, bf16[2,2,4,48,1024]{4,3,2,1,0:T(8,128)(2,1)}) custom-call(s32[4]{0:T(128)S(1)} %constant_dynamic-update-slice_fusion.place_ref, bf16[512,1536]{1,0:T(8,128)(2,1)} %copy-done.40, ...), custom_call_target="tpu_custom_call" | custom-call | flops 1610612736 | bytes 3145728 | tf_op jit(solution)/shard_map/grad_rows/pallas_call | solution.py:247
  571.7 3.1 add_convert_fusion.1.refs_3_
  576.8 4.1 fusion.6
  594.2 3.7 collective-permute-done.48.refs_0_
  597.9 7.6 %collective-permute-done.43.refs_1_ = bf16[2,4,48,1024]{3,2,1,0:T(8,128)(2,1)} collective-permute-done((bf16[2,4,48,1024]{3,2,1,0:T(8,128)(2,1)}, bf16[2,4,48,1024]{3,2,1,0:T(8,128)(2,1)}, u32[]{:S(2)}, u32[]{:S(2)}) %collective-permute-start.43) | collective-permute-done | bytes 786464 | tf_op jit(solution)/shard_map/ppermute | solution.py:115
  608.2 6.5 collective-permute-done.46.refs_2_
  623.0 2.9 collective-permute-done.47.refs_5_
  631.2 3.5 collective-permute-done.49
  636.4 7.8 %collective-permute-done.51 = bf16[144,1536]{1,0:T(8,128)(2,1)} collective-permute-done((bf16[144,1536]{1,0:T(8,128)(2,1)}, bf16[144,1536]{1,0:T(8,128)(2,1)}, u32[]{:S(2)}, u32[]{:S(2)}) %collective-permute-start.51) | collective-permute-done | bytes 442400 | tf_op jit(solution)/shard_map/ppermute | solution.py:115
  645.7 4.3 collective-permute-start.50
  650.2 8.6 %fusion = (f32[512]{0:T(512)}, f32[512]{0:T(512)}, f32[512,1536]{1,0:T(8,128)}) fusion(bf16[1,512,1536]{2,1,0:T(8,128)(2,1)S(1)} %copy-done.8, bf16[1536,2048]{1,0:T(8,128)(2,1)} %get-tuple-element.218, bf16[512,512]{1,0:T(8,128)(2,1)S(1)} %copy-done.21, bf16[512,1536]{1,0:T(8,128)(2,1)S(1)} %copy-done.23, f32[1536]{0:T(1024)S(1)} %copy-done.130), kind=kOutput, calls=%fused_computation.11 | convolution fusion | flops 3230137344 | bytes 13117440 | tf_op jit(solution)/shard_map/dot_general | solution.py:107
  680.3 5.2 fusion.13
  690.4 3.8 collective-permute-start.58
  706.6 4.2 multiply_subtract_fusion.1
  711.7 4.3 multiply_subtract_fusion
  (610 shorter events, 224.0 us)
Async XLA Ops:
  7.2 99.4 %all-gather.9.cloned.1.call-start = ((), (), s32[]{:S(2)}) async-start(), calls=%async_computation.10 | async-start | bytes 2211840 | tf_op jit(solution)/shard_map/all_gather | solution.py:1003
  12.3 17.2 %collective-permute-start.2 = (bf16[48,3712]{1,0:T(8,128)(2,1)}, bf16[48,3712]{1,0:T(8,128)(2,1)}, u32[]{:S(2)}, u32[]{:S(2)}) collective-permute-start(bf16[48,3712]{1,0:T(8,128)(2,1)} %concatenate.67), channel_id=1, source_target_pairs={{0,4},{4,8},{8,12},{12,0},{1,5},{5,9},{9,13},{13,1},{2,6},{6,10},{... | collective-permute-start | bytes 1069064 | tf_op jit(solution)/shard_map/ppermute | solution.py:120
  14.4 26.4 %collective-permute-start.1 = (bf16[48,3712]{1,0:T(8,128)(2,1)}, bf16[48,3712]{1,0:T(8,128)(2,1)}, u32[]{:S(2)}, u32[]{:S(2)}) collective-permute-start(bf16[48,3712]{1,0:T(8,128)(2,1)} %concatenate.67), channel_id=1, source_target_pairs={{0,8},{4,12},{8,0},{12,4},{1,9},{5,13},{9,1},{13,5},{2,10},{6,14},... | collective-permute-start | bytes 1069064 | tf_op jit(solution)/shard_map/ppermute | solution.py:120
  16.7 25.9 %collective-permute-start = (bf16[48,3712]{1,0:T(8,128)(2,1)}, bf16[48,3712]{1,0:T(8,128)(2,1)}, u32[]{:S(2)}, u32[]{:S(2)}) collective-permute-start(bf16[48,3712]{1,0:T(8,128)(2,1)} %concatenate.67), channel_id=1, source_target_pairs={{0,12},{4,0},{8,4},{12,8},{1,13},{5,1},{9,5},{13,9},{2,14},{6,2},{... | collective-permute-start | bytes 1069064 | tf_op jit(solution)/shard_map/ppermute | solution.py:120
  21.4 24.7 %collective-permute-start.3 = (bf16[2,2,72,1536]{3,2,1,0:T(8,128)(2,1)}, bf16[2,2,72,1536]{3,2,1,0:T(8,128)(2,1)S(1)}, u32[]{:S(2)}, u32[]{:S(2)}) collective-permute-start(bf16[2,2,72,1536]{3,2,1,0:T(8,128)(2,1)} %get-tuple-element.398), channel_id=1, source_target_pairs={{0,1},{1,0},{2,3},{3,2},{4,5},{5,4},{6,7},{7,6},{8,9},{9,8},{10,11... | collective-permute-start | bytes 2654216 | tf_op jit(solution)/shard_map/ppermute | solution.py:115
  28.6 53.9 %collective-permute-start.8 = (bf16[512,1536]{1,0:T(8,128)(2,1)}, bf16[512,1536]{1,0:T(8,128)(2,1)}, u32[]{:S(2)}, u32[]{:S(2)}) collective-permute-start(bf16[512,1536]{1,0:T(8,128)(2,1)} %hold.20), channel_id=1, source_target_pairs={{0,16},{16,0},{1,17},{17,1},{2,18},{18,2},{3,19},{19,3},{4,20},{20... | collective-permute-start | bytes 4718600 | tf_op jit(solution)/shard_map/ppermute | solution.py:115
  50.0 89.7 %all-gather.11.cloned.1.call-start = ((), (), s32[]{:S(2)}) async-start(), calls=%async_computation.11 | async-start | bytes 2211840 | tf_op jit(solution)/shard_map/all_gather | solution.py:1003
  50.1 23.0 %collective-permute-start.6 = (bf16[4,48,1024]{2,1,0:T(8,128)(2,1)}, bf16[4,48,1024]{2,1,0:T(8,128)(2,1)S(1)}, u32[]{:S(2)}, u32[]{:S(2)}) collective-permute-start(bf16[4,48,1024]{2,1,0:T(8,128)(2,1)} %get-tuple-element.138), channel_id=1, source_target_pairs={{0,16},{16,0},{1,17},{17,1},{2,18},{18,2},{3,19},{19,3},{4,20},{20... | collective-permute-start | bytes 1179656 | tf_op jit(solution)/shard_map/ppermute | solution.py:115
  51.4 23.6 %collective-permute-start.10 = (bf16[4,48,1152]{2,1,0:T(8,128)(2,1)}, bf16[4,48,1152]{2,1,0:T(8,128)(2,1)S(1)}, u32[]{:S(2)}, u32[]{:S(2)}) collective-permute-start(bf16[4,48,1152]{2,1,0:T(8,128)(2,1)} %get-tuple-element.140), channel_id=1, source_target_pairs={{0,2},{2,0},{1,3},{3,1},{4,6},{6,4},{5,7},{7,5},{8,10},{10,8},{9,1... | collective-permute-start | bytes 1327112 | tf_op jit(solution)/shard_map/ppermute | solution.py:115
  52.6 29.9 %collective-permute-start.7 = (bf16[144,1536]{1,0:T(8,128)(2,1)S(1)}, bf16[144,1536]{1,0:T(8,128)(2,1)S(1)}, u32[]{:S(2)}, u32[]{:S(2)}) collective-permute-start(bf16[144,1536]{1,0:T(8,128)(2,1)S(1)} %copy-done.86), channel_id=1, source_target_pairs={{0,16},{16,0},{1,17},{17,1},{2,18},{18,2},{3,19},{19,3},{4,20},{20... | collective-permute-start | bytes 1327112 | tf_op jit(solution)/shard_map/ppermute | solution.py:115
  76.3 25.0 %collective-permute-start.11 = (bf16[2,4,48,1152]{3,2,1,0:T(8,128)(2,1)}, bf16[2,4,48,1152]{3,2,1,0:T(8,128)(2,1)S(1)}, u32[]{:S(2)}, u32[]{:S(2)}) collective-permute-start(bf16[2,4,48,1152]{3,2,1,0:T(8,128)(2,1)} %get-tuple-element.410), channel_id=1, source_target_pairs={{0,16},{16,0},{1,17},{17,1},{2,18},{18,2},{3,19},{19,3},{4,20},{20... | collective-permute-start | bytes 2654216 | tf_op jit(solution)/shard_map/ppermute | solution.py:115
  83.3 18.1 %collective-permute-start.9 = (bf16[2,4,48,1024]{3,2,1,0:T(8,128)(2,1)}, bf16[2,4,48,1024]{3,2,1,0:T(8,128)(2,1)S(1)}, u32[]{:S(2)}, u32[]{:S(2)}) collective-permute-start(bf16[2,4,48,1024]{3,2,1,0:T(8,128)(2,1)} %get-tuple-element.139), channel_id=1, source_target_pairs={{0,2},{2,0},{1,3},{3,1},{4,6},{6,4},{5,7},{7,5},{8,10},{10,8},{9,1... | collective-permute-start | bytes 2359304 | tf_op jit(solution)/shard_map/ppermute | solution.py:115
  85.7 94.2 %all-gather.13.cloned.1.call-start = ((), (), s32[]{:S(2)}) async-start(), calls=%async_computation.12 | async-start | bytes 2211840 | tf_op jit(solution)/shard_map/all_gather | solution.py:1003
  113.0 40.5 %collective-permute-start.15 = (bf16[4,144,1536]{2,1,0:T(8,128)(2,1)}, bf16[4,144,1536]{2,1,0:T(8,128)(2,1)}, u32[]{:S(2)}, u32[]{:S(2)}) collective-permute-start(bf16[4,144,1536]{2,1,0:T(8,128)(2,1)} %get-tuple-element.145.refs_0_), channel_id=1, source_target_pairs={{0,2},{2,0},{1,3},{3,1},{4,6},{6,4},{5,7},{7,5},{8,10},{10,8},{9,1... | collective-permute-start | bytes 5308424 | tf_op jit(solution)/shard_map/ppermute | solution.py:115
  115.8 142.9 %all-gather.15.cloned.1.call-start = ((), (), s32[]{:S(2)}) async-start(), calls=%async_computation.13 | async-start | bytes 2211840 | tf_op jit(solution)/shard_map/all_gather | solution.py:1003
  119.3 20.4 %collective-permute-start.14 = (bf16[4,48,1536]{2,1,0:T(8,128)(2,1)}, bf16[4,48,1536]{2,1,0:T(8,128)(2,1)}, u32[]{:S(2)}, u32[]{:S(2)}) collective-permute-start(bf16[4,48,1536]{2,1,0:T(8,128)(2,1)} %hold.23), channel_id=1, source_target_pairs={{0,16},{16,0},{1,17},{17,1},{2,18},{18,2},{3,19},{19,3},{4,20},{20... | collective-permute-start | bytes 1769480 | tf_op jit(solution)/shard_map/ppermute | solution.py:115
  138.4 15.2 %collective-permute-start.13 = (bf16[512,512]{1,0:T(8,128)(2,1)}, bf16[512,512]{1,0:T(8,128)(2,1)S(1)}, u32[]{:S(2)}, u32[]{:S(2)}) collective-permute-start(bf16[512,512]{1,0:T(8,128)(2,1)} %get-tuple-element.144.ko_ref.vo_ref), channel_id=1, source_target_pairs={{0,16},{16,0},{1,17},{17,1},{2,18},{18,2},{3,19},{19,3},{4,20},{20... | collective-permute-start | bytes 1572872 | tf_op jit(solution)/shard_map/ppermute | solution.py:115
  158.2 27.0 %collective-permute-start.16 = (bf16[2,4,48,1536]{3,2,1,0:T(8,128)(2,1)}, bf16[2,4,48,1536]{3,2,1,0:T(8,128)(2,1)}, u32[]{:S(2)}, u32[]{:S(2)}) collective-permute-start(bf16[2,4,48,1536]{3,2,1,0:T(8,128)(2,1)} %get-tuple-element.400), channel_id=1, source_target_pairs={{0,2},{2,0},{1,3},{3,1},{4,6},{6,4},{5,7},{7,5},{8,10},{10,8},{9,1... | collective-permute-start | bytes 3538952 | tf_op jit(solution)/shard_map/ppermute | solution.py:115
  159.4 20.5 %collective-permute-start.17 = (bf16[144,1536]{1,0:T(8,128)(2,1)S(1)}, bf16[144,1536]{1,0:T(8,128)(2,1)}, u32[]{:S(2)}, u32[]{:S(2)}) collective-permute-start(bf16[144,1536]{1,0:T(8,128)(2,1)S(1)} %copy-done.84), channel_id=1, source_target_pairs={{0,16},{16,0},{1,17},{17,1},{2,18},{18,2},{3,19},{19,3},{4,20},{20... | collective-permute-start | bytes 1327112 | tf_op jit(solution)/shard_map/ppermute | solution.py:115
  207.7 35.9 %collective-permute-start.20 = (bf16[512,1536]{1,0:T(8,128)(2,1)}, bf16[512,1536]{1,0:T(8,128)(2,1)}, u32[]{:S(2)}, u32[]{:S(2)}) collective-permute-start(bf16[512,1536]{1,0:T(8,128)(2,1)} %get-tuple-element.159.refs_4_), channel_id=1, source_target_pairs={{0,16},{16,0},{1,17},{17,1},{2,18},{18,2},{3,19},{19,3},{4,20},{20... | collective-permute-start | bytes 4718600 | tf_op jit(solution)/shard_map/ppermute | solution.py:115
  208.2 238.6 %reduce-scatter.6.cloned.1.call-start = ((), (), s32[]{:S(2)}) async-start(), calls=%async_computation.5 | async-start | bytes 2211840 | tf_op jit(solution)/shard_map/reduce_scatter | solution.py:1129
  208.4 50.7 %collective-permute-start.19 = (bf16[4,144,1536]{2,1,0:T(8,128)(2,1)}, bf16[4,144,1536]{2,1,0:T(8,128)(2,1)}, u32[]{:S(2)}, u32[]{:S(2)}) collective-permute-start(bf16[4,144,1536]{2,1,0:T(8,128)(2,1)} %get-tuple-element.157.refs_1_), channel_id=1, source_target_pairs={{0,2},{2,0},{1,3},{3,1},{4,6},{6,4},{5,7},{7,5},{8,10},{10,8},{9,1... | collective-permute-start | bytes 5308424 | tf_op jit(solution)/shard_map/ppermute | solution.py:115
  244.9 14.2 %collective-permute-start.24 = (bf16[512,1536]{1,0:T(8,128)(2,1)}, bf16[512,1536]{1,0:T(8,128)(2,1)}, u32[]{:S(2)}, u32[]{:S(2)}) collective-permute-start(bf16[512,1536]{1,0:T(8,128)(2,1)} %get-tuple-element.162.refs_9_.refs_6_), channel_id=1, source_target_pairs={{0,1},{1,0},{2,3},{3,2},{4,5},{5,4},{6,7},{7,6},{8,9},{9,8},{10,11... | collective-permute-start | bytes 4718600 | tf_op jit(solution)/shard_map/ppermute | solution.py:115
  257.6 61.8 %collective-permute-start.25 = (bf16[4,144,1536]{2,1,0:T(8,128)(2,1)}, bf16[4,144,1536]{2,1,0:T(8,128)(2,1)}, u32[]{:S(2)}, u32[]{:S(2)}) collective-permute-start(bf16[4,144,1536]{2,1,0:T(8,128)(2,1)} %get-tuple-element.165.refs_0_), channel_id=1, source_target_pairs={{0,2},{2,0},{1,3},{3,1},{4,6},{6,4},{5,7},{7,5},{8,10},{10,8},{9,1... | collective-permute-start | bytes 5308424 | tf_op jit(solution)/shard_map/ppermute | solution.py:115
  258.8 76.7 %collective-permute-start.26 = (bf16[4,144,1536]{2,1,0:T(8,128)(2,1)}, bf16[4,144,1536]{2,1,0:T(8,128)(2,1)}, u32[]{:S(2)}, u32[]{:S(2)}) collective-permute-start(bf16[4,144,1536]{2,1,0:T(8,128)(2,1)} %get-tuple-element.166.refs_1_), channel_id=1, source_target_pairs={{0,2},{2,0},{1,3},{3,1},{4,6},{6,4},{5,7},{7,5},{8,10},{10,8},{9,1... | collective-permute-start | bytes 5308424 | tf_op jit(solution)/shard_map/ppermute | solution.py:115
  318.1 59.8 %collective-permute-start.27 = (bf16[4,144,1536]{2,1,0:T(8,128)(2,1)}, bf16[4,144,1536]{2,1,0:T(8,128)(2,1)}, u32[]{:S(2)}, u32[]{:S(2)}) collective-permute-start(bf16[4,144,1536]{2,1,0:T(8,128)(2,1)} %get-tuple-element.174), channel_id=1, source_target_pairs={{0,2},{2,0},{1,3},{3,1},{4,6},{6,4},{5,7},{7,5},{8,10},{10,8},{9,1... | collective-permute-start | bytes 5308424 | tf_op jit(solution)/shard_map/ppermute | solution.py:115
  366.2 15.1 %collective-permute-start.28 = (bf16[512,1536]{1,0:T(8,128)(2,1)}, bf16[512,1536]{1,0:T(8,128)(2,1)}, u32[]{:S(2)}, u32[]{:S(2)}) collective-permute-start(bf16[512,1536]{1,0:T(8,128)(2,1)} %add_convert_fusion.10), channel_id=1, source_target_pairs={{0,1},{1,0},{2,3},{3,2},{4,5},{5,4},{6,7},{7,6},{8,9},{9,8},{10,11... | collective-permute-start | bytes 4718600 | tf_op jit(solution)/shard_map/ppermute | solution.py:115
  376.2 60.1 %collective-permute-start.32 = (bf16[4,144,1536]{2,1,0:T(8,128)(2,1)}, bf16[4,144,1536]{2,1,0:T(8,128)(2,1)}, u32[]{:S(2)}, u32[]{:S(2)}) collective-permute-start(bf16[4,144,1536]{2,1,0:T(8,128)(2,1)} %get-tuple-element.195), channel_id=1, source_target_pairs={{0,2},{2,0},{1,3},{3,1},{4,6},{6,4},{5,7},{7,5},{8,10},{10,8},{9,1... | collective-permute-start | bytes 5308424 | tf_op jit(solution)/shard_map/ppermute | solution.py:115
  384.5 42.7 %collective-permute-start.30 = (bf16[512,1536]{1,0:T(8,128)(2,1)}, bf16[512,1536]{1,0:T(8,128)(2,1)}, u32[]{:S(2)}, u32[]{:S(2)}) collective-permute-start(bf16[512,1536]{1,0:T(8,128)(2,1)} %add_convert_fusion.8), channel_id=1, source_target_pairs={{0,16},{16,0},{1,17},{17,1},{2,18},{18,2},{3,19},{19,3},{4,20},{20... | collective-permute-start | bytes 4718600 | tf_op jit(solution)/shard_map/ppermute | solution.py:115
  384.6 154.4 %reduce-scatter.8.cloned.1.call-start = ((), (), s32[]{:S(2)}) async-start(), calls=%async_computation.6 | async-start | bytes 2211840 | tf_op jit(solution)/shard_map/reduce_scatter | solution.py:1138
  430.8 15.9 %collective-permute-start.31 = (bf16[512,1536]{1,0:T(8,128)(2,1)}, bf16[512,1536]{1,0:T(8,128)(2,1)}, u32[]{:S(2)}, u32[]{:S(2)}) collective-permute-start(bf16[512,1536]{1,0:T(8,128)(2,1)} %add_convert_fusion.7), channel_id=1, source_target_pairs={{0,1},{1,0},{2,3},{3,2},{4,5},{5,4},{6,7},{7,6},{8,9},{9,8},{10,11... | collective-permute-start | bytes 4718600 | tf_op jit(solution)/shard_map/ppermute | solution.py:115
  439.5 180.8 %reduce-scatter.12.cloned.1.call-start = ((), (), s32[]{:S(2)}) async-start(), calls=%async_computation.8 | async-start | bytes 2211840 | tf_op jit(solution)/shard_map/reduce_scatter | solution.py:1189
  439.7 40.1 %collective-permute-start.35 = (bf16[4,144,1536]{2,1,0:T(8,128)(2,1)}, bf16[4,144,1536]{2,1,0:T(8,128)(2,1)}, u32[]{:S(2)}, u32[]{:S(2)}) collective-permute-start(bf16[4,144,1536]{2,1,0:T(8,128)(2,1)} %get-tuple-element.200), channel_id=1, source_target_pairs={{0,2},{2,0},{1,3},{3,1},{4,6},{6,4},{5,7},{7,5},{8,10},{10,8},{9,1... | collective-permute-start | bytes 5308424 | tf_op jit(solution)/shard_map/ppermute | solution.py:115
  440.1 90.0 %collective-permute-start.37 = (bf16[4,144,1536]{2,1,0:T(8,128)(2,1)}, bf16[4,144,1536]{2,1,0:T(8,128)(2,1)}, u32[]{:S(2)}, u32[]{:S(2)}) collective-permute-start(bf16[4,144,1536]{2,1,0:T(8,128)(2,1)} %get-tuple-element.207), channel_id=1, source_target_pairs={{0,2},{2,0},{1,3},{3,1},{4,6},{6,4},{5,7},{7,5},{8,10},{10,8},{9,1... | collective-permute-start | bytes 5308424 | tf_op jit(solution)/shard_map/ppermute | solution.py:115
  464.7 55.0 %collective-permute-start.38 = (bf16[2,2,4,48,1664]{4,3,2,1,0:T(8,128)(2,1)}, bf16[2,2,4,48,1664]{4,3,2,1,0:T(8,128)(2,1)}, u32[]{:S(2)}, u32[]{:S(2)}) collective-permute-start(bf16[2,2,4,48,1664]{4,3,2,1,0:T(8,128)(2,1)} %get-tuple-element.201.refs_2_), channel_id=1, source_target_pairs={{0,1},{1,0},{2,3},{3,2},{4,5},{5,4},{6,7},{7,6},{8,9},{9,8},{10,11... | collective-permute-start | bytes 7667720 | tf_op jit(solution)/shard_map/ppermute | solution.py:115
  467.3 47.8 %collective-permute-start.40 = (bf16[512,1536]{1,0:T(8,128)(2,1)}, bf16[512,1536]{1,0:T(8,128)(2,1)}, u32[]{:S(2)}, u32[]{:S(2)}) collective-permute-start(bf16[512,1536]{1,0:T(8,128)(2,1)} %add_convert_fusion.6), channel_id=1, source_target_pairs={{0,1},{1,0},{2,3},{3,2},{4,5},{5,4},{6,7},{7,6},{8,9},{9,8},{10,11... | collective-permute-start | bytes 4718600 | tf_op jit(solution)/shard_map/ppermute | solution.py:115
  502.0 28.1 %collective-permute-start.36 = (bf16[512,512]{1,0:T(8,128)(2,1)}, bf16[512,512]{1,0:T(8,128)(2,1)}, u32[]{:S(2)}, u32[]{:S(2)}) collective-permute-start(bf16[512,512]{1,0:T(8,128)(2,1)} %pad_maximum_fusion.9), channel_id=1, source_target_pairs={{0,16},{16,0},{1,17},{17,1},{2,18},{18,2},{3,19},{19,3},{4,20},{20... | collective-permute-start | bytes 1572872 | tf_op jit(solution)/shard_map/ppermute | solution.py:115
  515.0 105.2 %reduce-scatter.14.cloned.1.call-start = ((), (), s32[]{:S(2)}) async-start(), calls=%async_computation.9 | async-start | bytes 2211840 | tf_op jit(solution)/shard_map/reduce_scatter | solution.py:1199
  519.3 36.8 %collective-permute-start.41 = (bf16[512,1536]{1,0:T(8,128)(2,1)}, bf16[512,1536]{1,0:T(8,128)(2,1)}, u32[]{:S(2)}, u32[]{:S(2)}) collective-permute-start(bf16[512,1536]{1,0:T(8,128)(2,1)} %add_convert_fusion.5), channel_id=1, source_target_pairs={{0,16},{16,0},{1,17},{17,1},{2,18},{18,2},{3,19},{19,3},{4,20},{20... | collective-permute-start | bytes 4718600 | tf_op jit(solution)/shard_map/ppermute | solution.py:115
  527.3 28.8 %collective-permute-start.39 = (bf16[2,4,48,1664]{3,2,1,0:T(8,128)(2,1)}, bf16[2,4,48,1664]{3,2,1,0:T(8,128)(2,1)}, u32[]{:S(2)}, u32[]{:S(2)}) collective-permute-start(bf16[2,4,48,1664]{3,2,1,0:T(8,128)(2,1)} %fusion.17), channel_id=1, source_target_pairs={{0,2},{2,0},{1,3},{3,1},{4,6},{6,4},{5,7},{7,5},{8,10},{10,8},{9,1... | collective-permute-start | bytes 3833864 | tf_op jit(solution)/shard_map/ppermute | solution.py:115
  569.0 14.8 %collective-permute-start.42 = (bf16[2,2,4,48,1024]{4,3,2,1,0:T(8,128)(2,1)}, bf16[2,2,4,48,1024]{4,3,2,1,0:T(8,128)(2,1)}, u32[]{:S(2)}, u32[]{:S(2)}) collective-permute-start(bf16[2,2,4,48,1024]{4,3,2,1,0:T(8,128)(2,1)} %get-tuple-element.221.refs_1_), channel_id=1, source_target_pairs={{0,1},{1,0},{2,3},{3,2},{4,5},{5,4},{6,7},{7,6},{8,9},{9,8},{10,11... | collective-permute-start | bytes 4718600 | tf_op jit(solution)/shard_map/ppermute | solution.py:115
  574.8 90.3 %reduce-scatter.10.cloned.1.call-start = ((), (), s32[]{:S(2)}) async-start(), calls=%async_computation.7 | async-start | bytes 1781760 | tf_op jit(solution)/shard_map/reduce_scatter | solution.py:1240
  582.3 15.6 %collective-permute-start.48 = (bf16[4,48,1664]{2,1,0:T(8,128)(2,1)S(1)}, bf16[4,48,1664]{2,1,0:T(8,128)(2,1)}, u32[]{:S(2)}, u32[]{:S(2)}) collective-permute-start(bf16[4,48,1664]{2,1,0:T(8,128)(2,1)S(1)} %fusion.32), channel_id=1, source_target_pairs={{0,16},{16,0},{1,17},{17,1},{2,18},{18,2},{3,19},{19,3},{4,20},{20... | collective-permute-start | bytes 1916936 | tf_op jit(solution)/shard_map/ppermute | solution.py:115
  586.9 18.6 %collective-permute-start.43 = (bf16[2,4,48,1024]{3,2,1,0:T(8,128)(2,1)}, bf16[2,4,48,1024]{3,2,1,0:T(8,128)(2,1)}, u32[]{:S(2)}, u32[]{:S(2)}) collective-permute-start(bf16[2,4,48,1024]{3,2,1,0:T(8,128)(2,1)} %fusion.26), channel_id=1, source_target_pairs={{0,2},{2,0},{1,3},{3,1},{4,6},{6,4},{5,7},{7,5},{8,10},{10,8},{9,1... | collective-permute-start | bytes 2359304 | tf_op jit(solution)/shard_map/ppermute | solution.py:115
  590.1 24.6 %collective-permute-start.46 = (bf16[2,4,48,1024]{3,2,1,0:T(8,128)(2,1)}, bf16[2,4,48,1024]{3,2,1,0:T(8,128)(2,1)}, u32[]{:S(2)}, u32[]{:S(2)}) collective-permute-start(bf16[2,4,48,1024]{3,2,1,0:T(8,128)(2,1)} %fusion.27), channel_id=1, source_target_pairs={{0,16},{16,0},{1,17},{17,1},{2,18},{18,2},{3,19},{19,3},{4,20},{20... | collective-permute-start | bytes 2359304 | tf_op jit(solution)/shard_map/ppermute | solution.py:115
  593.4 86.9 %collective-permute-start.29 = (bf16[512,1536]{1,0:T(8,128)(2,1)}, bf16[512,1536]{1,0:T(8,128)(2,1)}, u32[]{:S(2)}, u32[]{:S(2)}) collective-permute-start(bf16[512,1536]{1,0:T(8,128)(2,1)} %add_convert_fusion.9), channel_id=1, source_target_pairs={{0,1},{1,0},{2,3},{3,2},{4,5},{5,4},{6,7},{7,6},{8,9},{9,8},{10,11... | collective-permute-start | bytes 4718600 | tf_op jit(solution)/shard_map/ppermute | solution.py:115
  608.2 14.8 %collective-permute-start.44 = (bf16[4,48,1024]{2,1,0:T(8,128)(2,1)}, bf16[4,48,1024]{2,1,0:T(8,128)(2,1)S(1)}, u32[]{:S(2)}, u32[]{:S(2)}) collective-permute-start(bf16[4,48,1024]{2,1,0:T(8,128)(2,1)} %fusion.53), channel_id=1, source_target_pairs={{0,16},{16,0},{1,17},{17,1},{2,18},{18,2},{3,19},{19,3},{4,20},{20... | collective-permute-start | bytes 1179656 | tf_op jit(solution)/shard_map/ppermute | solution.py:115
  627.5 16.7 %collective-permute-start.51 = (bf16[144,1536]{1,0:T(8,128)(2,1)}, bf16[144,1536]{1,0:T(8,128)(2,1)}, u32[]{:S(2)}, u32[]{:S(2)}) collective-permute-start(bf16[144,1536]{1,0:T(8,128)(2,1)} %get-tuple-element.234), channel_id=1, source_target_pairs={{0,16},{16,0},{1,17},{17,1},{2,18},{18,2},{3,19},{19,3},{4,20},{20... | collective-permute-start | bytes 1327112 | tf_op jit(solution)/shard_map/ppermute | solution.py:115
  (167 other events, 849.0 us)
Sparse Core Ops, SparseCore 0:
  50.1 47.0 all-gather.8
  99.3 39.1 all-gather.10
  140.7 39.1 all-gather.12
  208.3 38.3 all-gather.14
  384.7 35.5 reduce-scatter.5
  439.6 34.4 reduce-scatter.7
  515.1 36.6 reduce-scatter.11
  574.9 35.4 reduce-scatter.13
  631.4 33.7 reduce-scatter.9
